TPU v7x, 128 devices: a whole 4x4x4 slice. The times are simulated.
128 devices in a mesh: lat: 16 (over y_lo, z, core), lon: 8 (over y_hi, x).
Axes of the slice: x: 4, y: 4 (y_hi: 2, y_lo: 2; y = y_hi * 2 + y_lo), z: 4, core: 2. Of those that a mesh axis runs over, the one named last changes fastest.
Arguments:
- features: bfloat16 [64, 4096, 256], P('lat', 'lon'), may hold values from -6 to 6
- basis: float32 [64, 9, 25], P('lat'), may hold values from -1.2 to 1.2
- span_lo: int32 [64], P('lat'), may hold values from -2 to 0
- span_hi: int32 [64], P('lat'), may hold values from 0 to 2
- weight: bfloat16 [9, 256, 256], replicated, may hold values from -0.125 to 0.125
- cotangent: bfloat16 [64, 4096, 256], P('lat', 'lon'), may hold values from -6 to 6
Outputs:
- mixed: bfloat16 [64, 4096, 256], P('lat', 'lon')
- grad_input: bfloat16 [64, 4096, 256], P('lat', 'lon')
- grad_weight: float32 [9, 256, 256], replicated
All inputs are finite; a program needn't handle non-finite values.
Results may differ from a plain program's by a relative error of at most 0.0049.
Values may be sent and summed in bfloat16 or wider, within the bound.
No kernel may reach another device: no remote copies, remote signals or barrier semaphores. Data moves between devices by JAX's collectives and lax.ppermute only.
A program may use at most 192 MiB of HBM per device.

v0:
```python
import math

import jax
import jax.numpy as jnp
from jax import lax
from jax.sharding import PartitionSpec as P

K = 9
RAD = 2
TAPS = 25


def extended_2(block, sides, width, periodic):
    for axis, dim in sides:
        count = lax.axis_size(axis)
        forward = [(i, i + 1) for i in range(count - 1)]
        if periodic:
            forward.append((count - 1, 0))
        backward = [(target, source) for source, target in forward]
        low = lax.ppermute(
            lax.slice_in_dim(block, block.shape[dim] - width, None, axis=dim), axis, forward
        )
        high = lax.ppermute(lax.slice_in_dim(block, 0, width, axis=dim), axis, backward)
        block = jnp.concatenate([low, block, high], axis=dim)
    return block


def from_behind(block, axis, distance):
    devices = range(lax.axis_size(axis))
    route = [((i - distance) % len(devices), i) for i in devices]
    return lax.ppermute(block, axis, route)


def passed_along(block, axis, distance):
    devices = range(lax.axis_size(axis))
    route = [(i - distance, i) for i in devices if i - distance in devices]
    return lax.ppermute(block, axis, route)


def kept_basis(basis, span_lo, span_hi):
    offsets = jnp.arange(TAPS, dtype=jnp.int32) // (2 * RAD + 1) - RAD
    keep = (offsets[None, :] >= span_lo[:, None]) & (offsets[None, :] <= span_hi[:, None])
    return jnp.where(keep[:, None, :], basis, jnp.zeros_like(basis))


def tap_shifts(tap_index):
    return (tap_index // (2 * RAD + 1) - RAD, tap_index % (2 * RAD + 1) - RAD)


def basis_planes(extended, kept, row_count, lon_count):
    planes = []
    for kernel in range(K):
        total = jnp.zeros((row_count, lon_count, extended.shape[2]), jnp.float32)
        for tap_index in range(TAPS):
            row_shift, col_shift = tap_shifts(tap_index)
            window = extended[
                RAD + row_shift : RAD + row_shift + row_count,
                RAD + col_shift : RAD + col_shift + lon_count,
            ]
            total = total + kept[:, kernel, tap_index][:, None, None] * window.astype(jnp.float32)
        planes.append(total.astype(jnp.bfloat16))
    return jnp.stack(planes)


def per_device(features, basis, span_lo, span_hi, weight, cotangent):
    row_count, lon_count, channels = features.shape
    kept = kept_basis(basis, span_lo, span_hi)
    feat_ext = extended_2(features, (("lon", 1),), RAD, True)
    feat_ext = extended_2(feat_ext, (("lat", 0),), RAD, False)
    planes = basis_planes(feat_ext, kept, row_count, lon_count)
    mixed = jnp.einsum("krjc,kco->rjo", planes, weight, preferred_element_type=jnp.float32).astype(
        jnp.bfloat16
    )
    local_grad = jnp.einsum("krjc,rjo->kco", planes, cotangent, preferred_element_type=jnp.float32)
    summed = lax.psum(local_grad, ("lat", "lon"))
    scale = 1.0 / math.sqrt(row_count * lax.axis_size("lat") * lon_count * lax.axis_size("lon"))
    grad_weight = summed * scale
    grad_planes = jnp.einsum("rjo,kco->krjc", cotangent, weight, preferred_element_type=jnp.float32)
    grad_planes = grad_planes.astype(jnp.bfloat16)
    width = 2 * RAD + 1
    spread = jnp.zeros((row_count + 2 * RAD, lon_count + 2 * RAD, channels), jnp.float32)
    for row_index in range(width):
        row_shift = row_index - RAD
        line = jnp.zeros((row_count, lon_count + 2 * RAD, channels), jnp.float32)
        for col_index in range(width):
            tap_index = row_index * width + col_index
            col_shift = col_index - RAD
            term = jnp.zeros((row_count, lon_count, channels), jnp.float32)
            for kernel in range(K):
                term = term + kept[:, kernel, tap_index][:, None, None] * grad_planes[
                    kernel
                ].astype(jnp.float32)
            line = line + jnp.pad(term, ((0, 0), (RAD + col_shift, RAD - col_shift), (0, 0)))
        spread = spread + jnp.pad(line, ((RAD + row_shift, RAD - row_shift), (0, 0), (0, 0)))
    core = spread[:, RAD : RAD + lon_count]
    for by_step in (1, -1):
        if by_step == 1:
            border = spread[:, lon_count + RAD :]
        else:
            border = spread[:, :RAD]
        moved = from_behind(border, "lon", by_step)
        if by_step == 1:
            core = jnp.concatenate([core[:, :RAD] + moved, core[:, RAD:]], axis=1)
        else:
            core = jnp.concatenate(
                [core[:, : lon_count - RAD], core[:, lon_count - RAD :] + moved], axis=1
            )
    middle = core[RAD : RAD + row_count]
    for by_step in (1, -1):
        if by_step == 1:
            border = core[row_count + RAD :]
        else:
            border = core[:RAD]
        moved = passed_along(border, "lat", by_step)
        if by_step == 1:
            middle = jnp.concatenate([middle[:RAD] + moved, middle[RAD:]], axis=0)
        else:
            middle = jnp.concatenate(
                [middle[: row_count - RAD], middle[row_count - RAD :] + moved], axis=0
            )
    grad_input = middle.astype(jnp.bfloat16)
    return (mixed, grad_input, grad_weight)


def solution(mesh):
    return jax.shard_map(
        per_device,
        mesh=mesh,
        in_specs=(
            P("lat", "lon", None),
            P("lat", None, None),
            P("lat"),
            P("lat"),
            P(),
            P("lat", "lon", None),
        ),
        out_specs=(P("lat", "lon", None), P("lat", "lon", None), P()),
        check_vma=False,
    )
```

profile of v0, /device:TPU:1, one launch (start us, length us, event | category | flops | bytes accessed | tf_op | source)
XLA Modules:
  0.0 385.8 jit_solution(6356468643673980459)
XLA Ops:
  18.3 3.9 %convert_bitcast_fusion = bf16[9,4,512,256]{3,2,1,0:T(8,128)(2,1)S(1)} fusion(bf16[9,256,256]{2,1,0:T(8,128)(2,1)S(1)} %copy-done, bf16[4,512,256]{2,1,0:T(8,128)(2,1)} %param.11), kind=kOutput, calls=%fused_computation.225 | convolution fusion | flops 2420637696 | bytes 11665408 | tf_op jit(solution)/shard_map/rjo,kco->krjc/dot_general | solution.py:78
  40.1 3.6 fusion.352
  54.5 4.0 %fusion.384 = f32[4,512,256]{2,1,0:T(8,128)} fusion(f32[4]{0:T(128)S(1)} %get-tuple-element.8, f32[4]{0:T(128)S(1)} %get-tuple-element.32, f32[4]{0:T(128)S(1)} %get-tuple-element.57, f32[4]{0:T(128)S(1)} %get-tuple-element.102, f32[4]{0:T(128)S(1)} %get-tuple-element.86, f32[4]{0:T(128)S(1)} %get-tuple-element.132, f32[4]{0:T(128)S(1)} %get-tuple-element.158, ...), kind=kLoop, calls=%fused_computation.843 | loop fusion | flops 13631488 | bytes 11534480 | tf_op jit(solution)/shard_map/add | solution.py:90
  58.5 3.6 fusion.392
  100.3 8.0 %pad_add_fusion.1 = (f32[4,516,256]{2,1,0:T(8,128)S(1)}, f32[4,516,256]{2,1,0:T(8,128)S(1)}) fusion(f32[4,512,256]{2,1,0:T(8,128)} %fusion.416, f32[4,512,256]{2,1,0:T(8,128)} %fusion.408, f32[4,512,256]{2,1,0:T(8,128)} %fusion.400, f32[4,512,256]{2,1,0:T(8,128)} %fusion.392, f32[4,512,256]{2,1,0:T(8,128)} %fusion.384, f32[4,512,256]{2,1,0:T(8,128)} %fusion.376, ...), kind=kLoop, calls=%fused_computation.455 | loop fusion | flops 4227072 | bytes 25198592 | tf_op jit(solution)/shard_map/add | solution.py:93
  108.6 3.8 pad_add_fusion.3
  112.4 6.0 %collective-permute-start.5 = (f32[8,2,256]{2,1,0:T(2,128)S(1)}, f32[8,2,256]{2,1,0:T(2,128)S(1)}, u32[]{:S(2)}, u32[]{:S(2)}) collective-permute-start(f32[8,2,256]{2,1,0:T(2,128)S(1)} %pad_add_fusion.6), channel_id=1, source_target_pairs={{1,0},{2,1},{3,2},{4,3},{5,4},{6,5},{7,6},{0,7},{9,8},{10,9},{11,1... | collective-permute-start | bytes 49160 | tf_op jit(solution)/shard_map/ppermute | solution.py:31
  118.5 5.1 %collective-permute-start.1 = (bf16[4,2,256]{2,1,0:T(2,128)(2,1)S(1)}, bf16[4,2,256]{2,1,0:T(2,128)(2,1)S(1)}, u32[]{:S(2)}, u32[]{:S(2)}) collective-permute-start(bf16[4,2,256]{2,1,0:T(2,128)(2,1)S(1)} %get-tuple-element.238), channel_id=1, source_target_pairs={{1,0},{2,1},{3,2},{4,3},{5,4},{6,5},{7,6},{0,7},{9,8},{10,9},{11,1... | collective-permute-start | bytes 12296 | tf_op jit(solution)/shard_map/ppermute | solution.py:23
  125.9 5.0 %collective-permute-start.2 = (bf16[2,516,256]{2,0,1:T(2,128)(2,1)S(1)}, bf16[2,516,256]{2,0,1:T(2,128)(2,1)S(1)}, u32[]{:S(2)}, u32[]{:S(2)}) collective-permute-start(bf16[2,516,256]{2,0,1:T(2,128)(2,1)S(1)} %copy.19), channel_id=1, source_target_pairs={{0,8},{8,16},{16,24},{24,32},{32,40},{40,48},{48,56},{56,64},{64,7... | collective-permute-start | bytes 1585160 | tf_op jit(solution)/shard_map/ppermute | solution.py:20
  133.3 6.5 %collective-permute-done.4 = f32[8,2,256]{2,1,0:T(2,128)S(1)} collective-permute-done((f32[8,2,256]{2,1,0:T(2,128)S(1)}, f32[8,2,256]{2,1,0:T(2,128)S(1)}, u32[]{:S(2)}, u32[]{:S(2)}) %collective-permute-start.4) | collective-permute-done | bytes 16416 | tf_op jit(solution)/shard_map/ppermute | solution.py:31
  140.4 4.5 %collective-permute-start.6 = (f32[2,512,256]{2,1,0:T(8,128)S(1)}, f32[2,512,256]{2,1,0:T(8,128)S(1)}, u32[]{:S(2)}, u32[]{:S(2)}) collective-permute-start(f32[2,512,256]{2,1,0:T(8,128)S(1)} %slice.2014), channel_id=1, source_target_pairs={{0,8},{8,16},{16,24},{24,32},{32,40},{40,48},{48,56},{56,64},{64,7... | collective-permute-start | bytes 3145736 | tf_op jit(solution)/shard_map/ppermute | solution.py:37
  146.3 8.0 %bitcast_dynamic-update-slice_fusion.7 = (bf16[9,4,512,256]{3,2,0,1:T(8,128)(2,1)S(1)}, bf16[4,512,256]{2,1,0:T(8,128)(2,1)S(1)}) fusion(f32[4]{0:T(128)} %get-tuple-element.203, f32[4]{0:T(128)} %get-tuple-element.204, f32[4]{0:T(128)} %get-tuple-element.205, f32[4]{0:T(128)} %get-tuple-element.206, f32[4]{0:T(128)} %get-tuple-element.207, ...), kind=kLoop, calls=%fused_computation.919 | loop fusion | flops 42991616 | bytes 26218896
  154.5 7.8 %bitcast_dynamic-update-slice_fusion.6 = bf16[9,4,512,256]{3,2,0,1:T(8,128)(2,1)S(1)} fusion(bf16[9,4,512,256]{3,2,0,1:T(8,128)(2,1)S(1)} %get-tuple-element.228, f32[4]{0:T(128)} %get-tuple-element.178, f32[4]{0:T(128)} %get-tuple-element.179, f32[4]{0:T(128)} %get-tuple-element.180, f32[4]{0:T(128)} %get-tuple-element.181, f32[4]{0:T(128)} %get-tuple-element.182, ...), kind=kLoop, calls=%fused_computation.918 | loop fusion | flops 40894464 | bytes 26221376
  162.4 7.6 %bitcast_dynamic-update-slice_fusion.5 = bf16[9,4,512,256]{3,2,0,1:T(8,128)(2,1)S(1)} fusion(bf16[9,4,512,256]{3,2,0,1:T(8,128)(2,1)S(1)} %bitcast_dynamic-update-slice_fusion.6, f32[4]{0:T(128)} %get-tuple-element.153, f32[4]{0:T(128)} %get-tuple-element.154, f32[4]{0:T(128)} %get-tuple-element.155, f32[4]{0:T(128)} %get-tuple-element.156, ...), kind=kLoop, calls=%fused_computation.917 | loop fusion | flops 40894464 | bytes 26229312
  170.2 7.7 %bitcast_dynamic-update-slice_fusion.4 = bf16[9,4,512,256]{3,2,0,1:T(8,128)(2,1)S(1)} fusion(bf16[9,4,512,256]{3,2,0,1:T(8,128)(2,1)S(1)} %bitcast_dynamic-update-slice_fusion.5, f32[4]{0:T(128)S(1)} %get-tuple-element.128, f32[4]{0:T(128)S(1)} %get-tuple-element.129, f32[4]{0:T(128)S(1)} %get-tuple-element.130, f32[4]{0:T(128)S(1)} %get-tuple-element.131, ...), kind=kLoop, calls=%fused_computation.916 | loop fusion | flops 40894464 | bytes 26226336
  178.1 7.6 %bitcast_dynamic-update-slice_fusion.3 = bf16[9,4,512,256]{3,2,0,1:T(8,128)(2,1)S(1)} fusion(bf16[9,4,512,256]{3,2,0,1:T(8,128)(2,1)S(1)} %bitcast_dynamic-update-slice_fusion.4, f32[4]{0:T(128)S(1)} %copy-done.73, f32[4]{0:T(128)S(1)} %copy-done.75, f32[4]{0:T(128)S(1)} %copy-done.77, f32[4]{0:T(128)S(1)} %copy-done.79, f32[4]{0:T(128)S(1)} %copy-done.81, ...), kind=kLoop, calls=%fused_computation.915 | loop fusion | flops 40894464 | bytes 26230304
  185.8 7.7 %bitcast_dynamic-update-slice_fusion.2 = bf16[9,4,512,256]{3,2,0,1:T(8,128)(2,1)S(1)} fusion(bf16[9,4,512,256]{3,2,0,1:T(8,128)(2,1)S(1)} %bitcast_dynamic-update-slice_fusion.3, f32[4]{0:T(128)S(1)} %get-tuple-element.78, f32[4]{0:T(128)S(1)} %get-tuple-element.99, f32[4]{0:T(128)S(1)} %get-tuple-element.100, f32[4]{0:T(128)S(1)} %get-tuple-element.101, ...), kind=kLoop, calls=%fused_computation.914 | loop fusion | flops 40894464 | bytes 26230800
  193.6 6.8 %bitcast_dynamic-update-slice_fusion.1 = bf16[9,4,512,256]{3,2,0,1:T(8,128)(2,1)S(1)} fusion(bf16[9,4,512,256]{3,2,0,1:T(8,128)(2,1)S(1)} %bitcast_dynamic-update-slice_fusion.2, f32[4]{0:T(128)S(1)} %get-tuple-element.53, f32[4]{0:T(128)S(1)} %get-tuple-element.54, f32[4]{0:T(128)S(1)} %get-tuple-element.55, f32[4]{0:T(128)S(1)} %get-tuple-element.56, ...), kind=kLoop, calls=%fused_computation.913 | loop fusion | flops 40894464 | bytes 26231296
  200.5 6.8 %bitcast_dynamic-update-slice_fusion = bf16[9,4,512,256]{3,2,0,1:T(8,128)(2,1)S(1)} fusion(bf16[9,4,512,256]{3,2,0,1:T(8,128)(2,1)S(1)} %bitcast_dynamic-update-slice_fusion.1, f32[4]{0:T(128)S(1)} %get-tuple-element.28, f32[4]{0:T(128)S(1)} %get-tuple-element.29, f32[4]{0:T(128)S(1)} %get-tuple-element.30, f32[4]{0:T(128)S(1)} %get-tuple-element.31, ...), kind=kLoop, calls=%fused_computation.912 | loop fusion | flops 40894464 | bytes 26231296
  207.5 6.8 %bitcast_dynamic-update-slice_fusion.8 = bf16[9,4,512,256]{3,2,0,1:T(8,128)(2,1)S(1)} fusion(bf16[9,4,512,256]{3,2,0,1:T(8,128)(2,1)S(1)} %bitcast_dynamic-update-slice_fusion, f32[4]{0:T(128)S(1)} %get-tuple-element.4, f32[4]{0:T(128)S(1)} %get-tuple-element.5, f32[4]{0:T(128)S(1)} %get-tuple-element.6, f32[4]{0:T(128)S(1)} %get-tuple-element.7, ...), kind=kLoop, calls=%fused_computation.921 | loop fusion | flops 40894464 | bytes 26231296 | tf_op jit(solution)/shard_map/stack | solution.py:62
  214.3 3.6 copy-done.6
  217.9 4.2 %convolution_bitcast_fusion = f32[9,256,256]{2,1,0:T(8,128)} fusion(bf16[9,4,512,256]{3,2,0,1:T(8,128)(2,1)S(1)} %bitcast_dynamic-update-slice_fusion.8, bf16[4,512,256]{2,1,0:T(8,128)(2,1)S(1)} %copy-done.5), kind=kOutput, calls=%fused_computation.886 | convolution fusion | flops 2415919104 | bytes 12845056 | tf_op jit(solution)/shard_map/krjc,rjo->kco/dot_general | solution.py:74
  227.1 7.5 %bitcast_convert_fusion = bf16[4,512,256]{2,1,0:T(8,128)(2,1)} fusion(bf16[9,4,512,256]{3,2,0,1:T(8,128)(2,1)} %copy-done.6, bf16[9,256,256]{2,1,0:T(8,128)(2,1)S(1)} %copy-done), kind=kOutput, calls=%fused_computation.876 | convolution fusion | flops 2416443392 | bytes 11665408 | tf_op jit(solution)/shard_map/krjc,kco->rjo/dot_general | solution.py:71
  234.6 138.3 %all-reduce.32.cloned.1.call-done = f32[9,256,256]{2,1,0:T(8,128)} async-done(((f32[9,256,256]{2,1,0:T(8,128)}), f32[9,256,256]{2,1,0:T(8,128)}) %all-reduce.32.cloned.1.call-update) | async-done | bytes 2359312 | tf_op jit(solution)/shard_map/psum | solution.py:75
  (335 shorter events, 94.8 us)
Async XLA Ops:
  7.2 365.6 %all-reduce.32.cloned.1.call-start = ((), (), s32[]{:S(2)}) async-start(), calls=%async_computation | async-start | bytes 4718592 | tf_op jit(solution)/shard_map/psum | solution.py:75
  9.8 30.3 %copy-start.11 = (f32[4]{0:T(128)}, f32[4]{0:T(128)S(1)}, u32[]{:S(2)}) copy-start(f32[4]{0:T(128)S(1)} %get-tuple-element.12) | copy-start | bytes 52
  9.8 33.9 %copy-start.9 = (f32[4]{0:T(128)}, f32[4]{0:T(128)S(1)}, u32[]{:S(2)}) copy-start(f32[4]{0:T(128)S(1)} %get-tuple-element.11) | copy-start | bytes 52
  11.3 61.5 %copy-start.41 = (f32[4]{0:T(128)}, f32[4]{0:T(128)S(1)}, u32[]{:S(2)}) copy-start(f32[4]{0:T(128)S(1)} %get-tuple-element.164) | copy-start | bytes 52
  11.3 64.1 %copy-start.54 = (f32[4]{0:T(128)}, f32[4]{0:T(128)S(1)}, u32[]{:S(2)}) copy-start(f32[4]{0:T(128)S(1)} %get-tuple-element.172) | copy-start | bytes 52
  11.3 66.8 %copy-start.52 = (f32[4]{0:T(128)}, f32[4]{0:T(128)S(1)}, u32[]{:S(2)}) copy-start(f32[4]{0:T(128)S(1)} %get-tuple-element.171) | copy-start | bytes 52
  11.3 69.4 %copy-start.50 = (f32[4]{0:T(128)}, f32[4]{0:T(128)S(1)}, u32[]{:S(2)}) copy-start(f32[4]{0:T(128)S(1)} %get-tuple-element.170) | copy-start | bytes 52
  11.4 72.1 %copy-start.48 = (f32[4]{0:T(128)}, f32[4]{0:T(128)S(1)}, u32[]{:S(2)}) copy-start(f32[4]{0:T(128)S(1)} %get-tuple-element.169) | copy-start | bytes 52
  15.6 28.1 %copy-start.86 = (f32[4]{0:T(128)}, f32[4]{0:T(128)S(1)}, u32[]{:S(2)}) copy-start(f32[4]{0:T(128)S(1)} %get-tuple-element.89) | copy-start | bytes 52
  15.6 31.7 %copy-start.84 = (f32[4]{0:T(128)}, f32[4]{0:T(128)S(1)}, u32[]{:S(2)}) copy-start(f32[4]{0:T(128)S(1)} %get-tuple-element.88) | copy-start | bytes 52
  15.6 35.3 %copy-start.82 = (f32[4]{0:T(128)}, f32[4]{0:T(128)S(1)}, u32[]{:S(2)}) copy-start(f32[4]{0:T(128)S(1)} %get-tuple-element.87) | copy-start | bytes 52
  15.6 38.8 %copy-start.80 = (f32[4]{0:T(128)}, f32[4]{0:T(128)S(1)}, u32[]{:S(2)}) copy-start(f32[4]{0:T(128)S(1)} %get-tuple-element.86) | copy-start | bytes 52
  15.7 42.8 %copy-start.78 = (f32[4]{0:T(128)}, f32[4]{0:T(128)S(1)}, u32[]{:S(2)}) copy-start(f32[4]{0:T(128)S(1)} %get-tuple-element.85) | copy-start | bytes 52
  15.7 46.4 %copy-start.76 = (f32[4]{0:T(128)}, f32[4]{0:T(128)S(1)}, u32[]{:S(2)}) copy-start(f32[4]{0:T(128)S(1)} %get-tuple-element.84) | copy-start | bytes 52
  15.7 50.0 %copy-start.74 = (f32[4]{0:T(128)}, f32[4]{0:T(128)S(1)}, u32[]{:S(2)}) copy-start(f32[4]{0:T(128)S(1)} %get-tuple-element.83) | copy-start | bytes 52
  15.7 53.6 %copy-start.72 = (f32[4]{0:T(128)}, f32[4]{0:T(128)S(1)}, u32[]{:S(2)}) copy-start(f32[4]{0:T(128)S(1)} %get-tuple-element.82) | copy-start | bytes 52
  112.4 20.8 %collective-permute-start.5 = (f32[8,2,256]{2,1,0:T(2,128)S(1)}, f32[8,2,256]{2,1,0:T(2,128)S(1)}, u32[]{:S(2)}, u32[]{:S(2)}) collective-permute-start(f32[8,2,256]{2,1,0:T(2,128)S(1)} %pad_add_fusion.6), channel_id=1, source_target_pairs={{1,0},{2,1},{3,2},{4,3},{5,4},{6,5},{7,6},{0,7},{9,8},{10,9},{11,1... | collective-permute-start | bytes 49160 | tf_op jit(solution)/shard_map/ppermute | solution.py:31
  118.4 6.7 %collective-permute-start = (bf16[4,2,256]{2,1,0:T(2,128)(2,1)S(1)}, bf16[4,2,256]{2,1,0:T(2,128)(2,1)S(1)}, u32[]{:S(2)}, u32[]{:S(2)}) collective-permute-start(bf16[4,2,256]{2,1,0:T(2,128)(2,1)S(1)} %get-tuple-element.239), channel_id=1, source_target_pairs={{0,1},{1,2},{2,3},{3,4},{4,5},{5,6},{6,7},{7,0},{8,9},{9,10},{10,1... | collective-permute-start | bytes 12296 | tf_op jit(solution)/shard_map/ppermute | solution.py:20
  118.5 6.6 %collective-permute-start.1 = (bf16[4,2,256]{2,1,0:T(2,128)(2,1)S(1)}, bf16[4,2,256]{2,1,0:T(2,128)(2,1)S(1)}, u32[]{:S(2)}, u32[]{:S(2)}) collective-permute-start(bf16[4,2,256]{2,1,0:T(2,128)(2,1)S(1)} %get-tuple-element.238), channel_id=1, source_target_pairs={{1,0},{2,1},{3,2},{4,3},{5,4},{6,5},{7,6},{0,7},{9,8},{10,9},{11,1... | collective-permute-start | bytes 12296 | tf_op jit(solution)/shard_map/ppermute | solution.py:23
  125.9 19.0 %collective-permute-start.2 = (bf16[2,516,256]{2,0,1:T(2,128)(2,1)S(1)}, bf16[2,516,256]{2,0,1:T(2,128)(2,1)S(1)}, u32[]{:S(2)}, u32[]{:S(2)}) collective-permute-start(bf16[2,516,256]{2,0,1:T(2,128)(2,1)S(1)} %copy.19), channel_id=1, source_target_pairs={{0,8},{8,16},{16,24},{24,32},{32,40},{40,48},{48,56},{56,64},{64,7... | collective-permute-start | bytes 1585160 | tf_op jit(solution)/shard_map/ppermute | solution.py:20
  131.3 13.7 %collective-permute-start.3 = (bf16[2,516,256]{2,0,1:T(2,128)(2,1)S(1)}, bf16[2,516,256]{2,0,1:T(2,128)(2,1)S(1)}, u32[]{:S(2)}, u32[]{:S(2)}) collective-permute-start(bf16[2,516,256]{2,0,1:T(2,128)(2,1)S(1)} %copy.21), channel_id=1, source_target_pairs={{8,0},{16,8},{24,16},{32,24},{40,32},{48,40},{56,48},{64,56},{72,6... | collective-permute-start | bytes 1585160 | tf_op jit(solution)/shard_map/ppermute | solution.py:23
  133.2 6.6 %collective-permute-start.4 = (f32[8,2,256]{2,1,0:T(2,128)S(1)}, f32[8,2,256]{2,1,0:T(2,128)S(1)}, u32[]{:S(2)}, u32[]{:S(2)}) collective-permute-start(f32[8,2,256]{2,1,0:T(2,128)S(1)} %get-tuple-element.231), channel_id=1, source_target_pairs={{7,0},{0,1},{1,2},{2,3},{3,4},{4,5},{5,6},{6,7},{15,8},{8,9},{9,10... | collective-permute-start | bytes 49160 | tf_op jit(solution)/shard_map/ppermute | solution.py:31
  140.4 81.8 %collective-permute-start.6 = (f32[2,512,256]{2,1,0:T(8,128)S(1)}, f32[2,512,256]{2,1,0:T(8,128)S(1)}, u32[]{:S(2)}, u32[]{:S(2)}) collective-permute-start(f32[2,512,256]{2,1,0:T(8,128)S(1)} %slice.2014), channel_id=1, source_target_pairs={{0,8},{8,16},{16,24},{24,32},{32,40},{40,48},{48,56},{56,64},{64,7... | collective-permute-start | bytes 3145736 | tf_op jit(solution)/shard_map/ppermute | solution.py:37
  224.8 151.3 %collective-permute-start.7 = (f32[2,512,256]{2,1,0:T(8,128)}, f32[2,512,256]{2,1,0:T(8,128)S(1)}, u32[]{:S(2)}, u32[]{:S(2)}) collective-permute-start(f32[2,512,256]{2,1,0:T(8,128)} %get-tuple-element.233), channel_id=1, source_target_pairs={{8,0},{16,8},{24,16},{32,24},{40,32},{48,40},{56,48},{64,56},{72,6... | collective-permute-start | bytes 3145736 | tf_op jit(solution)/shard_map/ppermute | solution.py:37
  (117 other events, 900.9 us)
Sparse Core Ops, SparseCore 0:
  222.3 150.4 all-reduce.31
where the time goes:
time: 391 us; the launch traced here: 386 us
  other arithmetic  169 us (43%)
  waiting for transfers between devices  145 us (37%)
  starting transfers between devices  24.8 us (6%)
  between operations  16.8 us (4%)
  matrix products  15.6 us (4%)
  local copies, waits for them, and re-layouts  15.1 us (4%)
    psum x1, waiting for transfers between devices, per_device(): summed = lax.psum(local_grad, ('lat', 'lon'))  138 us
    add x25, other arithmetic, per_device(): term + kept[:, kernel, tap_index][:, None, None] * grad_planes[kernel].as...  76.5 us
    unnamed x8, other arithmetic  60 us
    add x3, other arithmetic, per_device(): line + jnp.pad(term, ((0, 0), (RAD + col_shift, RAD - col_shift), (0, 0)))  12.6 us
    slice x12, local copies, waits for them, and re-layouts, basis_planes(): kept[:, kernel, tap_index][:, None, None] * window.astype(jnp.float32)  9.15 us
  transfers between devices with their start and end apart: 9, of which 2 were waited for; matrix products, arithmetic and copies ran while one was open for 23% of the time, Pallas kernels for 0%

commit v1 on v0

v1 whole, which is shorter than its diff:
```python
import functools
import math

import jax
import jax.numpy as jnp
import numpy as np
from jax import lax
from jax.experimental import pallas as pl
from jax.experimental.pallas import tpu as pltpu
from jax.sharding import Mesh
from jax.sharding import PartitionSpec as P

K = 9
RAD = 2
WIDTH = 2 * RAD + 1
TAPS = WIDTH * WIDTH
ROWS = 4
NJ = 512
C = 256
J = 32
OWN_WINDOW = 64
EXT_WINDOW = 48
LANES = 128
BLOCKS = 2 * K
PADDED_BLOCKS = 20
VMEM = 56 * 1024 * 1024
BF = jnp.bfloat16
F32 = jnp.float32


def kept_basis(basis, span_lo, span_hi):
    offsets = jnp.arange(TAPS, dtype=jnp.int32) // WIDTH - RAD
    keep = (offsets[None, :] >= span_lo[:, None]) & (offsets[None, :] <= span_hi[:, None])
    return jnp.where(keep[:, None, :], basis, jnp.zeros_like(basis))


def band(coef, window, first, depth):
    lane = lax.broadcasted_iota(jnp.int32, (J, depth), 1)
    sub = lax.broadcasted_iota(jnp.int32, (J, depth), 0)
    diff = lane % window - sub - first
    masks = [diff == s for s in range(WIDTH)]

    def build(coef):
        value = jnp.zeros((J, depth), F32)
        for s in range(WIDTH):
            value = jnp.where(masks[s], coef[s : s + 1, :], value)
        return value.astype(BF)

    return build


def own_kernel(coef_ref, cot_ref, feat_ref, z_ref, grad_ref, padded, bands, z_own):
    zero = jnp.zeros((ROWS, 16, C), BF)
    padded[:, 0:16, :] = zero
    padded[:, 16 + NJ : 32 + NJ, :] = zero
    padded[:, 16 : 16 + NJ, :] = cot_ref[...]
    build = band(None, OWN_WINDOW, 16 - RAD, ROWS * OWN_WINDOW)
    for block in range(8 * K):
        bands[block * J : (block + 1) * J, :] = build(coef_ref[block])

    def step(tile, _):
        start = pl.multiple_of(tile * J, J)
        cells = jnp.concatenate([padded[i, pl.ds(start, OWN_WINDOW), :] for i in range(ROWS)], axis=0)
        for row in range(8):
            found = jnp.dot(
                bands[row * K * J : (row + 1) * K * J, :], cells, preferred_element_type=F32
            ).astype(BF)
            for k in range(K):
                piece = found[k * J : (k + 1) * J]
                columns = slice(k * C, (k + 1) * C)
                if 2 <= row < 6:
                    z_own[pl.ds((row - 2) * NJ + start, J), columns] = piece
                else:
                    halo_row = row if row < 2 else row - 4
                    z_ref[pl.ds(halo_row * NJ + start, J), columns] = piece
        return 0

    lax.fori_loop(0, NJ // J, step, 0)
    turned = feat_ref[...].reshape(ROWS * NJ, C).T
    for k in range(K):
        columns = slice(k * C, (k + 1) * C)
        grad_ref[:, columns] = jnp.dot(turned, z_own[:, columns], preferred_element_type=F32)


def own_part(coef, cotangent, features):
    return pl.pallas_call(
        own_kernel,
        out_shape=(
            jax.ShapeDtypeStruct((ROWS * NJ, K * C), BF),
            jax.ShapeDtypeStruct((C, K * C), F32),
        ),
        in_specs=[pl.BlockSpec(memory_space=pltpu.VMEM)] * 3,
        out_specs=[pl.BlockSpec(memory_space=pltpu.VMEM)] * 2,
        scratch_shapes=[
            pltpu.VMEM((ROWS, NJ + 32, C), BF),
            pltpu.VMEM((8 * K * J, ROWS * OWN_WINDOW), BF),
            pltpu.VMEM((ROWS * NJ, K * C), BF),
        ],
        compiler_params=pltpu.CompilerParams(vmem_limit_bytes=VMEM),
        cost_estimate=pl.CostEstimate(
            flops=10_000_000_000, bytes_accessed=15_000_000, transcendentals=0
        ),
        name="own_part",
    )(coef, cotangent, features)


def halo_kernel(core_ref, low_ref, high_ref, z_ref, grad_ref, edge_coef_ref, edge_cot_ref, edge_feat_ref, own_ref, other_ref, total):
    low = low_ref[...].reshape(2 * NJ, C).T
    high = high_ref[...].reshape(2 * NJ, C).T
    turned = jnp.concatenate([low, high], axis=1)
    edge_z = jnp.dot(edge_coef_ref[...], edge_cot_ref[...], preferred_element_type=F32).astype(BF)
    edge_feat = edge_feat_ref[...].T
    for k in range(K):
        columns = slice(k * C, (k + 1) * C)
        total[:, columns] = (
            grad_ref[:, columns]
            + jnp.dot(turned, z_ref[:, columns], preferred_element_type=F32)
            + jnp.dot(edge_feat, edge_z[k * 32 : (k + 1) * 32], preferred_element_type=F32)
        )
    core = core_ref[0]
    mine = pl.multiple_of(core * LANES, LANES)
    theirs = pl.multiple_of((1 - core) * LANES, LANES)
    for block in range(BLOCKS):
        columns = slice(block * LANES, (block + 1) * LANES)
        own_ref[block] = total[pl.ds(mine, LANES), columns]
        other_ref[block] = total[pl.ds(theirs, LANES), columns].astype(BF)
    for block in range(BLOCKS, PADDED_BLOCKS):
        own_ref[block] = jnp.zeros((LANES, LANES), F32)
        other_ref[block] = jnp.zeros((LANES, LANES), BF)


def halo_part(core, low, high, z, grad, edge_coef, edge_cot, edge_feat):
    shape = (PADDED_BLOCKS, LANES, LANES)
    return pl.pallas_call(
        halo_kernel,
        out_shape=(jax.ShapeDtypeStruct(shape, F32), jax.ShapeDtypeStruct(shape, BF)),
        in_specs=[pl.BlockSpec(memory_space=pltpu.SMEM)] + [pl.BlockSpec(memory_space=pltpu.VMEM)] * 7,
        out_specs=[pl.BlockSpec(memory_space=pltpu.VMEM)] * 2,
        scratch_shapes=[pltpu.VMEM((C, K * C), F32)],
        compiler_params=pltpu.CompilerParams(vmem_limit_bytes=VMEM),
        cost_estimate=pl.CostEstimate(
            flops=2_400_000_000, bytes_accessed=15_000_000, transcendentals=0
        ),
        name="halo_part",
    )(core, low, high, z, grad, edge_coef, edge_cot, edge_feat)


def mix_kernel(coef_ref, ext_ref, weight_ref, _, out_ref, bands, filtered):
    depth = WIDTH * EXT_WINDOW
    build = band(None, EXT_WINDOW, 8 - RAD, depth)
    row = pl.program_id(0)
    for k in range(K):
        bands[k * J : (k + 1) * J, :] = build(coef_ref[0, k])

    def step(tile, _):
        start = pl.multiple_of(tile * J, J)
        cells = jnp.concatenate(
            [ext_ref[row + r, pl.ds(start, EXT_WINDOW), :] for r in range(WIDTH)], axis=0
        )
        found = jnp.dot(bands[...], cells, preferred_element_type=F32).astype(BF)
        for k in range(K):
            filtered[pl.ds(start, J), k * C : (k + 1) * C] = found[k * J : (k + 1) * J]
        return 0

    lax.fori_loop(0, NJ // J, step, 0, unroll=4)
    out_ref[0] = jnp.dot(filtered[...], weight_ref[...], preferred_element_type=F32).astype(BF)


def mix_part(coef, extended, weight, after, name):
    return pl.pallas_call(
        mix_kernel,
        grid=(ROWS,),
        out_shape=jax.ShapeDtypeStruct((ROWS, NJ, C), BF),
        in_specs=[
            pl.BlockSpec((1, K, WIDTH, WIDTH * EXT_WINDOW), lambda i: (i, 0, 0, 0)),
            pl.BlockSpec(memory_space=pltpu.VMEM),
            pl.BlockSpec(memory_space=pltpu.VMEM),
            pl.BlockSpec(memory_space=pl.ANY),
        ],
        out_specs=pl.BlockSpec((1, NJ, C), lambda i: (i, 0, 0)),
        scratch_shapes=[
            pltpu.VMEM((K * J, WIDTH * EXT_WINDOW), BF),
            pltpu.VMEM((NJ, K * C), BF),
        ],
        compiler_params=pltpu.CompilerParams(vmem_limit_bytes=VMEM),
        cost_estimate=pl.CostEstimate(
            flops=10_000_000_000, bytes_accessed=5_000_000, transcendentals=0
        ),
        name=name,
    )(coef, extended, weight, after)


def edge_choice():
    choice = np.zeros((TAPS, ROWS, 8, 4, 4), np.float32)
    halo_columns = (-2, -1, NJ, NJ + 1)
    edge_columns = (0, 1, NJ - 2, NJ - 1)
    for i in range(ROWS):
        for place in range(8):
            d = place - RAD - i
            for a, target in enumerate(edge_columns):
                for b, source in enumerate(halo_columns):
                    e = target - source
                    if abs(d) <= RAD and abs(e) <= RAD:
                        choice[(d + RAD) * WIDTH + e + RAD, i, place, a, b] = 1.0
    return choice


def shifted(block, axis, count, step, periodic):
    route = [(i, (i + step) % count) for i in range(count) if periodic or 0 <= i + step < count]
    return lax.ppermute(block, axis, route)


def per_device(features, basis, span_lo, span_hi, weight, cotangent):
    lat = ("yz", "core")
    lats, lons = lax.axis_size("yz") * lax.axis_size("core"), lax.axis_size("lon")
    core = lax.axis_index("core")
    kept = kept_basis(basis, span_lo, span_hi)

    low = shifted(features[ROWS - 2 :], lat, lats, 1, False)
    high = shifted(features[:2], lat, lats, -1, False)
    left = shifted(cotangent[:, NJ - 2 :], "lon", lons, 1, True)
    right = shifted(cotangent[:, :2], "lon", lons, -1, True)

    cells = kept.reshape(ROWS, K, WIDTH, WIDTH)[..., ::-1]
    spread = jnp.stack([jnp.pad(cells[i], ((0, 0), (i, 3 - i), (0, 0))) for i in range(ROWS)])
    own_coef = jnp.transpose(spread, (2, 1, 3, 0)).reshape(8 * K, WIDTH, ROWS)
    own_coef = jnp.repeat(own_coef, OWN_WINDOW, axis=2)
    z, grad_own = own_part(own_coef, cotangent, features)

    edge_coef = jnp.einsum("ikt,tipab->kpaib", kept, edge_choice()).reshape(K * 32, ROWS * 4).astype(BF)
    edge_coef = jnp.pad(edge_coef, ((0, 0), (0, LANES - ROWS * 4)))
    edge_cot = jnp.concatenate([left, right], axis=1).reshape(ROWS * 4, C)
    edge_cot = jnp.pad(edge_cot, ((0, LANES - ROWS * 4), (0, 0)))
    rows = jnp.concatenate([low, features, high], axis=0)
    edge_feat = jnp.concatenate([rows[:, :2], rows[:, NJ - 2 :]], axis=1).reshape(32, C)
    own, other = halo_part(
        core.reshape(1).astype(jnp.int32), low, high, z, grad_own, edge_coef, edge_cot, edge_feat
    )

    swap = [(0, 1), (1, 0)]
    chips = ("yz", "lon")
    parts = lax.axis_size("yz") * lons
    half = own + lax.ppermute(other, "core", swap).astype(F32)
    pieces = half.astype(BF).reshape(parts, PADDED_BLOCKS * LANES // parts, LANES)
    pieces = lax.all_to_all(pieces, chips, 0, 0)
    scale = 1.0 / math.sqrt(ROWS * lats * NJ * lons)
    piece = (jnp.sum(pieces.astype(F32), axis=0) * scale).astype(BF)
    gathered = lax.all_to_all(jnp.broadcast_to(piece, pieces.shape), chips, 0, 0)
    gathered = gathered.reshape(PADDED_BLOCKS, LANES, LANES)[:BLOCKS]
    swapped = lax.ppermute(gathered, "core", swap)
    first = jnp.where(core == 0, gathered, swapped)
    second = jnp.where(core == 0, swapped, gathered)
    halves = jnp.stack([first, second]).reshape(2, K, 2, LANES, LANES)
    grad_weight = jnp.transpose(halves, (1, 0, 3, 2, 4)).reshape(K, C, C).astype(F32)

    edges = shifted(rows[:, NJ - 2 :], "lon", lons, 1, True), shifted(rows[:, :2], "lon", lons, -1, True)
    gap = jnp.zeros((8, 6, C), BF)
    feat_ext = jnp.concatenate([gap, edges[0], rows, edges[1], gap], axis=1)
    feat_coef = kept.reshape(ROWS, K, WIDTH, WIDTH).transpose(0, 1, 3, 2)
    feat_coef = jnp.repeat(feat_coef, EXT_WINDOW, axis=3)
    mixed = mix_part(feat_coef, feat_ext, weight.reshape(K * C, C), own, "mixed_part")

    wide = jnp.concatenate([gap[:ROWS], left, cotangent, right, gap[:ROWS]], axis=1)
    cot_low = shifted(wide[ROWS - 2 :], lat, lats, 1, False)
    cot_high = shifted(wide[:2], lat, lats, -1, False)
    cot_ext = jnp.concatenate([cot_low, wide, cot_high], axis=0)
    kept_low = shifted(kept[ROWS - 2 :], lat, lats, 1, False)
    kept_high = shifted(kept[:2], lat, lats, -1, False)
    kept_ext = jnp.concatenate([kept_low, kept, kept_high], axis=0)
    flipped = kept_ext[..., ::-1].reshape(8, K, WIDTH, WIDTH)
    cot_coef = jnp.stack(
        [jnp.stack([flipped[i + r, :, r] for r in range(WIDTH)], axis=-1) for i in range(ROWS)]
    )
    cot_coef = jnp.repeat(cot_coef, EXT_WINDOW, axis=3)
    turned = jnp.transpose(weight, (0, 2, 1)).reshape(K * C, C)
    grad_input = mix_part(cot_coef, cot_ext, turned, own, "grad_input_part")
    return mixed, grad_input, grad_weight


def solution(mesh):
    lats, lons = mesh.devices.shape
    split = Mesh(mesh.devices.reshape(lats // 2, 2, lons), ("yz", "core", "lon"))
    lat = ("yz", "core")
    return jax.shard_map(
        per_device,
        mesh=split,
        in_specs=(P(lat, "lon", None), P(lat, None, None), P(lat), P(lat), P(), P(lat, "lon", None)),
        out_specs=(P(lat, "lon", None), P(lat, "lon", None), P()),
        check_vma=False,
    )
```

time: 391 us -> 136 us (0.35); the launches traced: 386 us -> 135 us
  other arithmetic: 169 us -> 6.95 us
  waiting for transfers between devices: 145 us -> 0.04 us
  Pallas kernels: 0 us -> 47.1 us
  starting transfers between devices: 24.8 us -> 47.2 us
  local copies, waits for them, and re-layouts: 15.1 us -> 33 us
  between operations: 16.8 us -> 1.03 us
  matrix products: 15.6 us -> 0.16 us
    psum x1 -> x0, waiting for transfers between devices: 138 us -> none  [per_device(): summed = lax.psum(local_grad, ('lat', 'lon'))]
    add x31 -> x0, other arithmetic: 90.2 us -> none  [the longest x25 76.5 us: per_device(): term + kept[:, kernel, tap_index][:, None, None] * grad_planes[kernel].as...]
    unnamed x8 -> x0, other arithmetic: 60 us -> none
    pallas_call x0 -> x4, Pallas kernels: none -> 47.1 us  [the longest x2 23.1 us: mix_part(): pl.pallas_call(mix_kernel, grid=(ROWS,), out_shape=jax.ShapeDtypeStruct((...]
    all_to_all x0 -> x2, starting transfers between devices: none -> 17.9 us  [the longest x1 11.2 us: per_device(): pieces = lax.all_to_all(pieces, chips, 0, 0)]
    dot_general x3 -> x1, matrix products: 15.6 us -> 0.16 us  [per_device(): jnp.einsum('ikt,tipab->kpaib', kept, edge_choice())]
    concatenate x1 -> x4, local copies, waits for them, and re-layouts: 0.01 us -> 11.8 us  [the longest x1 6.74 us: per_device(): feat_ext = jnp.concatenate([gap, edges[0], rows, edges[1], gap], axis=1)]
    another operation x3 -> x1, other arithmetic: 10.8 us -> 0.01 us  [per_device(): jnp.stack([jnp.stack([flipped[i + r, :, r] for r in range(WIDTH)], axis=-...]
  transfers between devices with their start and end apart: 9 -> 14, of which waited for: 2 -> 0; matrix products, arithmetic and copies ran while one was open for 23% -> 21% of each run, Pallas kernels for 0% -> 28%
where the time goes in v1:
time: 136 us; the launch traced here: 135 us
  starting transfers between devices  47.2 us (35%)
  Pallas kernels  47.1 us (35%)
  local copies, waits for them, and re-layouts  33 us (24%)
  other arithmetic  6.95 us (5%)
    ppermute x10, starting transfers between devices, shifted(): return lax.ppermute(block, axis, route)  28.4 us
    pallas_call x2, Pallas kernels, mix_part(): pl.pallas_call(mix_kernel, grid=(ROWS,), out_shape=jax.ShapeDtypeStruct((...  23.1 us
    pallas_call x1, Pallas kernels, own_part(): pl.pallas_call(own_kernel, out_shape=(jax.ShapeDtypeStruct((ROWS * NJ, K...  14.8 us
    all_to_all x1, starting transfers between devices, per_device(): pieces = lax.all_to_all(pieces, chips, 0, 0)  11.2 us
    pallas_call x1, Pallas kernels, halo_part(): pl.pallas_call(halo_kernel, out_shape=(jax.ShapeDtypeStruct(shape, F32),...  9.12 us
    concatenate x1, local copies, waits for them, and re-layouts, per_device(): feat_ext = jnp.concatenate([gap, edges[0], rows, edges[1], gap], axis=1)  6.74 us
    all_to_all x1, starting transfers between devices, per_device(): lax.all_to_all(jnp.broadcast_to(piece, pieces.shape), chips, 0, 0)  6.67 us
    convert_element_type x2, local copies, waits for them, and re-layouts, per_device(): jnp.transpose(halves, (1, 0, 3, 2, 4)).reshape(K, C, C).astype(F32)  4.77 us
  transfers between devices with their start and end apart: 14, of which 0 were waited for; matrix products, arithmetic and copies ran while one was open for 21% of the time, Pallas kernels for 28%

profile of v1, /device:TPU:1, one launch (start us, length us, event | category | flops | bytes accessed | tf_op | source)
XLA Modules:
  0.0 135.4 jit_solution(16431193568783685324)
XLA Ops:
  0.7 2.1 %fusion.6 = (bf16[2,512,256]{2,1,0:T(8,128)(2,1)}, bf16[2,512,256]{2,1,0:T(8,128)(2,1)S(1)}) fusion(bf16[4,512,256]{2,1,0:T(8,128)(2,1)} %feat_ref.1), kind=kLoop, calls=%fused_computation.53 | loop fusion | bytes 2097152 | tf_op jit(solution)/shard_map/slice | solution.py:220
  2.7 4.9 %collective-permute-start = (bf16[2,512,256]{2,1,0:T(8,128)(2,1)S(1)}, bf16[2,512,256]{2,1,0:T(8,128)(2,1)}, u32[]{:S(2)}, u32[]{:S(2)}) collective-permute-start(bf16[2,512,256]{2,1,0:T(8,128)(2,1)S(1)} %get-tuple-element.20), channel_id=1, source_target_pairs={{0,8},{8,16},{16,24},{24,32},{32,40},{40,48},{48,56},{56,64},{64,7... | collective-permute-start | bytes 1572872 | tf_op jit(solution)/shard_map/ppermute | solution.py:210
  7.7 1.9 %collective-permute-start.1 = (bf16[2,512,256]{2,1,0:T(8,128)(2,1)}, bf16[2,512,256]{2,1,0:T(8,128)(2,1)}, u32[]{:S(2)}, u32[]{:S(2)}) collective-permute-start(bf16[2,512,256]{2,1,0:T(8,128)(2,1)} %get-tuple-element.19), channel_id=1, source_target_pairs={{8,0},{16,8},{24,16},{32,24},{40,32},{48,40},{56,48},{64,56},{72,6... | collective-permute-start | bytes 1572872 | tf_op jit(solution)/shard_map/ppermute | solution.py:210
  10.4 1.3 collective-permute-start.4
  11.6 4.0 %collective-permute-start.5 = (bf16[4,2,256]{2,1,0:T(2,128)(2,1)S(1)}, bf16[4,2,256]{2,1,0:T(2,128)(2,1)S(1)}, u32[]{:S(2)}, u32[]{:S(2)}) collective-permute-start(bf16[4,2,256]{2,1,0:T(2,128)(2,1)S(1)} %get-tuple-element.18), channel_id=1, source_target_pairs={{0,7},{1,0},{2,1},{3,2},{4,3},{5,4},{6,5},{7,6},{8,15},{9,8},{10,9... | collective-permute-start | bytes 12296 | tf_op jit(solution)/shard_map/ppermute | solution.py:210
  18.4 14.8 %own_part.1 = (bf16[2048,2304]{1,0:T(8,128)(2,1)}, f32[256,2304]{1,0:T(8,128)}) custom-call(f32[72,5,256]{2,1,0:T(8,128)} %copy.77.coef_ref, bf16[4,512,256]{2,1,0:T(8,128)(2,1)} %cot_ref.1, bf16[4,512,256]{2,1,0:T(8,128)(2,1)} %feat_ref.1), custom_call_target="tpu_custom_call" | custom-call | flops 10000000000 | bytes 15000000 | tf_op jit(solution)/shard_map/own_part/pallas_call | solution.py:86
  38.9 9.1 %halo_part.1 = (f32[20,128,128]{2,1,0:T(8,128)}, bf16[20,128,128]{2,1,0:T(8,128)(2,1)}) custom-call(s32[1]{0:T(128)} %bitcast.3.core_ref, bf16[2,512,256]{2,1,0:T(8,128)(2,1)} %collective-permute-done.low_ref, bf16[2,512,256]{2,1,0:T(8,128)(2,1)} %collective-permute-done.1.high_ref, bf16[2048,2304]{1,0:T(8,128)(2,1)} %get-tuple-element.7.z_ref, ...), custom_call_target="tpu_custom_call" | custom-call | flops 2400000000 | bytes 15000000 | tf_op jit(solution)/shard_map/halo_part/pallas_call | solution.py:134
  48.0 4.1 %collective-permute-start.6 = (f32[2,9,25]{2,0,1:T(2,128)S(1)}, f32[2,9,25]{2,0,1:T(2,128)S(1)}, u32[]{:S(2)}, u32[]{:S(2)}) collective-permute-start(f32[2,9,25]{2,0,1:T(2,128)S(1)} %get-tuple-element.40), channel_id=1, source_target_pairs={{0,8},{8,16},{16,24},{24,32},{32,40},{40,48},{48,56},{56,64},{64,7... | collective-permute-start | bytes 5408 | tf_op jit(solution)/shard_map/ppermute | solution.py:210
  52.1 1.9 %collective-permute-start.7 = (f32[2,9,25]{2,0,1:T(2,128)S(1)}, f32[2,9,25]{2,0,1:T(2,128)S(1)}, u32[]{:S(2)}, u32[]{:S(2)}) collective-permute-start(f32[2,9,25]{2,0,1:T(2,128)S(1)} %get-tuple-element.41), channel_id=1, source_target_pairs={{8,0},{16,8},{24,16},{32,24},{40,32},{48,40},{56,48},{64,56},{72,6... | collective-permute-start | bytes 5408 | tf_op jit(solution)/shard_map/ppermute | solution.py:210
  54.1 1.5 %copy.84 = bf16[9,256,256]{2,1,0:T(8,128)(2,1)} copy(bf16[9,256,256]{1,2,0:T(8,128)(2,1)S(1)} %bitcast.98) | data formatting | bytes 2359296 | tf_op jit(solution)/shard_map/transpose | solution.py:275
  57.4 2.5 %add_convert_fusion = bf16[20,128,128]{2,1,0:T(8,128)(2,1)} fusion(f32[20,128,128]{2,1,0:T(8,128)} %get-tuple-element.9._, bf16[20,128,128]{2,1,0:T(8,128)(2,1)} %collective-permute-done.10), kind=kLoop, calls=%fused_computation.3 | loop fusion | flops 983040 | bytes 2621440 | tf_op jit(solution)/shard_map/convert_element_type | solution.py:244
  59.9 11.2 %all-to-all-start = ((bf16[64,40,128]{2,1,0:T(8,128)(2,1)}), bf16[64,40,128]{2,1,0:T(8,128)(2,1)}, u32[]{:S(2)}, u32[]{:S(2)}) async-start(bf16[64,40,128]{2,1,0:T(8,128)(2,1)} %bitcast.45), calls=%async_computation | async-start | bytes 1310720 | tf_op jit(solution)/shard_map/all_to_all | solution.py:245
  72.8 3.9 %concatenate.27 = bf16[4,528,256]{2,1,0:T(8,128)(2,1)S(1)} concatenate(bf16[4,6,256]{2,1,0:T(8,128)(2,1)S(1)} %broadcast.79, bf16[4,2,256]{2,1,0:T(2,128)(2,1)S(1)} %collective-permute-done.4, bf16[4,512,256]{2,1,0:T(8,128)(2,1)} %cot_ref.1, bf16[4,2,256]{2,1,0:T(2,128)(2,1)S(1)} %collective-permute-done.5, bf16[4,6,256]{2,1,0:T(8,128)(2,1)S(1)} %broadcast.79), dimensions={1} | concatenate | bytes 2162688 | tf_op jit(solution)/shard_map/concatenate | solution.py:263
  77.5 4.3 %collective-permute-start.3 = (bf16[8,2,256]{2,1,0:T(2,128)(2,1)S(1)}, bf16[8,2,256]{2,1,0:T(2,128)(2,1)S(1)}, u32[]{:S(2)}, u32[]{:S(2)}) collective-permute-start(bf16[8,2,256]{2,1,0:T(2,128)(2,1)S(1)} %get-tuple-element.11), channel_id=1, source_target_pairs={{0,7},{1,0},{2,1},{3,2},{4,3},{5,4},{6,5},{7,6},{8,15},{9,8},{10,9... | collective-permute-start | bytes 24584 | tf_op jit(solution)/shard_map/ppermute | solution.py:210
  82.8 2.3 %collective-permute-start.8 = (bf16[2,528,256]{2,1,0:T(8,128)(2,1)}, bf16[2,528,256]{2,1,0:T(8,128)(2,1)}, u32[]{:S(2)}, u32[]{:S(2)}) collective-permute-start(bf16[2,528,256]{2,1,0:T(8,128)(2,1)} %get-tuple-element.15), channel_id=1, source_target_pairs={{0,8},{8,16},{16,24},{24,32},{32,40},{40,48},{48,56},{56,64},{64,7... | collective-permute-start | bytes 1622024 | tf_op jit(solution)/shard_map/ppermute | solution.py:210
  85.2 2.8 %collective-permute-start.9 = (bf16[2,528,256]{2,1,0:T(8,128)(2,1)}, bf16[2,528,256]{2,1,0:T(8,128)(2,1)}, u32[]{:S(2)}, u32[]{:S(2)}) collective-permute-start(bf16[2,528,256]{2,1,0:T(8,128)(2,1)} %get-tuple-element.16), channel_id=1, source_target_pairs={{8,0},{16,8},{24,16},{32,24},{40,32},{48,40},{56,48},{64,56},{72,6... | collective-permute-start | bytes 1622024 | tf_op jit(solution)/shard_map/ppermute | solution.py:210
  88.0 6.7 %concatenate.23.ext_ref = bf16[8,528,256]{2,1,0:T(8,128)(2,1)} concatenate(bf16[8,6,256]{2,1,0:T(8,128)(2,1)S(1)} %broadcast_in_dim.34, bf16[8,2,256]{2,1,0:T(2,128)(2,1)S(1)} %collective-permute-done.2, bf16[8,512,256]{2,1,0:T(8,128)(2,1)S(1)} %constant_dynamic-update-slice_fusion, bf16[8,2,256]{2,1,0:T(2,128)(2,1)S(1)} %collective-permute-done.3, ...), dimensions={1} | concatenate | bytes 4325376 | tf_op jit(solution)/shard_map/concatenate | solution.py:258
  94.7 1.2 convert_reduce_fusion
  96.9 6.7 %all-to-all-start.1 = ((bf16[64,40,128]{2,1,0:T(8,128)(2,1)}), bf16[64,40,128]{2,1,0:T(8,128)(2,1)S(1)}, u32[]{:S(2)}, u32[]{:S(2)}) async-start(bf16[64,40,128]{2,1,0:T(8,128)(2,1)} %broadcast_in_dim.37), calls=%async_computation.1 | async-start | bytes 1310720 | tf_op jit(solution)/shard_map/all_to_all | solution.py:248
  103.5 11.6 %mixed_part.1 = bf16[4,512,256]{2,1,0:T(8,128)(2,1)} custom-call(f32[4,9,5,240]{3,2,1,0:T(8,128)} %copy.81.coef_ref, bf16[8,528,256]{2,1,0:T(8,128)(2,1)} %concatenate.23.ext_ref, bf16[2304,256]{1,0:T(8,128)(2,1)} %bitcast.97, f32[20,128,128]{2,1,0:T(8,128)} %get-tuple-element.9._), custom_call_target="tpu_custom_call" | custom-call | flops 10000000000 | bytes 5000000 | tf_op jit(solution)/shard_map/mixed_part/pallas_call | solution.py:170
  115.1 2.8 %pad_maximum_fusion.ext_ref = bf16[8,528,256]{2,1,0:T(8,128)(2,1)} fusion(bf16[2,528,256]{2,1,0:T(8,128)(2,1)} %collective-permute-done.9, bf16[4,528,256]{2,1,0:T(8,128)(2,1)S(1)} %concatenate.27, bf16[2,528,256]{2,1,0:T(8,128)(2,1)} %collective-permute-done.8), kind=kLoop, calls=%fused_computation.1 | loop fusion | flops 2162688 | bytes 4325376 | tf_op jit(solution)/shard_map/concatenate | solution.py:266
  118.9 11.5 %grad_input_part.1 = bf16[4,512,256]{2,1,0:T(8,128)(2,1)} custom-call(f32[4,9,5,240]{3,2,1,0:T(8,128)} %copy.85.coef_ref, bf16[8,528,256]{2,1,0:T(8,128)(2,1)} %pad_maximum_fusion.ext_ref, bf16[2304,256]{1,0:T(8,128)(2,1)} %bitcast.99, f32[20,128,128]{2,1,0:T(8,128)} %get-tuple-element.9._), custom_call_target="tpu_custom_call" | custom-call | flops 10000000000 | bytes 5000000 | tf_op jit(solution)/shard_map/grad_input_part/pallas_call | solution.py:170
  130.6 1.8 %copy.86 = f32[9,2,128,2,128]{4,3,2,1,0:T(2,128)S(1)} copy(f32[9,2,128,2,128]{4,2,3,0,1:T(8,128)S(1)} %convert_bitcast_fusion) | data formatting | bytes 4718592 | tf_op jit(solution)/shard_map/convert_element_type | solution.py:254
  132.5 2.9 %reshape.134 = f32[9,256,256]{2,1,0:T(8,128)} reshape(f32[9,2,128,2,128]{4,3,2,1,0:T(2,128)S(1)} %copy.86) | data formatting | bytes 4718592 | tf_op jit(solution)/shard_map/convert_element_type | solution.py:254
  (97 shorter events, 16.4 us)
Async XLA Ops:
  0.6 15.0 %copy-start.4 = (s32[4]{0:T(128)S(1)}, s32[4]{0:T(128)}, u32[]{:S(2)}) copy-start(s32[4]{0:T(128)} %param.10) | copy-start | bytes 52
  0.6 15.0 %copy-start.5 = (s32[4]{0:T(128)S(1)}, s32[4]{0:T(128)}, u32[]{:S(2)}) copy-start(s32[4]{0:T(128)} %param.9) | copy-start | bytes 52
  0.7 15.1 %copy-start.3 = (f32[4,9,25]{2,0,1:T(4,128)S(1)}, f32[4,9,25]{2,0,1:T(4,128)}, u32[]{:S(2)}) copy-start(f32[4,9,25]{2,0,1:T(4,128)} %param.8) | copy-start | bytes 10804
  2.7 33.2 %collective-permute-start = (bf16[2,512,256]{2,1,0:T(8,128)(2,1)S(1)}, bf16[2,512,256]{2,1,0:T(8,128)(2,1)}, u32[]{:S(2)}, u32[]{:S(2)}) collective-permute-start(bf16[2,512,256]{2,1,0:T(8,128)(2,1)S(1)} %get-tuple-element.20), channel_id=1, source_target_pairs={{0,8},{8,16},{16,24},{24,32},{32,40},{40,48},{48,56},{56,64},{64,7... | collective-permute-start | bytes 1572872 | tf_op jit(solution)/shard_map/ppermute | solution.py:210
  7.7 29.4 %collective-permute-start.1 = (bf16[2,512,256]{2,1,0:T(8,128)(2,1)}, bf16[2,512,256]{2,1,0:T(8,128)(2,1)}, u32[]{:S(2)}, u32[]{:S(2)}) collective-permute-start(bf16[2,512,256]{2,1,0:T(8,128)(2,1)} %get-tuple-element.19), channel_id=1, source_target_pairs={{8,0},{16,8},{24,16},{32,24},{40,32},{48,40},{56,48},{64,56},{72,6... | collective-permute-start | bytes 1572872 | tf_op jit(solution)/shard_map/ppermute | solution.py:210
  10.4 24.9 %collective-permute-start.4 = (bf16[4,2,256]{2,1,0:T(2,128)(2,1)S(1)}, bf16[4,2,256]{2,1,0:T(2,128)(2,1)S(1)}, u32[]{:S(2)}, u32[]{:S(2)}) collective-permute-start(bf16[4,2,256]{2,1,0:T(2,128)(2,1)S(1)} %get-tuple-element.17), channel_id=1, source_target_pairs={{0,1},{1,2},{2,3},{3,4},{4,5},{5,6},{6,7},{7,0},{8,9},{9,10},{10,1... | collective-permute-start | bytes 12296 | tf_op jit(solution)/shard_map/ppermute | solution.py:210
  11.6 23.6 %collective-permute-start.5 = (bf16[4,2,256]{2,1,0:T(2,128)(2,1)S(1)}, bf16[4,2,256]{2,1,0:T(2,128)(2,1)S(1)}, u32[]{:S(2)}, u32[]{:S(2)}) collective-permute-start(bf16[4,2,256]{2,1,0:T(2,128)(2,1)S(1)} %get-tuple-element.18), channel_id=1, source_target_pairs={{0,7},{1,0},{2,1},{3,2},{4,3},{5,4},{6,5},{7,6},{8,15},{9,8},{10,9... | collective-permute-start | bytes 12296 | tf_op jit(solution)/shard_map/ppermute | solution.py:210
  18.4 14.9 %copy-start.2 = (bf16[25,4,8,4,4]{0,2,4,3,1:T(8,128)(2,1)S(1)}, bf16[25,4,8,4,4]{0,2,4,3,1:T(8,128)(2,1)}, u32[]{:S(2)}) copy-start(bf16[25,4,8,4,4]{0,2,4,3,1:T(8,128)(2,1)} %constant.78) | copy-start | bytes 76804
  33.3 3.7 %copy-start = (bf16[4,512,256]{2,1,0:T(8,128)(2,1)S(1)}, bf16[4,512,256]{2,1,0:T(8,128)(2,1)}, u32[]{:S(2)}) copy-start(bf16[4,512,256]{2,1,0:T(8,128)(2,1)} %feat_ref.1) | copy-start | bytes 3145732
  38.8 15.3 %copy-start.1 = (bf16[9,256,256]{2,1,0:T(8,128)(2,1)S(1)}, bf16[9,256,256]{2,1,0:T(8,128)(2,1)}, u32[]{:S(2)}) copy-start(bf16[9,256,256]{2,1,0:T(8,128)(2,1)} %param.11) | copy-start | bytes 3538948
  48.0 9.4 %collective-permute-start.10 = (bf16[20,128,128]{2,1,0:T(8,128)(2,1)}, bf16[20,128,128]{2,1,0:T(8,128)(2,1)}, u32[]{:S(2)}, u32[]{:S(2)}) collective-permute-start(bf16[20,128,128]{2,1,0:T(8,128)(2,1)} %get-tuple-element.10), channel_id=1, source_target_pairs={{0,8},{8,0},{1,9},{9,1},{2,10},{10,2},{3,11},{11,3},{4,12},{12,4},... | collective-permute-start | bytes 1966088 | tf_op jit(solution)/shard_map/ppermute | solution.py:243
  48.0 9.2 %collective-permute-start.6 = (f32[2,9,25]{2,0,1:T(2,128)S(1)}, f32[2,9,25]{2,0,1:T(2,128)S(1)}, u32[]{:S(2)}, u32[]{:S(2)}) collective-permute-start(f32[2,9,25]{2,0,1:T(2,128)S(1)} %get-tuple-element.40), channel_id=1, source_target_pairs={{0,8},{8,16},{16,24},{24,32},{32,40},{40,48},{48,56},{56,64},{64,7... | collective-permute-start | bytes 5408 | tf_op jit(solution)/shard_map/ppermute | solution.py:210
  52.1 5.1 %collective-permute-start.7 = (f32[2,9,25]{2,0,1:T(2,128)S(1)}, f32[2,9,25]{2,0,1:T(2,128)S(1)}, u32[]{:S(2)}, u32[]{:S(2)}) collective-permute-start(f32[2,9,25]{2,0,1:T(2,128)S(1)} %get-tuple-element.41), channel_id=1, source_target_pairs={{8,0},{16,8},{24,16},{32,24},{40,32},{48,40},{56,48},{64,56},{72,6... | collective-permute-start | bytes 5408 | tf_op jit(solution)/shard_map/ppermute | solution.py:210
  59.9 34.8 %all-to-all-start = ((bf16[64,40,128]{2,1,0:T(8,128)(2,1)}), bf16[64,40,128]{2,1,0:T(8,128)(2,1)}, u32[]{:S(2)}, u32[]{:S(2)}) async-start(bf16[64,40,128]{2,1,0:T(8,128)(2,1)} %bitcast.45), calls=%async_computation | async-start | bytes 1310720 | tf_op jit(solution)/shard_map/all_to_all | solution.py:245
  76.6 11.3 %collective-permute-start.2 = (bf16[8,2,256]{2,1,0:T(2,128)(2,1)S(1)}, bf16[8,2,256]{2,1,0:T(2,128)(2,1)S(1)}, u32[]{:S(2)}, u32[]{:S(2)}) collective-permute-start(bf16[8,2,256]{2,1,0:T(2,128)(2,1)S(1)} %get-tuple-element.12), channel_id=1, source_target_pairs={{0,1},{1,2},{2,3},{3,4},{4,5},{5,6},{6,7},{7,0},{8,9},{9,10},{10,1... | collective-permute-start | bytes 24584 | tf_op jit(solution)/shard_map/ppermute | solution.py:210
  77.5 10.5 %collective-permute-start.3 = (bf16[8,2,256]{2,1,0:T(2,128)(2,1)S(1)}, bf16[8,2,256]{2,1,0:T(2,128)(2,1)S(1)}, u32[]{:S(2)}, u32[]{:S(2)}) collective-permute-start(bf16[8,2,256]{2,1,0:T(2,128)(2,1)S(1)} %get-tuple-element.11), channel_id=1, source_target_pairs={{0,7},{1,0},{2,1},{3,2},{4,3},{5,4},{6,5},{7,6},{8,15},{9,8},{10,9... | collective-permute-start | bytes 24584 | tf_op jit(solution)/shard_map/ppermute | solution.py:210
  82.8 32.3 %collective-permute-start.8 = (bf16[2,528,256]{2,1,0:T(8,128)(2,1)}, bf16[2,528,256]{2,1,0:T(8,128)(2,1)}, u32[]{:S(2)}, u32[]{:S(2)}) collective-permute-start(bf16[2,528,256]{2,1,0:T(8,128)(2,1)} %get-tuple-element.15), channel_id=1, source_target_pairs={{0,8},{8,16},{16,24},{24,32},{32,40},{40,48},{48,56},{56,64},{64,7... | collective-permute-start | bytes 1622024 | tf_op jit(solution)/shard_map/ppermute | solution.py:210
  85.2 29.9 %collective-permute-start.9 = (bf16[2,528,256]{2,1,0:T(8,128)(2,1)}, bf16[2,528,256]{2,1,0:T(8,128)(2,1)}, u32[]{:S(2)}, u32[]{:S(2)}) collective-permute-start(bf16[2,528,256]{2,1,0:T(8,128)(2,1)} %get-tuple-element.16), channel_id=1, source_target_pairs={{8,0},{16,8},{24,16},{32,24},{40,32},{48,40},{56,48},{64,56},{72,6... | collective-permute-start | bytes 1622024 | tf_op jit(solution)/shard_map/ppermute | solution.py:210
  96.9 21.0 %all-to-all-start.1 = ((bf16[64,40,128]{2,1,0:T(8,128)(2,1)}), bf16[64,40,128]{2,1,0:T(8,128)(2,1)S(1)}, u32[]{:S(2)}, u32[]{:S(2)}) async-start(bf16[64,40,128]{2,1,0:T(8,128)(2,1)} %broadcast_in_dim.37), calls=%async_computation.1 | async-start | bytes 1310720 | tf_op jit(solution)/shard_map/all_to_all | solution.py:248
  117.9 12.5 %collective-permute-start.11 = (bf16[18,128,128]{2,1,0:T(8,128)(2,1)S(1)}, bf16[18,128,128]{2,1,0:T(8,128)(2,1)S(1)}, u32[]{:S(2)}, u32[]{:S(2)}) collective-permute-start(bf16[18,128,128]{2,1,0:T(8,128)(2,1)S(1)} %slice.204), channel_id=1, source_target_pairs={{0,8},{8,0},{1,9},{9,1},{2,10},{10,2},{3,11},{11,3},{4,12},{12,4},... | collective-permute-start | bytes 1769480 | tf_op jit(solution)/shard_map/ppermute | solution.py:250

commit v2 on v1

v2 whole, which is shorter than its diff:
```python
import functools
import math

import jax
import jax.numpy as jnp
from jax import lax
from jax.experimental import pallas as pl
from jax.experimental.pallas import tpu as pltpu
from jax.sharding import Mesh
from jax.sharding import PartitionSpec as P

K = 9
RAD = 2
WIDTH = 2 * RAD + 1
TAPS = WIDTH * WIDTH
ROWS = 4
PLACES = ROWS + 2 * RAD
NJ = 512
C = 256
J = 32
STEPS = NJ // J
EDGE = 16
OWN_WINDOW = 64
EXT_WINDOW = 48
EXT = NJ + 16
LANES = 128
BLOCKS = 2 * K
PADDED_BLOCKS = 20
MIB = 1024 * 1024
BF = jnp.bfloat16
F32 = jnp.float32

IN_VMEM = pl.BlockSpec(memory_space=pltpu.VMEM)
IN_SMEM = pl.BlockSpec(memory_space=pltpu.SMEM)
IN_HBM = pl.BlockSpec(memory_space=pltpu.HBM)
ANYWHERE = pl.BlockSpec(memory_space=pl.ANY)


def in_hbm(array):
    return pltpu.with_memory_space_constraint(array, pltpu.HBM)


def params(mib):
    return pltpu.CompilerParams(vmem_limit_bytes=mib * MIB)


def cost(flops, moved):
    return pl.CostEstimate(flops=int(flops), bytes_accessed=int(moved), transcendentals=0)


def banded(line):
    return pltpu.roll(jnp.broadcast_to(line, (J, 256)), 0, axis=1, stride=1, stride_axis=0).astype(BF)


def one_hot(lane_of_tap):
    tap = lax.broadcasted_iota(jnp.int32, (LANES, 256), 0)
    lane = lax.broadcasted_iota(jnp.int32, (LANES, 256), 1)
    return jnp.where((lane == lane_of_tap(tap)) & (tap < TAPS), 1.0, 0.0).astype(BF)


def send_kernel(lo_ref, hi_ref, basis_ref, feat_ref, cot_ref, chip_ref, link_ref, kept_ref, lines_ref, lo, hi, sems):
    core = lax.axis_index("core")
    to_chip, to_link = 2 - 2 * core, 2 * core
    copies = [
        (lo_ref, lo),
        (hi_ref, hi),
        (feat_ref.at[pl.ds(to_link, 2)], link_ref.at[pl.ds(0, 2), pl.ds(0, NJ)]),
        (cot_ref.at[pl.ds(to_link, 2)], link_ref.at[pl.ds(2, 2), pl.ds(0, NJ)]),
        (feat_ref.at[pl.ds(to_chip, 2)], chip_ref.at[pl.ds(0, 2), pl.ds(0, NJ)]),
        (cot_ref.at[pl.ds(to_chip, 2)], chip_ref.at[pl.ds(2, 2), pl.ds(0, NJ)]),
    ]
    copies = [pltpu.make_async_copy(a, b, sems.at[n]) for n, (a, b) in enumerate(copies)]
    for copy in copies:
        copy.start()
    offset = lax.broadcasted_iota(jnp.int32, (16, LANES), 1) // WIDTH - RAD
    for ref in (chip_ref, link_ref):
        ref[:, NJ:, :] = jnp.zeros((ROWS, 16, C), BF)
    copies[0].wait()
    copies[1].wait()
    lines = jnp.zeros((16, 256), F32)
    for i in range(ROWS):
        cells = jnp.pad(basis_ref[:, i, :], ((0, 16 - K), (0, LANES - TAPS)))
        cells = jnp.where((offset >= lo[i]) & (offset <= hi[i]), cells, jnp.zeros_like(cells)).astype(BF)
        kept_ref[i] = cells
        place = one_hot(lambda tap, i=i: i * OWN_WINDOW + (TAPS - 1 - tap) - WIDTH * i + 16)
        lines = lines + jnp.dot(cells, place, preferred_element_type=F32)
    lines_ref[...] = lines
    for n in range(2):
        link_ref[2 + n, NJ:, 0:LANES] = kept_ref[to_link + n]
        chip_ref[2 + n, NJ:, 0:LANES] = kept_ref[to_chip + n]
    for copy in copies[2:]:
        copy.wait()


def send_part(span_lo, span_hi, basis, features, cotangent):
    return pl.pallas_call(
        send_kernel,
        out_shape=(
            pltpu.VMEM((ROWS, EXT, C), BF),
            pltpu.VMEM((ROWS, EXT, C), BF),
            pltpu.VMEM((ROWS, 16, LANES), BF),
            pltpu.VMEM((16, 256), F32),
        ),
        in_specs=[IN_HBM, IN_HBM, IN_VMEM, IN_HBM, IN_HBM],
        out_specs=[IN_VMEM] * 4,
        scratch_shapes=[
            pltpu.SMEM((ROWS,), jnp.int32),
            pltpu.SMEM((ROWS,), jnp.int32),
            pltpu.SemaphoreType.DMA((6,)),
        ],
        compiler_params=params(8),
        cost_estimate=cost(0, 4e6),
        name="send_part",
    )(in_hbm(span_lo), in_hbm(span_hi), jnp.transpose(basis, (1, 0, 2)), in_hbm(features), in_hbm(cotangent))


def own_kernel(lines_ref, cot_ref, feat_ref, z_ref, grad_ref, bands_ref, to_right_ref, to_left_ref, padded, z_own):
    zero = jnp.zeros((ROWS, EDGE, C), BF)
    padded[:, 0:EDGE, :] = zero
    padded[:, EDGE + NJ :, :] = zero
    padded[:, EDGE : EDGE + NJ, :] = cot_ref[...]
    to_right_ref[...] = cot_ref[:, NJ - EDGE :, :]
    to_left_ref[...] = cot_ref[:, :EDGE, :]
    window_cell = lax.broadcasted_iota(jnp.int32, (16, 256), 1) % OWN_WINDOW
    inside = (window_cell >= EDGE - RAD) & (window_cell <= EDGE + RAD)
    for place in range(PLACES):
        lines = pltpu.roll(lines_ref[...], (WIDTH * place - 22) % 256, axis=1)
        lines = jnp.where(inside, lines, jnp.zeros_like(lines))
        for k in range(K):
            block = place * K + k
            bands_ref[block * J : (block + 1) * J, :] = banded(lines[k : k + 1, :])

    def step(tile, _):
        start = pl.multiple_of(tile * J, J)
        cells = jnp.concatenate([padded[i, pl.ds(start, OWN_WINDOW), :] for i in range(ROWS)], axis=0)
        for place in range(PLACES):
            found = jnp.dot(
                bands_ref[place * K * J : (place + 1) * K * J, :], cells, preferred_element_type=F32
            ).astype(BF)
            for k in range(K):
                piece = found[k * J : (k + 1) * J]
                columns = slice(k * C, (k + 1) * C)
                if 2 <= place < 6:
                    z_own[pl.ds((place - 2) * NJ + start, J), columns] = piece
                else:
                    halo = place if place < 2 else place - 4
                    z_ref[pl.ds(halo * NJ + start, J), columns] = piece
        return 0

    lax.fori_loop(0, STEPS, step, 0, unroll=4)
    turned = feat_ref[...].reshape(ROWS * NJ, C).T
    for k in range(K):
        columns = slice(k * C, (k + 1) * C)
        grad_ref[:, columns] = jnp.dot(turned, z_own[:, columns], preferred_element_type=F32)


def own_part(lines, cotangent, features):
    return pl.pallas_call(
        own_kernel,
        out_shape=(
            pltpu.VMEM((ROWS * NJ, K * C), BF),
            pltpu.VMEM((C, K * C), F32),
            pltpu.VMEM((PLACES * K * J, 256), BF),
            pltpu.VMEM((ROWS, EDGE, C), BF),
            pltpu.VMEM((ROWS, EDGE, C), BF),
        ),
        in_specs=[IN_VMEM] * 3,
        out_specs=[IN_VMEM] * 5,
        scratch_shapes=[
            pltpu.VMEM((ROWS, NJ + 2 * EDGE, C), BF),
            pltpu.VMEM((ROWS * NJ, K * C), BF),
        ],
        compiler_params=params(18),
        cost_estimate=cost(10e9, 4e6),
        name="own_part",
    )(lines, cotangent, features)


def halo_kernel(
    chip_ref, link_ref, left_ref, right_ref, feat_ref, z_ref, grad_ref, bands_ref,
    own_ref, other_ref, to_right_ref, to_left_ref, total, edge_z,
):
    core = lax.axis_index("core")
    from_chip = chip_ref[0:2, 0:NJ, :].reshape(2 * NJ, C).T
    from_link = link_ref[0:2, 0:NJ, :].reshape(2 * NJ, C).T
    chip_rows = pl.ds(pl.multiple_of((1 - core) * 2 * NJ, 2 * NJ), 2 * NJ)
    link_rows = pl.ds(pl.multiple_of(core * 2 * NJ, 2 * NJ), 2 * NJ)
    gap = jnp.zeros((OWN_WINDOW - 2 * EDGE, C), BF)
    pieces = []
    for i in range(ROWS):
        pieces += [left_ref[i], gap, right_ref[i]]
    cells = jnp.concatenate(pieces, axis=0)
    for place in range(PLACES):
        found = jnp.dot(
            bands_ref[place * K * J : (place + 1) * K * J, :], cells, preferred_element_type=F32
        ).astype(BF)
        for k in range(K):
            edge_z[place * J : (place + 1) * J, k * C : (k + 1) * C] = found[k * J : (k + 1) * J]
    first, last = slice(0, EDGE), slice(NJ - EDGE, NJ)

    def ends(n):
        chip = [chip_ref[n, part, :] for part in (first, last)]
        link = [link_ref[n, part, :] for part in (first, last)]
        low = [jnp.where(core == 0, b, a) for a, b in zip(chip, link, strict=True)]
        high = [jnp.where(core == 0, a, b) for a, b in zip(chip, link, strict=True)]
        return low, high

    halo = [ends(n) for n in range(4)]
    rows = [halo[0][0], halo[1][0]]
    rows += [[feat_ref[i, part, :] for part in (first, last)] for i in range(ROWS)]
    rows += [halo[0][1], halo[1][1]]
    edge_feat = jnp.concatenate([end for row in rows for end in row], axis=0).T
    for n, row in enumerate(rows + [halo[2][0], halo[3][0], halo[2][1], halo[3][1]]):
        to_left_ref[n], to_right_ref[n] = row
    for k in range(K):
        columns = slice(k * C, (k + 1) * C)
        total[:, columns] = (
            grad_ref[:, columns]
            + jnp.dot(from_chip, z_ref[chip_rows, columns], preferred_element_type=F32)
            + jnp.dot(from_link, z_ref[link_rows, columns], preferred_element_type=F32)
            + jnp.dot(edge_feat, edge_z[:, columns], preferred_element_type=F32)
        )
    mine = pl.multiple_of(core * LANES, LANES)
    theirs = pl.multiple_of((1 - core) * LANES, LANES)
    for block in range(BLOCKS):
        columns = slice(block * LANES, (block + 1) * LANES)
        own_ref[block] = total[pl.ds(mine, LANES), columns]
        other_ref[block] = total[pl.ds(theirs, LANES), columns].astype(BF)
    for block in range(BLOCKS, PADDED_BLOCKS):
        own_ref[block] = jnp.zeros((LANES, LANES), F32)
        other_ref[block] = jnp.zeros((LANES, LANES), BF)


def halo_part(chip, link, left, right, features, z, grad, bands):
    shape = (PADDED_BLOCKS, LANES, LANES)
    return pl.pallas_call(
        halo_kernel,
        out_shape=(
            pltpu.VMEM(shape, F32),
            pltpu.VMEM(shape, BF),
            pltpu.VMEM((12, EDGE, C), BF),
            pltpu.VMEM((12, EDGE, C), BF),
        ),
        in_specs=[IN_VMEM] * 8,
        out_specs=[IN_VMEM] * 4,
        scratch_shapes=[pltpu.VMEM((C, K * C), F32), pltpu.VMEM((PLACES * J, K * C), BF)],
        compiler_params=params(14),
        cost_estimate=cost(4e9, 4e6),
        name="halo_part",
    )(chip, link, left, right, features, z, grad, bands)


def half_kernel(own_ref, other_ref, to_right_in, to_left_in, out_ref, to_right_ref, to_left_ref):
    out_ref[...] = (own_ref[...] + other_ref[...].astype(F32)).astype(BF)
    to_right_ref[...] = to_right_in[...]
    to_left_ref[...] = to_left_in[...]


def half_part(own, other, to_right, to_left):
    return pl.pallas_call(
        half_kernel,
        out_shape=(
            pltpu.VMEM(own.shape, BF),
            pltpu.VMEM(to_right.shape, BF),
            pltpu.VMEM(to_left.shape, BF),
        ),
        in_specs=[IN_VMEM] * 4,
        out_specs=[IN_VMEM] * 3,
        compiler_params=params(4),
        cost_estimate=cost(1e6, 3e6),
        name="half_part",
    )(own, other, to_right, to_left)


def sum_kernel(scale, pieces_ref, _, out_ref):
    piece = (jnp.sum(pieces_ref[...].astype(F32), axis=0) * scale).astype(BF)
    out_ref[...] = jnp.broadcast_to(piece, out_ref.shape)


def sum_part(pieces, scale, after):
    return pl.pallas_call(
        functools.partial(sum_kernel, scale),
        out_shape=pltpu.VMEM(pieces.shape, BF),
        in_specs=[IN_VMEM, ANYWHERE],
        out_specs=IN_VMEM,
        compiler_params=params(4),
        cost_estimate=cost(1e6, 2e6),
        name="sum_part",
    )(pieces, after)


def order_kernel(*_):
    pass


def ordered(value, after):
    return pl.pallas_call(
        order_kernel,
        out_shape=jax.ShapeDtypeStruct(value.shape, value.dtype),
        in_specs=[ANYWHERE, ANYWHERE],
        out_specs=ANYWHERE,
        input_output_aliases={0: 0},
        compiler_params=params(1),
        name="ordered",
    )(value, after)


def result_kernel(own_ref, other_ref, out_ref):
    core = lax.axis_index("core")
    for n in range(out_ref.shape[0]):
        for part in range(2):
            columns = slice(part * LANES, (part + 1) * LANES)
            mine = own_ref[2 * n + part].astype(F32)
            theirs = other_ref[2 * n + part].astype(F32)
            out_ref[n, pl.ds(pl.multiple_of(core * LANES, LANES), LANES), columns] = mine
            out_ref[n, pl.ds(pl.multiple_of((1 - core) * LANES, LANES), LANES), columns] = theirs


def result_part(own, other):
    step = 3
    return pl.pallas_call(
        result_kernel,
        grid=(K // step,),
        out_shape=jax.ShapeDtypeStruct((K, C, C), F32),
        in_specs=[pl.BlockSpec((2 * step, LANES, LANES), lambda n: (n, 0, 0))] * 2,
        out_specs=pl.BlockSpec((step, C, C), lambda n: (n, 0, 0)),
        compiler_params=params(6),
        cost_estimate=cost(1e6, 4e6),
        name="result_part",
    )(own, other)


def mix_rows(lines, extended, weight_copy, weight, out_ref, bands, filtered, mixed, sems, turned=None):
    copies = [pltpu.make_async_copy(mixed.at[row], out_ref.at[row], sems.at[row]) for row in range(ROWS)]
    for row in range(ROWS):
        slot = row % 2
        for k in range(K):
            bands[slot, k * J : (k + 1) * J, :] = banded(lines[row][k : k + 1, :])[:, : WIDTH * EXT_WINDOW]
        for tile in range(STEPS):
            start = tile * J
            cells = jnp.concatenate(
                [extended[row + r, start : start + EXT_WINDOW, :] for r in range(WIDTH)], axis=0
            )
            found = jnp.dot(bands[slot], cells, preferred_element_type=F32).astype(BF)
            for k in range(K):
                filtered[slot, start : start + J, k * C : (k + 1) * C] = found[k * J : (k + 1) * J]
        if row == 0:
            weight_copy.wait()
            if turned is not None:
                for k in range(K):
                    turned[k * C : (k + 1) * C, :] = weight[k].T
                weight = turned
        mixed[row] = jnp.dot(filtered[slot], weight[...], preferred_element_type=F32).astype(BF)
        copies[row].start()
    for copy in copies:
        copy.wait()


def extend(extended, n, row, left, right):
    extended[n] = jnp.concatenate([left[8:], row, right[:8]], axis=0)


def mixed_kernel(kept_ref, chip_ref, link_ref, left_ref, right_ref, feat_hbm, weight_hbm, _, out_ref, done_ref, feat, weight, extended, bands, filtered, mixed, sems):
    core = lax.axis_index("core")
    feat_copy = pltpu.make_async_copy(feat_hbm, feat, sems.at[ROWS])
    weight_copy = pltpu.make_async_copy(weight_hbm, weight, sems.at[ROWS + 1])
    feat_copy.start()
    weight_copy.start()

    def fill(low, high):
        for n in range(2):
            extend(extended, n, low[n, 0:NJ, :], left_ref[n], right_ref[n])
            extend(extended, 6 + n, high[n, 0:NJ, :], left_ref[6 + n], right_ref[6 + n])

    pl.when(core == 0)(lambda: fill(link_ref, chip_ref))
    pl.when(core == 1)(lambda: fill(chip_ref, link_ref))
    place = one_hot(lambda tap: tap // WIDTH * EXT_WINDOW + 8 - RAD + tap % WIDTH)
    lines = [jnp.dot(kept_ref[row], place, preferred_element_type=F32) for row in range(ROWS)]
    feat_copy.wait()
    for n in range(ROWS):
        extend(extended, 2 + n, feat[n], left_ref[2 + n], right_ref[2 + n])
    mix_rows(lines, extended, weight_copy, weight, out_ref, bands, filtered, mixed, sems)
    done_ref[...] = jnp.zeros_like(done_ref)


def grad_kernel(kept_ref, chip_ref, link_ref, near_left_ref, near_right_ref, left_ref, right_ref, cot_hbm, weight_hbm, _, out_ref, done_ref, cot, weight, extended, bands, filtered, mixed, sems, cells, turned):
    core = lax.axis_index("core")
    cot_copy = pltpu.make_async_copy(cot_hbm, cot, sems.at[ROWS])
    weight_copy = pltpu.make_async_copy(weight_hbm, weight, sems.at[ROWS + 1])
    cot_copy.start()
    weight_copy.start()

    def fill(low, high):
        for n in range(2):
            extend(extended, n, low[2 + n, 0:NJ, :], left_ref[PLACES + n], right_ref[PLACES + n])
            extend(extended, 6 + n, high[2 + n, 0:NJ, :], left_ref[PLACES + 2 + n], right_ref[PLACES + 2 + n])
            cells[n] = low[2 + n, NJ:, 0:LANES]
            cells[6 + n] = high[2 + n, NJ:, 0:LANES]

    pl.when(core == 0)(lambda: fill(link_ref, chip_ref))
    pl.when(core == 1)(lambda: fill(chip_ref, link_ref))
    for n in range(ROWS):
        cells[2 + n] = kept_ref[n]

    away = (TAPS - 1 - lax.broadcasted_iota(jnp.int32, (16, LANES), 1)) // WIDTH
    place = one_hot(lambda tap: (TAPS - 1 - tap) // WIDTH * EXT_WINDOW + 8 - RAD + (TAPS - 1 - tap) % WIDTH)
    lines = []
    for row in range(ROWS):
        taken = jnp.zeros((16, LANES), F32)
        for r in range(WIDTH):
            taken = jnp.where(away == r, cells[row + r].astype(F32), taken)
        lines.append(jnp.dot(taken.astype(BF), place, preferred_element_type=F32))
    cot_copy.wait()
    for n in range(ROWS):
        extend(extended, 2 + n, cot[n], near_left_ref[n], near_right_ref[n])
    mix_rows(lines, extended, weight_copy, weight, out_ref, bands, filtered, mixed, sems, turned)
    done_ref[...] = jnp.zeros_like(done_ref)


def mix_part(kernel, operands, field, weight, after, extra, name):
    return pl.pallas_call(
        kernel,
        out_shape=(jax.ShapeDtypeStruct((ROWS, NJ, C), BF), pltpu.VMEM((8, LANES), F32)),
        in_specs=[IN_VMEM] * len(operands) + [IN_HBM, IN_HBM, ANYWHERE],
        out_specs=[IN_HBM, IN_VMEM],
        scratch_shapes=[
            pltpu.VMEM(field.shape, BF),
            pltpu.VMEM(weight.shape, BF),
            pltpu.VMEM((PLACES, EXT, C), BF),
            pltpu.VMEM((2, K * J, WIDTH * EXT_WINDOW), BF),
            pltpu.VMEM((2, NJ, K * C), BF),
            pltpu.VMEM((ROWS, NJ, C), BF),
            pltpu.SemaphoreType.DMA((ROWS + 2,)),
        ]
        + extra,
        compiler_params=params(20),
        cost_estimate=cost(8e9, 5e6),
        name=name,
    )(*operands, in_hbm(field), in_hbm(weight), after)


def shifted(block, axis, count, step, periodic):
    route = [(i, (i + step) % count) for i in range(count) if periodic or 0 <= i + step < count]
    return lax.ppermute(block, axis, route)


def per_device(features, basis, span_lo, span_hi, weight, cotangent):
    lat, chips = ("yz", "core"), ("yz", "lon")
    lats, lons = lax.axis_size("yz") * lax.axis_size("core"), lax.axis_size("lon")
    parts = lax.axis_size("yz") * lons
    swap = [(0, 1), (1, 0)]

    chip, link, kept, lines = send_part(span_lo, span_hi, basis, features, cotangent)
    pairs = [(i, i + 1) for i in range(1, lats - 1, 2)]
    link = lax.ppermute(link, lat, pairs + [(b, a) for a, b in pairs])
    chip = lax.ppermute(chip, "core", swap)

    z, grad_own, bands, to_right, to_left = own_part(lines, cotangent, features)
    near_left = shifted(to_right, "lon", lons, 1, True)
    near_right = shifted(to_left, "lon", lons, -1, True)
    own, other, to_right, to_left = halo_part(
        chip, link, near_left, near_right, features, z, grad_own, bands
    )

    half, to_right, to_left = half_part(own, lax.ppermute(other, "core", swap), to_right, to_left)
    pieces = lax.all_to_all(half.reshape(parts, -1, LANES), chips, 0, 0)
    left = shifted(to_right, "lon", lons, 1, True)
    right = shifted(to_left, "lon", lons, -1, True)
    mixed, mixed_done = mix_part(
        mixed_kernel, (kept, chip, link, left, right), features, weight.reshape(K * C, C), half, [],
        "mixed_part",
    )
    scale = 1.0 / math.sqrt(ROWS * lats * NJ * lons)
    copies = sum_part(pieces, scale, mixed_done)
    gathered = lax.all_to_all(copies, chips, 0, 0).reshape(PADDED_BLOCKS, LANES, LANES)
    grad_input, grad_done = mix_part(
        grad_kernel,
        (kept, chip, link, near_left, near_right, left, right),
        cotangent, weight, copies,
        [pltpu.VMEM((PLACES, 16, LANES), BF), pltpu.VMEM((K * C, C), BF)],
        "grad_input_part",
    )
    gathered = ordered(gathered, grad_done)
    grad_weight = result_part(gathered, lax.ppermute(gathered, "core", swap))
    return mixed, grad_input, grad_weight


def solution(mesh):
    lats, lons = mesh.devices.shape
    split = Mesh(mesh.devices.reshape(lats // 2, 2, lons), ("yz", "core", "lon"))
    lat = ("yz", "core")
    return jax.shard_map(
        per_device,
        mesh=split,
        in_specs=(P(lat, "lon", None), P(lat, None, None), P(lat), P(lat), P(), P(lat, "lon", None)),
        out_specs=(P(lat, "lon", None), P(lat, "lon", None), P()),
        check_vma=False,
    )
```

time: 136 us -> 83.3 us (0.61)
  local copies, waits for them, and re-layouts: 33 us -> 0.87 us
  starting transfers between devices: 47.2 us -> 34.3 us
  Pallas kernels: 47.1 us -> 35.3 us
  waiting for transfers between devices: 0.04 us -> 11.7 us
  other arithmetic: 6.95 us -> 0 us
    ppermute x10 -> x4, starting transfers between devices: 28.4 us -> 10.4 us  [shifted(): return lax.ppermute(block, axis, route)]
    concatenate x4 -> x0, local copies, waits for them, and re-layouts: 11.8 us -> none  [the longest x1 6.74 us: per_device(): feat_ext = jnp.concatenate([gap, edges[0], rows, edges[1], gap], axis=1)]
    pallas_call x4 -> x9, Pallas kernels: 47.1 us -> 35.3 us  [the longest x2 16.9 us: mix_part(): pl.pallas_call(kernel, out_shape=(jax.ShapeDtypeStruct((ROWS, NJ, C), BF)...]
    ppermute x2 -> x4, starting transfers between devices: 0.92 us -> 9.21 us  [the longest x1 4.09 us: per_device(): grad_weight = result_part(gathered, lax.ppermute(gathered, 'core', swap))]
    all_to_all x2, waiting for transfers between devices: 0.01 us -> 6.66 us  [the longest x1 4.02 us: per_device(): pieces = lax.all_to_all(half.reshape(parts, -1, LANES), chips, 0, 0)]
    convert_element_type x4 -> x0, local copies, waits for them, and re-layouts: 5.9 us -> none  [the longest x2 4.77 us: per_device(): jnp.transpose(halves, (1, 0, 3, 2, 4)).reshape(K, C, C).astype(F32)]
    slice x18 -> x0, local copies, waits for them, and re-layouts: 4.42 us -> none  [the longest x1 2.08 us: per_device(): high = shifted(features[:2], lat, lats, -1, False)]
    reshape x10 -> x0, local copies, waits for them, and re-layouts: 4.23 us -> none  [the longest x2 1.41 us: per_device(): own_coef = jnp.repeat(own_coef, OWN_WINDOW, axis=2)]
  transfers between devices with their start and end apart: 14 -> 10, of which waited for: 0 -> 5; matrix products, arithmetic and copies ran while one was open for 21% -> 0% of each run, Pallas kernels for 28% -> 32%
where the time goes in v2:
time: 83.3 us; the launch traced here: 82.9 us
  Pallas kernels  35.3 us (42%)
  starting transfers between devices  34.3 us (41%)
  waiting for transfers between devices  11.7 us (14%)
  local copies, waits for them, and re-layouts  0.87 us (1%)
    pallas_call x2, Pallas kernels, mix_part(): pl.pallas_call(kernel, out_shape=(jax.ShapeDtypeStruct((ROWS, NJ, C), BF)...  16.9 us
    ppermute x4, starting transfers between devices, shifted(): return lax.ppermute(block, axis, route)  10.4 us
    pallas_call x1, Pallas kernels, own_part(): pl.pallas_call(own_kernel, out_shape=(pltpu.VMEM((ROWS * NJ, K * C), BF),...  9.25 us
    all_to_all x1, starting transfers between devices, per_device(): pieces = lax.all_to_all(half.reshape(parts, -1, LANES), chips, 0, 0)  8.74 us
    all_to_all x1, starting transfers between devices, per_device(): lax.all_to_all(copies, chips, 0, 0).reshape(PADDED_BLOCKS, LANES, LANES)  5.91 us
    ppermute x1, starting transfers between devices, per_device(): grad_weight = result_part(gathered, lax.ppermute(gathered, 'core', swap))  4.09 us
    all_to_all x1, waiting for transfers between devices, per_device(): pieces = lax.all_to_all(half.reshape(parts, -1, LANES), chips, 0, 0)  4.02 us
    pallas_call x1, Pallas kernels, halo_part(): pl.pallas_call(halo_kernel, out_shape=(pltpu.VMEM(shape, F32), pltpu.VMEM...  3.8 us
  transfers between devices with their start and end apart: 10, of which 5 were waited for; matrix products, arithmetic and copies ran while one was open for 0% of the time, Pallas kernels for 32%

profile of v2, /device:TPU:1, one launch (start us, length us, event | category | flops | bytes accessed | tf_op | source)
XLA Modules:
  0.0 82.9 jit_solution(2364813224794938853)
XLA Ops:
  0.6 0.0 copy-start
  0.7 0.9 %copy-done.2 = f32[4,9,25]{2,0,1:T(4,128)S(1)} copy-done((f32[4,9,25]{2,0,1:T(4,128)S(1)}, f32[4,9,25]{2,0,1:T(4,128)}, u32[]{:S(2)}) %copy-start.2) | copy-done | bytes 3624
  1.5 1.6 %send_part.1 = (bf16[4,528,256]{2,1,0:T(8,128)(2,1)S(1)}, bf16[4,528,256]{2,1,0:T(8,128)(2,1)S(1)}, bf16[4,16,128]{2,1,0:T(8,128)(2,1)S(1)}, f32[16,256]{1,0:T(8,128)S(1)}) custom-call(s32[4]{0:T(128)} %lo_ref.1, s32[4]{0:T(128)} %hi_ref.1, f32[9,4,25]{2,1,0:T(4,128)S(1)} %bitcast.5, bf16[4,512,256]{2,1,0:T(8,128)(2,1)} %feat_hbm.1, bf16[4,512,256]{2,1,0:T(8,128)(2,1)} %cot_hbm.1), custom_call_target="tpu_custom_call" | custom-call | bytes 4000000 | tf_op jit(solution)/shard_map/send_part/pallas_call | solution.py:96
  3.1 1.5 %collective-permute-start = (bf16[4,528,256]{2,1,0:T(8,128)(2,1)S(1)}, bf16[4,528,256]{2,1,0:T(8,128)(2,1)S(1)}, u32[]{:S(2)}, u32[]{:S(2)}) collective-permute-start(bf16[4,528,256]{2,1,0:T(8,128)(2,1)S(1)} %get-tuple-element.24), channel_id=1, source_target_pairs={{0,8},{8,0},{1,9},{9,1},{2,10},{10,2},{3,11},{11,3},{4,12},{12,4},... | collective-permute-start | bytes 3244040 | tf_op jit(solution)/shard_map/ppermute | solution.py:456
  4.6 3.5 %collective-permute-start.1 = (bf16[4,528,256]{2,1,0:T(8,128)(2,1)S(1)}, bf16[4,528,256]{2,1,0:T(8,128)(2,1)S(1)}, u32[]{:S(2)}, u32[]{:S(2)}) collective-permute-start(bf16[4,528,256]{2,1,0:T(8,128)(2,1)S(1)} %get-tuple-element.25), channel_id=1, source_target_pairs={{8,16},{24,32},{40,48},{56,64},{72,80},{88,96},{104,112},{16,8},{3... | collective-permute-start | bytes 3244040 | tf_op jit(solution)/shard_map/ppermute | solution.py:455
  8.2 9.3 %own_part.1 = (bf16[2048,2304]{1,0:T(8,128)(2,1)S(1)}, f32[256,2304]{1,0:T(8,128)S(1)}, bf16[2304,256]{1,0:T(8,128)(2,1)S(1)}, bf16[4,16,256]{2,1,0:T(8,128)(2,1)S(1)}, bf16[4,16,256]{2,1,0:T(8,128)(2,1)S(1)}) custom-call(f32[16,256]{1,0:T(8,128)S(1)} %get-tuple-element.26.lines_ref, bf16[4,512,256]{2,1,0:T(8,128)(2,1)S(1)} %copy-done.1, ...), custom_call_target="tpu_custom_call" | custom-call | flops 10000000000 | bytes 4000000 | tf_op jit(solution)/shard_map/own_part/pallas_call | solution.py:158
  17.4 1.3 %collective-permute-start.2 = (bf16[4,16,256]{2,1,0:T(8,128)(2,1)S(1)}, bf16[4,16,256]{2,1,0:T(8,128)(2,1)S(1)}, u32[]{:S(2)}, u32[]{:S(2)}) collective-permute-start(bf16[4,16,256]{2,1,0:T(8,128)(2,1)S(1)} %get-tuple-element.27), channel_id=1, source_target_pairs={{0,1},{1,2},{2,3},{3,4},{4,5},{5,6},{6,7},{7,0},{8,9},{9,10},{10,1... | collective-permute-start | bytes 98312 | tf_op jit(solution)/shard_map/ppermute | solution.py:444
  18.7 4.0 %collective-permute-start.3 = (bf16[4,16,256]{2,1,0:T(8,128)(2,1)S(1)}, bf16[4,16,256]{2,1,0:T(8,128)(2,1)S(1)}, u32[]{:S(2)}, u32[]{:S(2)}) collective-permute-start(bf16[4,16,256]{2,1,0:T(8,128)(2,1)S(1)} %get-tuple-element.28), channel_id=1, source_target_pairs={{0,7},{1,0},{2,1},{3,2},{4,3},{5,4},{6,5},{7,6},{8,15},{9,8},{10,9... | collective-permute-start | bytes 98312 | tf_op jit(solution)/shard_map/ppermute | solution.py:444
  22.7 1.2 %collective-permute-done.2.left_ref.near_left_ref = bf16[4,16,256]{2,1,0:T(8,128)(2,1)S(1)} collective-permute-done((bf16[4,16,256]{2,1,0:T(8,128)(2,1)S(1)}, bf16[4,16,256]{2,1,0:T(8,128)(2,1)S(1)}, u32[]{:S(2)}, u32[]{:S(2)}) %collective-permute-start.2) | collective-permute-done | bytes 32800 | tf_op jit(solution)/shard_map/ppermute | solution.py:444
  23.9 3.8 %halo_part.1 = (f32[20,128,128]{2,1,0:T(8,128)S(1)}, bf16[20,128,128]{2,1,0:T(8,128)(2,1)S(1)}, bf16[12,16,256]{2,1,0:T(8,128)(2,1)S(1)}, bf16[12,16,256]{2,1,0:T(8,128)(2,1)S(1)}) custom-call(bf16[4,528,256]{2,1,0:T(8,128)(2,1)S(1)} %collective-permute-done.chip_ref, bf16[4,528,256]{2,1,0:T(8,128)(2,1)S(1)} %collective-permute-done.1.link_ref, ...), custom_call_target="tpu_custom_call" | custom-call | flops 4000000000 | bytes 4000000 | tf_op jit(solution)/shard_map/halo_part/pallas_call | solution.py:236
  27.7 0.1 collective-permute-start.4
  27.8 2.1 %collective-permute-done.4.other_ref = bf16[20,128,128]{2,1,0:T(8,128)(2,1)S(1)} collective-permute-done((bf16[20,128,128]{2,1,0:T(8,128)(2,1)S(1)}, bf16[20,128,128]{2,1,0:T(8,128)(2,1)S(1)}, u32[]{:S(2)}, u32[]{:S(2)}) %collective-permute-start.4) | collective-permute-done | bytes 655392 | tf_op jit(solution)/shard_map/ppermute | solution.py:465
  29.9 1.0 %half_part.1 = (bf16[20,128,128]{2,1,0:T(8,128)(2,1)}, bf16[12,16,256]{2,1,0:T(8,128)(2,1)S(1)}, bf16[12,16,256]{2,1,0:T(8,128)(2,1)S(1)}) custom-call(f32[20,128,128]{2,1,0:T(8,128)S(1)} %get-tuple-element.32.own_ref, bf16[20,128,128]{2,1,0:T(8,128)(2,1)S(1)} %collective-permute-done.4.other_ref, bf16[12,16,256]{2,1,0:T(8,128)(2,1)S(1)} %get-tuple-element.34.to_right_in, ...), custom_call_target="tpu_custom_call" | custom-call | flops 1000000 | bytes 3000000 | tf_op jit(solution)/shard_map/half_part/pallas_call | solution.py:260
  30.9 5.2 %collective-permute-start.6 = (bf16[12,16,256]{2,1,0:T(8,128)(2,1)S(1)}, bf16[12,16,256]{2,1,0:T(8,128)(2,1)S(1)}, u32[]{:S(2)}, u32[]{:S(2)}) collective-permute-start(bf16[12,16,256]{2,1,0:T(8,128)(2,1)S(1)} %get-tuple-element.37), channel_id=1, source_target_pairs={{0,7},{1,0},{2,1},{3,2},{4,3},{5,4},{6,5},{7,6},{8,15},{9,8},{10,9... | collective-permute-start | bytes 294920 | tf_op jit(solution)/shard_map/ppermute | solution.py:444
  36.0 8.7 %all-to-all-start = ((bf16[64,40,128]{2,1,0:T(8,128)(2,1)}), bf16[64,40,128]{2,1,0:T(8,128)(2,1)S(1)}, u32[]{:S(2)}, u32[]{:S(2)}) async-start(bf16[64,40,128]{2,1,0:T(8,128)(2,1)} %bitcast.2), calls=%async_computation | async-start | bytes 1310720 | tf_op jit(solution)/shard_map/all_to_all | solution.py:466
  44.8 8.4 %mixed_part.1 = (bf16[4,512,256]{2,1,0:T(8,128)(2,1)}, f32[8,128]{1,0:T(8,128)S(1)}) custom-call(bf16[4,16,128]{2,1,0:T(8,128)(2,1)S(1)} %get-tuple-element.23.kept_ref, bf16[4,528,256]{2,1,0:T(8,128)(2,1)S(1)} %collective-permute-done.chip_ref, bf16[4,528,256]{2,1,0:T(8,128)(2,1)S(1)} %collective-permute-done.1.link_ref, ...), custom_call_target="tpu_custom_call" | custom-call | flops 8000000000 | bytes 5000000 | tf_op jit(solution)/shard_map/mixed_part/pallas_call | solution.py:421
  53.2 4.0 %all-to-all-done.pieces_ref = bf16[64,40,128]{2,1,0:T(8,128)(2,1)S(1)} async-done(((bf16[64,40,128]{2,1,0:T(8,128)(2,1)}), bf16[64,40,128]{2,1,0:T(8,128)(2,1)S(1)}, u32[]{:S(2)}, u32[]{:S(2)}) %all-to-all-start) | async-done | bytes 655392 | tf_op jit(solution)/shard_map/all_to_all | solution.py:466
  57.2 1.0 %sum_part.1._ = bf16[64,40,128]{2,1,0:T(8,128)(2,1)} custom-call(bf16[64,40,128]{2,1,0:T(8,128)(2,1)S(1)} %all-to-all-done.pieces_ref, f32[8,128]{1,0:T(8,128)S(1)} %get-tuple-element.40._), custom_call_target="tpu_custom_call" | custom-call | flops 1000000 | bytes 2000000 | tf_op jit(solution)/shard_map/sum_part/pallas_call | solution.py:281
  58.2 5.9 %all-to-all-start.1 = ((bf16[64,40,128]{2,1,0:T(8,128)(2,1)}), bf16[64,40,128]{2,1,0:T(8,128)(2,1)S(1)}, u32[]{:S(2)}, u32[]{:S(2)}) async-start(bf16[64,40,128]{2,1,0:T(8,128)(2,1)} %sum_part.1._), calls=%async_computation.1 | async-start | bytes 1310720 | tf_op jit(solution)/shard_map/all_to_all | solution.py:475
  64.1 8.5 %grad_input_part.1 = (bf16[4,512,256]{2,1,0:T(8,128)(2,1)}, f32[8,128]{1,0:T(8,128)S(1)}) custom-call(bf16[4,16,128]{2,1,0:T(8,128)(2,1)S(1)} %get-tuple-element.23.kept_ref, bf16[4,528,256]{2,1,0:T(8,128)(2,1)S(1)} %collective-permute-done.chip_ref, bf16[4,528,256]{2,1,0:T(8,128)(2,1)S(1)} %collective-permute-done.1.link_ref, ...), custom_call_target="tpu_custom_call" | custom-call | flops 8000000000 | bytes 5000000 | tf_op jit(solution)/shard_map/grad_input_part/pallas_call | solution.py:421
  72.6 2.6 %all-to-all-done.1 = bf16[64,40,128]{2,1,0:T(8,128)(2,1)S(1)} async-done(((bf16[64,40,128]{2,1,0:T(8,128)(2,1)}), bf16[64,40,128]{2,1,0:T(8,128)(2,1)S(1)}, u32[]{:S(2)}, u32[]{:S(2)}) %all-to-all-start.1) | async-done | bytes 655392 | tf_op jit(solution)/shard_map/all_to_all | solution.py:475
  75.2 4.1 %collective-permute-start.7 = (bf16[20,128,128]{2,1,0:T(8,128)(2,1)S(1)}, bf16[20,128,128]{2,1,0:T(8,128)(2,1)S(1)}, u32[]{:S(2)}, u32[]{:S(2)}) collective-permute-start(bf16[20,128,128]{2,1,0:T(8,128)(2,1)S(1)} %ordered.1.own_ref), channel_id=1, source_target_pairs={{0,8},{8,0},{1,9},{9,1},{2,10},{10,2},{3,11},{11,3},{4,12},{12,4},... | collective-permute-start | bytes 1966088 | tf_op jit(solution)/shard_map/ppermute | solution.py:484
  79.3 1.7 %collective-permute-done.7.other_ref = bf16[20,128,128]{2,1,0:T(8,128)(2,1)S(1)} collective-permute-done((bf16[20,128,128]{2,1,0:T(8,128)(2,1)S(1)}, bf16[20,128,128]{2,1,0:T(8,128)(2,1)S(1)}, u32[]{:S(2)}, u32[]{:S(2)}) %collective-permute-start.7) | collective-permute-done | bytes 655392 | tf_op jit(solution)/shard_map/ppermute | solution.py:484
  81.0 1.9 %result_part.1 = f32[9,256,256]{2,1,0:T(8,128)} custom-call(bf16[20,128,128]{2,1,0:T(8,128)(2,1)S(1)} %ordered.1.own_ref, bf16[20,128,128]{2,1,0:T(8,128)(2,1)S(1)} %collective-permute-done.7.other_ref), custom_call_target="tpu_custom_call" | custom-call | flops 1000000 | bytes 4000000 | tf_op jit(solution)/shard_map/result_part/pallas_call | solution.py:321
  (11 shorter events, 0.0 us)
Async XLA Ops:
  0.6 7.5 %copy-start = (bf16[4,512,256]{2,1,0:T(8,128)(2,1)S(1)}, bf16[4,512,256]{2,1,0:T(8,128)(2,1)}, u32[]{:S(2)}) copy-start(bf16[4,512,256]{2,1,0:T(8,128)(2,1)} %feat_hbm.1) | copy-start | bytes 3145732
  0.6 7.5 %copy-start.1 = (bf16[4,512,256]{2,1,0:T(8,128)(2,1)S(1)}, bf16[4,512,256]{2,1,0:T(8,128)(2,1)}, u32[]{:S(2)}) copy-start(bf16[4,512,256]{2,1,0:T(8,128)(2,1)} %cot_hbm.1) | copy-start | bytes 3145732
  0.7 0.9 %copy-start.2 = (f32[4,9,25]{2,0,1:T(4,128)S(1)}, f32[4,9,25]{2,0,1:T(4,128)}, u32[]{:S(2)}) copy-start(f32[4,9,25]{2,0,1:T(4,128)} %param.7) | copy-start | bytes 10804
  3.1 20.8 %collective-permute-start = (bf16[4,528,256]{2,1,0:T(8,128)(2,1)S(1)}, bf16[4,528,256]{2,1,0:T(8,128)(2,1)S(1)}, u32[]{:S(2)}, u32[]{:S(2)}) collective-permute-start(bf16[4,528,256]{2,1,0:T(8,128)(2,1)S(1)} %get-tuple-element.24), channel_id=1, source_target_pairs={{0,8},{8,0},{1,9},{9,1},{2,10},{10,2},{3,11},{11,3},{4,12},{12,4},... | collective-permute-start | bytes 3244040 | tf_op jit(solution)/shard_map/ppermute | solution.py:456
  4.6 19.3 %collective-permute-start.1 = (bf16[4,528,256]{2,1,0:T(8,128)(2,1)S(1)}, bf16[4,528,256]{2,1,0:T(8,128)(2,1)S(1)}, u32[]{:S(2)}, u32[]{:S(2)}) collective-permute-start(bf16[4,528,256]{2,1,0:T(8,128)(2,1)S(1)} %get-tuple-element.25), channel_id=1, source_target_pairs={{8,16},{24,32},{40,48},{56,64},{72,80},{88,96},{104,112},{16,8},{3... | collective-permute-start | bytes 3244040 | tf_op jit(solution)/shard_map/ppermute | solution.py:455
  17.4 6.5 %collective-permute-start.2 = (bf16[4,16,256]{2,1,0:T(8,128)(2,1)S(1)}, bf16[4,16,256]{2,1,0:T(8,128)(2,1)S(1)}, u32[]{:S(2)}, u32[]{:S(2)}) collective-permute-start(bf16[4,16,256]{2,1,0:T(8,128)(2,1)S(1)} %get-tuple-element.27), channel_id=1, source_target_pairs={{0,1},{1,2},{2,3},{3,4},{4,5},{5,6},{6,7},{7,0},{8,9},{9,10},{10,1... | collective-permute-start | bytes 98312 | tf_op jit(solution)/shard_map/ppermute | solution.py:444
  18.7 5.2 %collective-permute-start.3 = (bf16[4,16,256]{2,1,0:T(8,128)(2,1)S(1)}, bf16[4,16,256]{2,1,0:T(8,128)(2,1)S(1)}, u32[]{:S(2)}, u32[]{:S(2)}) collective-permute-start(bf16[4,16,256]{2,1,0:T(8,128)(2,1)S(1)} %get-tuple-element.28), channel_id=1, source_target_pairs={{0,7},{1,0},{2,1},{3,2},{4,3},{5,4},{6,5},{7,6},{8,15},{9,8},{10,9... | collective-permute-start | bytes 98312 | tf_op jit(solution)/shard_map/ppermute | solution.py:444
  27.7 2.2 %collective-permute-start.4 = (bf16[20,128,128]{2,1,0:T(8,128)(2,1)S(1)}, bf16[20,128,128]{2,1,0:T(8,128)(2,1)S(1)}, u32[]{:S(2)}, u32[]{:S(2)}) collective-permute-start(bf16[20,128,128]{2,1,0:T(8,128)(2,1)S(1)} %get-tuple-element.33), channel_id=1, source_target_pairs={{0,8},{8,0},{1,9},{9,1},{2,10},{10,2},{3,11},{11,3},{4,12},{12,4},... | collective-permute-start | bytes 1966088 | tf_op jit(solution)/shard_map/ppermute | solution.py:465
  30.9 13.9 %collective-permute-start.5 = (bf16[12,16,256]{2,1,0:T(8,128)(2,1)S(1)}, bf16[12,16,256]{2,1,0:T(8,128)(2,1)S(1)}, u32[]{:S(2)}, u32[]{:S(2)}) collective-permute-start(bf16[12,16,256]{2,1,0:T(8,128)(2,1)S(1)} %get-tuple-element.36), channel_id=1, source_target_pairs={{0,1},{1,2},{2,3},{3,4},{4,5},{5,6},{6,7},{7,0},{8,9},{9,10},{10,1... | collective-permute-start | bytes 294920 | tf_op jit(solution)/shard_map/ppermute | solution.py:444
  30.9 13.9 %collective-permute-start.6 = (bf16[12,16,256]{2,1,0:T(8,128)(2,1)S(1)}, bf16[12,16,256]{2,1,0:T(8,128)(2,1)S(1)}, u32[]{:S(2)}, u32[]{:S(2)}) collective-permute-start(bf16[12,16,256]{2,1,0:T(8,128)(2,1)S(1)} %get-tuple-element.37), channel_id=1, source_target_pairs={{0,7},{1,0},{2,1},{3,2},{4,3},{5,4},{6,5},{7,6},{8,15},{9,8},{10,9... | collective-permute-start | bytes 294920 | tf_op jit(solution)/shard_map/ppermute | solution.py:444
  36.0 21.2 %all-to-all-start = ((bf16[64,40,128]{2,1,0:T(8,128)(2,1)}), bf16[64,40,128]{2,1,0:T(8,128)(2,1)S(1)}, u32[]{:S(2)}, u32[]{:S(2)}) async-start(bf16[64,40,128]{2,1,0:T(8,128)(2,1)} %bitcast.2), calls=%async_computation | async-start | bytes 1310720 | tf_op jit(solution)/shard_map/all_to_all | solution.py:466
  58.2 17.0 %all-to-all-start.1 = ((bf16[64,40,128]{2,1,0:T(8,128)(2,1)}), bf16[64,40,128]{2,1,0:T(8,128)(2,1)S(1)}, u32[]{:S(2)}, u32[]{:S(2)}) async-start(bf16[64,40,128]{2,1,0:T(8,128)(2,1)} %sum_part.1._), calls=%async_computation.1 | async-start | bytes 1310720 | tf_op jit(solution)/shard_map/all_to_all | solution.py:475
  75.2 5.8 %collective-permute-start.7 = (bf16[20,128,128]{2,1,0:T(8,128)(2,1)S(1)}, bf16[20,128,128]{2,1,0:T(8,128)(2,1)S(1)}, u32[]{:S(2)}, u32[]{:S(2)}) collective-permute-start(bf16[20,128,128]{2,1,0:T(8,128)(2,1)S(1)} %ordered.1.own_ref), channel_id=1, source_target_pairs={{0,8},{8,0},{1,9},{9,1},{2,10},{10,2},{3,11},{11,3},{4,12},{12,4},... | collective-permute-start | bytes 1966088 | tf_op jit(solution)/shard_map/ppermute | solution.py:484

commit v3 on v2

v3 whole, which is shorter than its diff:
```python
import functools
import math

import jax
import jax.numpy as jnp
from jax import lax
from jax.experimental import pallas as pl
from jax.experimental.pallas import tpu as pltpu
from jax.sharding import Mesh
from jax.sharding import PartitionSpec as P

K = 9
RAD = 2
WIDTH = 2 * RAD + 1
TAPS = WIDTH * WIDTH
ROWS = 4
PLACES = ROWS + 2 * RAD
NJ = 512
C = 256
J = 32
STEPS = NJ // J
EDGE = 16
EXT_WINDOW = 48
EXT = NJ + 16
DEPTH = WIDTH * EXT_WINDOW
WIDE = NJ + 2 * EDGE + 16
LANES = 128
BLOCKS = 2 * K
PADDED_BLOCKS = 20
MIB = 1024 * 1024
BF = jnp.bfloat16
F32 = jnp.float32

IN_VMEM = pl.BlockSpec(memory_space=pltpu.VMEM)
IN_SMEM = pl.BlockSpec(memory_space=pltpu.SMEM)
IN_HBM = pl.BlockSpec(memory_space=pltpu.HBM)
ANYWHERE = pl.BlockSpec(memory_space=pl.ANY)


def in_hbm(array):
    return pltpu.with_memory_space_constraint(array, pltpu.HBM)


def params(mib):
    return pltpu.CompilerParams(vmem_limit_bytes=mib * MIB)


def cost(flops, moved):
    return pl.CostEstimate(flops=int(flops), bytes_accessed=int(moved), transcendentals=0)


def banded(line):
    return pltpu.roll(jnp.broadcast_to(line, (J, 256)), 0, axis=1, stride=1, stride_axis=0).astype(BF)


def one_hot(lane_of_tap):
    tap = lax.broadcasted_iota(jnp.int32, (LANES, 256), 0)
    lane = lax.broadcasted_iota(jnp.int32, (LANES, 256), 1)
    return jnp.where((lane == lane_of_tap(tap)) & (tap < TAPS), 1.0, 0.0).astype(BF)


def send_kernel(lo_ref, hi_ref, basis_ref, feat_ref, cot_ref, chip_ref, link_ref, right_ref, left_ref, kept_ref, lo, hi, basis, sems):
    core = lax.axis_index("core")
    to_chip, to_link = 2 - 2 * core, 2 * core
    copies = [
        (lo_ref, lo),
        (hi_ref, hi),
        (basis_ref, basis),
        (feat_ref.at[pl.ds(to_link, 2)], link_ref),
        (feat_ref.at[pl.ds(to_chip, 2)], chip_ref),
        (cot_ref.at[:, pl.ds(NJ - EDGE, EDGE)], right_ref),
        (cot_ref.at[:, pl.ds(0, EDGE)], left_ref),
    ]
    copies = [pltpu.make_async_copy(a, b, sems.at[n]) for n, (a, b) in enumerate(copies)]
    for copy in copies:
        copy.start()
    offset = lax.broadcasted_iota(jnp.int32, (16, LANES), 1) // WIDTH - RAD
    for copy in copies[:3]:
        copy.wait()
    for i in range(ROWS):
        cells = jnp.pad(basis[:, i, :], ((0, 16 - K), (0, LANES - TAPS)))
        cells = jnp.where((offset >= lo[i]) & (offset <= hi[i]), cells, jnp.zeros_like(cells))
        kept_ref[i] = cells.astype(BF)
    for copy in copies[3:]:
        copy.wait()


def send_part(span_lo, span_hi, basis, features, cotangent):
    basis = jnp.transpose(basis, (1, 0, 2))
    return pl.pallas_call(
        send_kernel,
        out_shape=(
            pltpu.VMEM((2, NJ, C), BF),
            pltpu.VMEM((2, NJ, C), BF),
            pltpu.VMEM((ROWS, EDGE, C), BF),
            pltpu.VMEM((ROWS, EDGE, C), BF),
            pltpu.VMEM((ROWS, 16, LANES), BF),
        ),
        in_specs=[IN_HBM] * 5,
        out_specs=[IN_VMEM] * 5,
        scratch_shapes=[
            pltpu.SMEM((ROWS,), jnp.int32),
            pltpu.SMEM((ROWS,), jnp.int32),
            pltpu.VMEM(basis.shape, F32),
            pltpu.SemaphoreType.DMA((7,)),
        ],
        compiler_params=params(4),
        cost_estimate=cost(0, 2e6),
        name="send_part",
    )(in_hbm(span_lo), in_hbm(span_hi), in_hbm(basis), in_hbm(features), in_hbm(cotangent))


def own_kernel(kept_ref, cot_ref, feat_ref, weight_hbm, turned_ref, extended_ref, bands_ref, weight_ref, sem):
    weight_copy = pltpu.make_async_copy(weight_hbm, weight_ref, sem)
    weight_copy.start()
    turned_ref[...] = cot_ref[...].reshape(ROWS * NJ, C).T
    gap = jnp.zeros((8, C), BF)
    for i in range(ROWS):
        extended_ref[i] = jnp.concatenate([gap, feat_ref[i], gap], axis=0)
    place = one_hot(lambda tap: tap // WIDTH * EXT_WINDOW + 8 - RAD + tap % WIDTH)
    for i in range(ROWS):
        line = jnp.dot(kept_ref[i], place, preferred_element_type=F32)
        for k in range(K):
            bands_ref[i, k * J : (k + 1) * J, :] = banded(line[k : k + 1, :])[:, :DEPTH]
    weight_copy.wait()


def own_part(kept, cotangent, features, weight):
    return pl.pallas_call(
        own_kernel,
        out_shape=(
            pltpu.VMEM((C, ROWS * NJ), BF),
            pltpu.VMEM((ROWS, EXT, C), BF),
            pltpu.VMEM((ROWS, K * J, DEPTH), BF),
            pltpu.VMEM((K * C, C), BF),
        ),
        in_specs=[IN_VMEM] * 3 + [IN_HBM],
        out_specs=[IN_VMEM] * 4,
        scratch_shapes=[pltpu.SemaphoreType.DMA(())],
        compiler_params=params(4),
        cost_estimate=cost(1e9, 4e6),
        name="own_part",
    )(kept, cotangent, features, in_hbm(weight))


def halo_kernel(chip_ref, link_ref, left_ref, right_ref, turned_ref, extended_ref, bands_ref, kept_ref, cot_ref, own_ref, other_ref, filtered, chip_cot_ref, link_cot_ref, halo, total, kept, sems):
    core = lax.axis_index("core")
    copies = []
    for n, (ref, first) in enumerate(((chip_cot_ref, 2 - 2 * core), (link_cot_ref, 2 * core))):
        kept[n] = jnp.zeros((2, 16, C), BF)
        for i in range(2):
            kept[n, i, :, 0:LANES] = kept_ref[first + i]
        pair = pl.ds(first, 2)
        for source, start, size in (
            (left_ref.at[pair], 0, EDGE),
            (cot_ref.at[pair], EDGE, NJ),
            (right_ref.at[pair], EDGE + NJ, EDGE),
            (kept.at[n], 2 * EDGE + NJ, 16),
        ):
            copies.append(
                pltpu.make_async_copy(source, ref.at[:, pl.ds(start, size)], sems.at[len(copies)])
            )
    for copy in copies:
        copy.start()
    gap = jnp.zeros((8, C), BF)

    def fill(low, high):
        for n in range(2):
            extend(halo, n, low[n], gap, gap)
            extend(halo, 2 + n, high[n], gap, gap)

    pl.when(core == 0)(lambda: fill(link_ref, chip_ref))
    pl.when(core == 1)(lambda: fill(chip_ref, link_ref))
    rows = [halo.at[0], halo.at[1]] + [extended_ref.at[i] for i in range(ROWS)] + [halo.at[2], halo.at[3]]
    middle = jnp.zeros((EXT_WINDOW - 16, C), BF)
    for row in range(ROWS):
        for tile in range(STEPS + 1):
            if tile < STEPS:
                start = tile * J
                first = row * NJ + start
                cells = [rows[row + r][start : start + EXT_WINDOW, :] for r in range(WIDTH)]
            else:
                first = ROWS * NJ + row * J
                cells = []
                for r in range(WIDTH):
                    cells += [rows[row + r][NJ : NJ + 8, :], middle, rows[row + r][8:16, :]]
            found = jnp.dot(
                bands_ref[row], jnp.concatenate(cells, axis=0), preferred_element_type=F32
            ).astype(BF)
            for k in range(K):
                filtered[first : first + J, k * C : (k + 1) * C] = found[k * J : (k + 1) * J]
    edges = [piece for i in range(ROWS) for piece in (right_ref[i], left_ref[i])]
    edges = jnp.concatenate(edges, axis=0).T
    for k in range(K):
        columns = slice(k * C, (k + 1) * C)
        total[:, columns] = jnp.dot(
            turned_ref[...], filtered[0 : ROWS * NJ, columns], preferred_element_type=F32
        ) + jnp.dot(edges, filtered[ROWS * NJ :, columns], preferred_element_type=F32)
    mine = pl.multiple_of(core * LANES, LANES)
    theirs = pl.multiple_of((1 - core) * LANES, LANES)
    for block in range(BLOCKS):
        columns = slice(block * LANES, (block + 1) * LANES)
        own_ref[block] = total[pl.ds(mine, LANES), columns]
        other_ref[block] = total[pl.ds(theirs, LANES), columns].astype(BF)
    for block in range(BLOCKS, PADDED_BLOCKS):
        own_ref[block] = jnp.zeros((LANES, LANES), F32)
        other_ref[block] = jnp.zeros((LANES, LANES), BF)
    for copy in copies:
        copy.wait()


def halo_part(chip, link, left, right, turned, extended, bands, kept, cotangent):
    shape = (PADDED_BLOCKS, LANES, LANES)
    return pl.pallas_call(
        halo_kernel,
        out_shape=(
            pltpu.VMEM(shape, F32),
            pltpu.VMEM(shape, BF),
            pltpu.VMEM((ROWS * (NJ + J), K * C), BF),
            pltpu.VMEM((2, WIDE, C), BF),
            pltpu.VMEM((2, WIDE, C), BF),
        ),
        in_specs=[IN_VMEM] * 8 + [IN_HBM],
        out_specs=[IN_VMEM] * 5,
        scratch_shapes=[
            pltpu.VMEM((ROWS, EXT, C), BF),
            pltpu.VMEM((C, K * C), F32),
            pltpu.VMEM((2, 2, 16, C), BF),
            pltpu.SemaphoreType.DMA((8,)),
        ],
        compiler_params=params(14),
        cost_estimate=cost(8e9, 4e6),
        name="halo_part",
    )(chip, link, left, right, turned, extended, bands, kept, in_hbm(cotangent))


def half_kernel(own_ref, other_ref, _, out_ref):
    out_ref[...] = (own_ref[...] + other_ref[...].astype(F32)).astype(BF)


def half_part(own, other, after):
    return pl.pallas_call(
        half_kernel,
        out_shape=pltpu.VMEM(own.shape, BF),
        in_specs=[IN_VMEM] * 2 + [ANYWHERE],
        out_specs=IN_VMEM,
        compiler_params=params(4),
        cost_estimate=cost(1e6, 3e6),
        name="half_part",
    )(own, other, after)


def mixed_kernel(filtered_ref, weight_ref, out_ref, ends_ref, to_right_ref, to_left_ref, mixed, sems):
    copies = [pltpu.make_async_copy(mixed.at[row], out_ref.at[row], sems.at[row]) for row in range(ROWS)]
    beyond = jnp.dot(filtered_ref[ROWS * NJ :, :], weight_ref[...], preferred_element_type=F32)
    for row in range(ROWS):
        to_right_ref[row] = beyond[row * J : row * J + EDGE]
        to_left_ref[row] = beyond[row * J + EDGE : (row + 1) * J]
        found = jnp.dot(
            filtered_ref[row * NJ : (row + 1) * NJ, :], weight_ref[...], preferred_element_type=F32
        )
        ends_ref[row, 0:EDGE, :] = found[0:EDGE]
        ends_ref[row, EDGE:, :] = found[NJ - EDGE :]
        mixed[row] = found.astype(BF)
        copies[row].start()
    for copy in copies:
        copy.wait()


def mixed_part(filtered, weight):
    return pl.pallas_call(
        mixed_kernel,
        out_shape=(
            jax.ShapeDtypeStruct((ROWS, NJ, C), BF),
            pltpu.VMEM((ROWS, 2 * EDGE, C), F32),
            pltpu.VMEM((ROWS, EDGE, C), F32),
            pltpu.VMEM((ROWS, EDGE, C), F32),
        ),
        in_specs=[IN_VMEM] * 2,
        out_specs=[IN_HBM] + [IN_VMEM] * 3,
        scratch_shapes=[pltpu.VMEM((ROWS, NJ, C), BF), pltpu.SemaphoreType.DMA((ROWS,))],
        compiler_params=params(6),
        cost_estimate=cost(1e9, 2e6),
        name="mixed_part",
    )(filtered, weight)


def ends_kernel(ends_ref, left_ref, right_ref, _, __, out_ref, done_ref, ends, sems):
    ends[0] = (ends_ref[:, 0:EDGE, :] + left_ref[...]).astype(BF)
    ends[1] = (ends_ref[:, EDGE:, :] + right_ref[...]).astype(BF)
    copies = [
        pltpu.make_async_copy(ends.at[n], out_ref.at[:, pl.ds(first, EDGE)], sems.at[n])
        for n, first in enumerate((0, NJ - EDGE))
    ]
    for copy in copies:
        copy.start()
    done_ref[...] = jnp.zeros_like(done_ref)
    for copy in copies:
        copy.wait()


def ends_part(ends, left, right, mixed, after):
    return pl.pallas_call(
        ends_kernel,
        out_shape=(jax.ShapeDtypeStruct(mixed.shape, BF), pltpu.VMEM((8, LANES), F32)),
        in_specs=[IN_VMEM] * 3 + [IN_HBM, ANYWHERE],
        out_specs=[IN_HBM, IN_VMEM],
        input_output_aliases={3: 0},
        scratch_shapes=[pltpu.VMEM((2, ROWS, EDGE, C), BF), pltpu.SemaphoreType.DMA((2,))],
        compiler_params=params(4),
        cost_estimate=cost(1e6, 1e6),
        name="ends_part",
    )(ends, left, right, mixed, after)


def sum_kernel(scale, pieces_ref, out_ref):
    piece = (jnp.sum(pieces_ref[...].astype(F32), axis=0) * scale).astype(BF)
    out_ref[...] = jnp.broadcast_to(piece, out_ref.shape)


def sum_part(pieces, scale):
    return pl.pallas_call(
        functools.partial(sum_kernel, scale),
        out_shape=pltpu.VMEM(pieces.shape, BF),
        in_specs=[IN_VMEM],
        out_specs=IN_VMEM,
        compiler_params=params(4),
        cost_estimate=cost(1e6, 2e6),
        name="sum_part",
    )(pieces)


def order_kernel(*_):
    pass


def ordered(value, after):
    return pl.pallas_call(
        order_kernel,
        out_shape=jax.ShapeDtypeStruct(value.shape, value.dtype),
        in_specs=[ANYWHERE, ANYWHERE],
        out_specs=ANYWHERE,
        input_output_aliases={0: 0},
        compiler_params=params(1),
        name="ordered",
    )(value, after)


def result_kernel(own_ref, other_ref, out_ref):
    core = lax.axis_index("core")
    for n in range(out_ref.shape[0]):
        for part in range(2):
            rows = slice(part * LANES, (part + 1) * LANES)
            mine = own_ref[2 * n + part].astype(F32).T
            theirs = other_ref[2 * n + part].astype(F32).T
            out_ref[n, rows, 0:LANES] = jnp.where(core == 0, mine, theirs)
            out_ref[n, rows, LANES:] = jnp.where(core == 0, theirs, mine)


def result_part(own, other):
    step = 3
    return pl.pallas_call(
        result_kernel,
        grid=(K // step,),
        out_shape=jax.ShapeDtypeStruct((K, C, C), F32),
        in_specs=[pl.BlockSpec((2 * step, LANES, LANES), lambda n: (n, 0, 0))] * 2,
        out_specs=pl.BlockSpec((step, C, C), lambda n: (n, 0, 0)),
        compiler_params=params(6),
        cost_estimate=cost(1e6, 4e6),
        name="result_part",
    )(own, other)


def extend(extended, n, row, left, right):
    extended[n] = jnp.concatenate([left, row, right], axis=0)


def grad_kernel(kept_ref, chip_ref, link_ref, left_ref, right_ref, weight_hbm, cot_hbm, _, out_ref, done_ref, weight, weight_turned, cot, extended, bands, cells, filtered, mixed, sems):
    core = lax.axis_index("core")
    cot_copy = pltpu.make_async_copy(cot_hbm, cot, sems.at[ROWS])
    cot_copy.start()
    weight_copy = pltpu.make_async_copy(weight_hbm, weight, sems.at[ROWS + 1])
    weight_copy.start()

    def fill(low, high):
        for n in range(2):
            extended[n] = low[n, 8 : 8 + EXT, :]
            extended[6 + n] = high[n, 8 : 8 + EXT, :]
            cells[n] = low[n, 2 * EDGE + NJ :, 0:LANES]
            cells[6 + n] = high[n, 2 * EDGE + NJ :, 0:LANES]

    pl.when(core == 0)(lambda: fill(link_ref, chip_ref))
    pl.when(core == 1)(lambda: fill(chip_ref, link_ref))
    for n in range(ROWS):
        cells[2 + n] = kept_ref[n]

    away = (TAPS - 1 - lax.broadcasted_iota(jnp.int32, (16, LANES), 1)) // WIDTH
    place = one_hot(lambda tap: (TAPS - 1 - tap) // WIDTH * EXT_WINDOW + 8 - RAD + (TAPS - 1 - tap) % WIDTH)
    lines = []
    for row in range(ROWS):
        taken = jnp.zeros((16, LANES), F32)
        for r in range(WIDTH):
            taken = jnp.where(away == r, cells[row + r].astype(F32), taken)
        lines.append(jnp.dot(taken.astype(BF), place, preferred_element_type=F32))
    cot_copy.wait()
    for n in range(ROWS):
        extend(extended, 2 + n, cot[n], left_ref[n, 8:, :], right_ref[n, :8, :])
    copies = [pltpu.make_async_copy(mixed.at[row], out_ref.at[row], sems.at[row]) for row in range(ROWS)]
    for row in range(ROWS):
        slot = row % 2
        for k in range(K):
            bands[slot, k * J : (k + 1) * J, :] = banded(lines[row][k : k + 1, :])[:, :DEPTH]
        for tile in range(STEPS):
            start = tile * J
            window = jnp.concatenate(
                [extended[row + r, start : start + EXT_WINDOW, :] for r in range(WIDTH)], axis=0
            )
            found = jnp.dot(bands[slot], window, preferred_element_type=F32).astype(BF)
            for k in range(K):
                filtered[slot, start : start + J, k * C : (k + 1) * C] = found[k * J : (k + 1) * J]
        if row == 0:
            weight_copy.wait()
            for k in range(K):
                columns = slice(k * C, (k + 1) * C)
                weight_turned[columns, :] = weight[columns, :].T
        mixed[row] = jnp.dot(filtered[slot], weight_turned[...], preferred_element_type=F32).astype(BF)
        copies[row].start()
    for copy in copies:
        copy.wait()
    done_ref[...] = jnp.zeros_like(done_ref)


def grad_part(kept, chip, link, left, right, weight, cotangent, after):
    return pl.pallas_call(
        grad_kernel,
        out_shape=(jax.ShapeDtypeStruct((ROWS, NJ, C), BF), pltpu.VMEM((8, LANES), F32)),
        in_specs=[IN_VMEM] * 5 + [IN_HBM, IN_HBM, ANYWHERE],
        out_specs=[IN_HBM, IN_VMEM],
        scratch_shapes=[
            pltpu.VMEM((K * C, C), BF),
            pltpu.VMEM((K * C, C), BF),
            pltpu.VMEM((ROWS, NJ, C), BF),
            pltpu.VMEM((PLACES, EXT, C), BF),
            pltpu.VMEM((2, K * J, DEPTH), BF),
            pltpu.VMEM((PLACES, 16, LANES), BF),
            pltpu.VMEM((2, NJ, K * C), BF),
            pltpu.VMEM((ROWS, NJ, C), BF),
            pltpu.SemaphoreType.DMA((ROWS + 2,)),
        ],
        compiler_params=params(20),
        cost_estimate=cost(8e9, 5e6),
        name="grad_input_part",
    )(kept, chip, link, left, right, in_hbm(weight), in_hbm(cotangent), after)


def shifted(block, axis, count, step, periodic):
    route = [(i, (i + step) % count) for i in range(count) if periodic or 0 <= i + step < count]
    return lax.ppermute(block, axis, route)


def per_device(features, basis, span_lo, span_hi, weight, cotangent):
    lat, chips = ("yz", "core"), ("yz", "lon")
    lats, lons = lax.axis_size("yz") * lax.axis_size("core"), lax.axis_size("lon")
    parts = lax.axis_size("yz") * lons
    swap = [(0, 1), (1, 0)]

    pairs = [(i, i + 1) for i in range(1, lats - 1, 2)]
    pairs = pairs + [(b, a) for a, b in pairs]
    chip, link, to_right, to_left, kept = send_part(span_lo, span_hi, basis, features, cotangent)
    link = lax.ppermute(link, lat, pairs)
    chip = lax.ppermute(chip, "core", swap)
    near_left = shifted(to_right, "lon", lons, 1, True)
    near_right = shifted(to_left, "lon", lons, -1, True)
    weight = weight.reshape(K * C, C)
    turned, extended, bands, weight_near = own_part(kept, cotangent, features, weight)
    own, other, filtered, chip_cot, link_cot = halo_part(
        chip, link, near_left, near_right, turned, extended, bands, kept, cotangent
    )

    other = lax.ppermute(other, "core", swap)
    mixed, ends, to_right, to_left = mixed_part(filtered, weight_near)
    half = half_part(own, other, ends)
    pieces = lax.all_to_all(half.reshape(parts, -1, LANES), chips, 0, 0)
    link_cot = lax.ppermute(ordered(link_cot, half), lat, pairs)
    chip_cot = lax.ppermute(ordered(chip_cot, half), "core", swap)
    left = shifted(ordered(to_right, half), "lon", lons, 1, True)
    right = shifted(ordered(to_left, half), "lon", lons, -1, True)
    scale = 1.0 / math.sqrt(ROWS * lats * NJ * lons)
    copies = sum_part(pieces, scale)
    gathered = lax.all_to_all(copies, chips, 0, 0).reshape(PADDED_BLOCKS, LANES, LANES)
    mixed, mixed_done = ends_part(ends, left, right, mixed, copies)
    grad_input, grad_done = grad_part(
        kept, chip_cot, link_cot, near_left, near_right, weight, cotangent, mixed_done
    )
    gathered = ordered(gathered, grad_done)
    grad_weight = result_part(gathered, lax.ppermute(gathered, "core", swap))
    return mixed, grad_input, grad_weight


def solution(mesh):
    lats, lons = mesh.devices.shape
    split = Mesh(mesh.devices.reshape(lats // 2, 2, lons), ("yz", "core", "lon"))
    lat = ("yz", "core")
    return jax.shard_map(
        per_device,
        mesh=split,
        in_specs=(P(lat, "lon", None), P(lat, None, None), P(lat), P(lat), P(), P(lat, "lon", None)),
        out_specs=(P(lat, "lon", None), P(lat, "lon", None), P()),
        check_vma=False,
    )
```

time: 83.3 us -> 78.2 us (0.939)
  Pallas kernels: 35.3 us -> 26.1 us
  starting transfers between devices: 34.3 us -> 43.3 us
  waiting for transfers between devices: 11.7 us -> 7.55 us
  local copies, waits for them, and re-layouts: 0.87 us -> 0.01 us
    pallas_call x5 -> x6, Pallas kernels: 28.7 us -> 16.4 us  [the longest x1 8.46 us: grad_part(): pl.pallas_call(grad_kernel, out_shape=(jax.ShapeDtypeStruct((ROWS, NJ, C)...]
    all_to_all x1, starting transfers between devices: 8.74 us -> 13.8 us  [per_device(): pieces = lax.all_to_all(half.reshape(parts, -1, LANES), chips, 0, 0)]
    ppermute x2 -> x4, starting transfers between devices: 3.61 us -> 7.57 us  [the longest x1 3.53 us: per_device(): link = lax.ppermute(link, lat, pairs)]
    pallas_call x1, Pallas kernels: 3.8 us -> 6.68 us  [halo_part(): pl.pallas_call(halo_kernel, out_shape=(pltpu.VMEM(shape, F32), pltpu.VMEM...]
    ppermute x2 -> x4, waiting for transfers between devices: 2.09 us -> 0.36 us  [the longest x1 0.36 us: per_device(): link = lax.ppermute(link, lat, pairs)]
    ppermute x4, waiting for transfers between devices: 1.23 us -> 0.01 us  [shifted(): return lax.ppermute(block, axis, route)]
    unnamed x6 -> x4, local copies, waits for them, and re-layouts: 0.87 us -> 0.01 us
  transfers between devices with their start and end apart: 10 -> 12, of which waited for: 5 -> 4; matrix products, arithmetic and copies ran while one was open for 0% -> 0% of each run, Pallas kernels for 32% -> 19%
where the time goes in v3:
time: 78.2 us; the launch traced here: 77.9 us
  starting transfers between devices  43.3 us (55%)
  Pallas kernels  26.1 us (33%)
  waiting for transfers between devices  7.55 us (10%)
  between operations  0.84 us (1%)
    all_to_all x1, starting transfers between devices, per_device(): pieces = lax.all_to_all(half.reshape(parts, -1, LANES), chips, 0, 0)  13.8 us
    ppermute x4, starting transfers between devices, shifted(): return lax.ppermute(block, axis, route)  10.4 us
    pallas_call x1, Pallas kernels, grad_part(): pl.pallas_call(grad_kernel, out_shape=(jax.ShapeDtypeStruct((ROWS, NJ, C)...  8.46 us
    pallas_call x1, Pallas kernels, halo_part(): pl.pallas_call(halo_kernel, out_shape=(pltpu.VMEM(shape, F32), pltpu.VMEM...  6.68 us
    all_to_all x1, starting transfers between devices, per_device(): lax.all_to_all(copies, chips, 0, 0).reshape(PADDED_BLOCKS, LANES, LANES)  6.03 us
    ppermute x1, starting transfers between devices, per_device(): grad_weight = result_part(gathered, lax.ppermute(gathered, 'core', swap))  4.06 us
    pallas_call x1, Pallas kernels, mixed_part(): pl.pallas_call(mixed_kernel, out_shape=(jax.ShapeDtypeStruct((ROWS, NJ, C...  3.57 us
    ppermute x1, starting transfers between devices, per_device(): link = lax.ppermute(link, lat, pairs)  3.53 us
  transfers between devices with their start and end apart: 12, of which 4 were waited for; matrix products, arithmetic and copies ran while one was open for 0% of the time, Pallas kernels for 19%

profile of v3, /device:TPU:1, one launch (start us, length us, event | category | flops | bytes accessed | tf_op | source)
XLA Modules:
  0.0 77.9 jit_solution(15029714295296346219)
XLA Ops:
  0.7 1.4 %send_part.1 = (bf16[2,512,256]{2,1,0:T(8,128)(2,1)S(1)}, bf16[2,512,256]{2,1,0:T(8,128)(2,1)S(1)}, bf16[4,16,256]{2,1,0:T(8,128)(2,1)S(1)}, bf16[4,16,256]{2,1,0:T(8,128)(2,1)S(1)}, bf16[4,16,128]{2,1,0:T(8,128)(2,1)S(1)}) custom-call(s32[4]{0:T(128)} %lo_ref.1, s32[4]{0:T(128)} %hi_ref.1, f32[9,4,25]{2,1,0:T(4,128)} %bitcast.5, ...), custom_call_target="tpu_custom_call" | custom-call | bytes 2000000 | tf_op jit(solution)/shard_map/send_part/pallas_call | solution.py:90
  2.1 1.5 %collective-permute-start = (bf16[2,512,256]{2,1,0:T(8,128)(2,1)S(1)}, bf16[2,512,256]{2,1,0:T(8,128)(2,1)S(1)}, u32[]{:S(2)}, u32[]{:S(2)}) collective-permute-start(bf16[2,512,256]{2,1,0:T(8,128)(2,1)S(1)} %get-tuple-element.25), channel_id=1, source_target_pairs={{0,8},{8,0},{1,9},{9,1},{2,10},{10,2},{3,11},{11,3},{4,12},{12,4},... | collective-permute-start | bytes 1572872 | tf_op jit(solution)/shard_map/ppermute | solution.py:471
  3.6 3.5 %collective-permute-start.1 = (bf16[2,512,256]{2,1,0:T(8,128)(2,1)S(1)}, bf16[2,512,256]{2,1,0:T(8,128)(2,1)S(1)}, u32[]{:S(2)}, u32[]{:S(2)}) collective-permute-start(bf16[2,512,256]{2,1,0:T(8,128)(2,1)S(1)} %get-tuple-element.26), channel_id=1, source_target_pairs={{8,16},{24,32},{40,48},{56,64},{72,80},{88,96},{104,112},{16,8},{3... | collective-permute-start | bytes 1572872 | tf_op jit(solution)/shard_map/ppermute | solution.py:470
  7.1 1.3 %collective-permute-start.2 = (bf16[4,16,256]{2,1,0:T(8,128)(2,1)S(1)}, bf16[4,16,256]{2,1,0:T(8,128)(2,1)S(1)}, u32[]{:S(2)}, u32[]{:S(2)}) collective-permute-start(bf16[4,16,256]{2,1,0:T(8,128)(2,1)S(1)} %get-tuple-element.27), channel_id=1, source_target_pairs={{0,1},{1,2},{2,3},{3,4},{4,5},{5,6},{6,7},{7,0},{8,9},{9,10},{10,1... | collective-permute-start | bytes 98312 | tf_op jit(solution)/shard_map/ppermute | solution.py:458
  8.4 4.0 %collective-permute-start.3 = (bf16[4,16,256]{2,1,0:T(8,128)(2,1)S(1)}, bf16[4,16,256]{2,1,0:T(8,128)(2,1)S(1)}, u32[]{:S(2)}, u32[]{:S(2)}) collective-permute-start(bf16[4,16,256]{2,1,0:T(8,128)(2,1)S(1)} %get-tuple-element.28), channel_id=1, source_target_pairs={{0,7},{1,0},{2,1},{3,2},{4,3},{5,4},{6,5},{7,6},{8,15},{9,8},{10,9... | collective-permute-start | bytes 98312 | tf_op jit(solution)/shard_map/ppermute | solution.py:458
  12.4 1.3 %own_part.1 = (bf16[256,2048]{1,0:T(8,128)(2,1)S(1)}, bf16[4,528,256]{2,1,0:T(8,128)(2,1)S(1)}, bf16[4,288,240]{2,1,0:T(8,128)(2,1)S(1)}, bf16[2304,256]{1,0:T(8,128)(2,1)S(1)}) custom-call(bf16[4,16,128]{2,1,0:T(8,128)(2,1)S(1)} %get-tuple-element.29.kept_ref, bf16[4,512,256]{2,1,0:T(8,128)(2,1)S(1)} %copy-done.1, bf16[4,512,256]{2,1,0:T(8,128)(2,1)S(1)} %copy-done, ...), custom_call_target="tpu_custom_call" | custom-call | flops 1000000000 | bytes 4000000 | tf_op jit(solution)/shard_map/own_part/pallas_call | solution.py:129
  13.7 0.4 collective-permute-done.1.link_ref
  14.1 6.7 %halo_part.1 = (f32[20,128,128]{2,1,0:T(8,128)S(1)}, bf16[20,128,128]{2,1,0:T(8,128)(2,1)S(1)}, bf16[2176,2304]{1,0:T(8,128)(2,1)S(1)}, bf16[2,560,256]{2,1,0:T(8,128)(2,1)S(1)}, bf16[2,560,256]{2,1,0:T(8,128)(2,1)S(1)}) custom-call(bf16[2,512,256]{2,1,0:T(8,128)(2,1)S(1)} %collective-permute-done.chip_ref, ...), custom_call_target="tpu_custom_call" | custom-call | flops 8000000000 | bytes 4000000 | tf_op jit(solution)/shard_map/halo_part/pallas_call | solution.py:214
  20.9 3.6 %mixed_part.1 = (bf16[4,512,256]{2,1,0:T(8,128)(2,1)}, f32[4,32,256]{2,1,0:T(8,128)S(1)}, f32[4,16,256]{2,1,0:T(8,128)S(1)}, f32[4,16,256]{2,1,0:T(8,128)S(1)}) custom-call(bf16[2176,2304]{1,0:T(8,128)(2,1)S(1)} %get-tuple-element.33.filtered_ref, bf16[2304,256]{1,0:T(8,128)(2,1)S(1)} %get-tuple-element.34.weight_ref), custom_call_target="tpu_custom_call" | custom-call | flops 1000000000 | bytes 2000000 | tf_op jit(solution)/shard_map/mixed_part/pallas_call | solution.py:271
  24.4 0.9 %half_part.1.__1_ = bf16[20,128,128]{2,1,0:T(8,128)(2,1)} custom-call(f32[20,128,128]{2,1,0:T(8,128)S(1)} %get-tuple-element.37.own_ref, bf16[20,128,128]{2,1,0:T(8,128)(2,1)S(1)} %collective-permute-done.4.other_ref, f32[4,32,256]{2,1,0:T(8,128)S(1)} %get-tuple-element.35._.ends_ref), custom_call_target="tpu_custom_call" | custom-call | flops 1000000 | bytes 3000000 | tf_op jit(solution)/shard_map/half_part/pallas_call | solution.py:242
  25.4 13.8 %all-to-all-start = ((bf16[64,40,128]{2,1,0:T(8,128)(2,1)}), bf16[64,40,128]{2,1,0:T(8,128)(2,1)S(1)}, u32[]{:S(2)}, u32[]{:S(2)}) async-start(bf16[64,40,128]{2,1,0:T(8,128)(2,1)} %bitcast.2), calls=%async_computation | async-start | bytes 1310720 | tf_op jit(solution)/shard_map/all_to_all | solution.py:483
  39.2 0.9 %collective-permute-start.7 = (bf16[2,560,256]{2,1,0:T(8,128)(2,1)S(1)}, bf16[2,560,256]{2,1,0:T(8,128)(2,1)S(1)}, u32[]{:S(2)}, u32[]{:S(2)}) collective-permute-start(bf16[2,560,256]{2,1,0:T(8,128)(2,1)S(1)} %ordered.7), channel_id=1, source_target_pairs={{0,8},{8,0},{1,9},{9,1},{2,10},{10,2},{3,11},{11,3},{4,12},{12,4},... | collective-permute-start | bytes 1720328 | tf_op jit(solution)/shard_map/ppermute | solution.py:485
  40.0 3.1 %collective-permute-start.8 = (bf16[2,560,256]{2,1,0:T(8,128)(2,1)S(1)}, bf16[2,560,256]{2,1,0:T(8,128)(2,1)S(1)}, u32[]{:S(2)}, u32[]{:S(2)}) collective-permute-start(bf16[2,560,256]{2,1,0:T(8,128)(2,1)S(1)} %ordered.8), channel_id=1, source_target_pairs={{8,16},{24,32},{40,48},{56,64},{72,80},{88,96},{104,112},{16,8},{3... | collective-permute-start | bytes 1720328 | tf_op jit(solution)/shard_map/ppermute | solution.py:484
  43.2 1.3 %collective-permute-start.5 = (f32[4,16,256]{2,1,0:T(8,128)S(1)}, f32[4,16,256]{2,1,0:T(8,128)S(1)}, u32[]{:S(2)}, u32[]{:S(2)}) collective-permute-start(f32[4,16,256]{2,1,0:T(8,128)S(1)} %ordered.5), channel_id=1, source_target_pairs={{0,1},{1,2},{2,3},{3,4},{4,5},{5,6},{6,7},{7,0},{8,9},{9,10},{10,1... | collective-permute-start | bytes 196616 | tf_op jit(solution)/shard_map/ppermute | solution.py:458
  44.4 3.9 %collective-permute-start.6 = (f32[4,16,256]{2,1,0:T(8,128)S(1)}, f32[4,16,256]{2,1,0:T(8,128)S(1)}, u32[]{:S(2)}, u32[]{:S(2)}) collective-permute-start(f32[4,16,256]{2,1,0:T(8,128)S(1)} %ordered.6), channel_id=1, source_target_pairs={{0,7},{1,0},{2,1},{3,2},{4,3},{5,4},{6,5},{7,6},{8,15},{9,8},{10,9... | collective-permute-start | bytes 196616 | tf_op jit(solution)/shard_map/ppermute | solution.py:458
  48.3 3.5 %all-to-all-done.pieces_ref = bf16[64,40,128]{2,1,0:T(8,128)(2,1)S(1)} async-done(((bf16[64,40,128]{2,1,0:T(8,128)(2,1)}), bf16[64,40,128]{2,1,0:T(8,128)(2,1)S(1)}, u32[]{:S(2)}, u32[]{:S(2)}) %all-to-all-start) | async-done | bytes 655392 | tf_op jit(solution)/shard_map/all_to_all | solution.py:483
  51.8 1.0 %sum_part.1.__ = bf16[64,40,128]{2,1,0:T(8,128)(2,1)} custom-call(bf16[64,40,128]{2,1,0:T(8,128)(2,1)S(1)} %all-to-all-done.pieces_ref), custom_call_target="tpu_custom_call" | custom-call | flops 1000000 | bytes 2000000 | tf_op jit(solution)/shard_map/sum_part/pallas_call | solution.py:322
  52.8 6.0 %all-to-all-start.1 = ((bf16[64,40,128]{2,1,0:T(8,128)(2,1)}), bf16[64,40,128]{2,1,0:T(8,128)(2,1)S(1)}, u32[]{:S(2)}, u32[]{:S(2)}) async-start(bf16[64,40,128]{2,1,0:T(8,128)(2,1)} %sum_part.1.__), calls=%async_computation.1 | async-start | bytes 1310720 | tf_op jit(solution)/shard_map/all_to_all | solution.py:490
  58.8 0.7 ends_part.1
  59.5 8.5 %grad_input_part.1 = (bf16[4,512,256]{2,1,0:T(8,128)(2,1)}, f32[8,128]{1,0:T(8,128)S(1)}) custom-call(bf16[4,16,128]{2,1,0:T(8,128)(2,1)S(1)} %get-tuple-element.29.kept_ref, bf16[2,560,256]{2,1,0:T(8,128)(2,1)S(1)} %collective-permute-done.7.chip_ref, bf16[2,560,256]{2,1,0:T(8,128)(2,1)S(1)} %collective-permute-done.8.link_ref, ...), custom_call_target="tpu_custom_call" | custom-call | flops 8000000000 | bytes 5000000 | tf_op jit(solution)/shard_map/grad_input_part/pallas_call | solution.py:434
  68.0 2.0 %all-to-all-done.1 = bf16[64,40,128]{2,1,0:T(8,128)(2,1)S(1)} async-done(((bf16[64,40,128]{2,1,0:T(8,128)(2,1)}), bf16[64,40,128]{2,1,0:T(8,128)(2,1)S(1)}, u32[]{:S(2)}, u32[]{:S(2)}) %all-to-all-start.1) | async-done | bytes 655392 | tf_op jit(solution)/shard_map/all_to_all | solution.py:490
  70.0 4.1 %collective-permute-start.9 = (bf16[20,128,128]{2,1,0:T(8,128)(2,1)S(1)}, bf16[20,128,128]{2,1,0:T(8,128)(2,1)S(1)}, u32[]{:S(2)}, u32[]{:S(2)}) collective-permute-start(bf16[20,128,128]{2,1,0:T(8,128)(2,1)S(1)} %ordered.9.own_ref), channel_id=1, source_target_pairs={{0,8},{8,0},{1,9},{9,1},{2,10},{10,2},{3,11},{11,3},{4,12},{12,4},... | collective-permute-start | bytes 1966088 | tf_op jit(solution)/shard_map/ppermute | solution.py:496
  74.0 1.7 %collective-permute-done.9.other_ref = bf16[20,128,128]{2,1,0:T(8,128)(2,1)S(1)} collective-permute-done((bf16[20,128,128]{2,1,0:T(8,128)(2,1)S(1)}, bf16[20,128,128]{2,1,0:T(8,128)(2,1)S(1)}, u32[]{:S(2)}, u32[]{:S(2)}) %collective-permute-start.9) | collective-permute-done | bytes 655392 | tf_op jit(solution)/shard_map/ppermute | solution.py:496
  75.7 2.1 %result_part.1 = f32[9,256,256]{2,1,0:T(8,128)} custom-call(bf16[20,128,128]{2,1,0:T(8,128)(2,1)S(1)} %ordered.9.own_ref, bf16[20,128,128]{2,1,0:T(8,128)(2,1)S(1)} %collective-permute-done.9.other_ref), custom_call_target="tpu_custom_call" | custom-call | flops 1000000 | bytes 4000000 | tf_op jit(solution)/shard_map/result_part/pallas_call | solution.py:362
  (18 shorter events, 0.1 us)
Async XLA Ops:
  0.6 11.8 %copy-start.1 = (bf16[4,512,256]{2,1,0:T(8,128)(2,1)S(1)}, bf16[4,512,256]{2,1,0:T(8,128)(2,1)}, u32[]{:S(2)}) copy-start(bf16[4,512,256]{2,1,0:T(8,128)(2,1)} %cot_hbm.1) | copy-start | bytes 3145732
  0.6 11.8 %copy-start = (bf16[4,512,256]{2,1,0:T(8,128)(2,1)S(1)}, bf16[4,512,256]{2,1,0:T(8,128)(2,1)}, u32[]{:S(2)}) copy-start(bf16[4,512,256]{2,1,0:T(8,128)(2,1)} %feat_ref.3) | copy-start | bytes 3145732
  2.1 11.6 %collective-permute-start = (bf16[2,512,256]{2,1,0:T(8,128)(2,1)S(1)}, bf16[2,512,256]{2,1,0:T(8,128)(2,1)S(1)}, u32[]{:S(2)}, u32[]{:S(2)}) collective-permute-start(bf16[2,512,256]{2,1,0:T(8,128)(2,1)S(1)} %get-tuple-element.25), channel_id=1, source_target_pairs={{0,8},{8,0},{1,9},{9,1},{2,10},{10,2},{3,11},{11,3},{4,12},{12,4},... | collective-permute-start | bytes 1572872 | tf_op jit(solution)/shard_map/ppermute | solution.py:471
  3.6 10.5 %collective-permute-start.1 = (bf16[2,512,256]{2,1,0:T(8,128)(2,1)S(1)}, bf16[2,512,256]{2,1,0:T(8,128)(2,1)S(1)}, u32[]{:S(2)}, u32[]{:S(2)}) collective-permute-start(bf16[2,512,256]{2,1,0:T(8,128)(2,1)S(1)} %get-tuple-element.26), channel_id=1, source_target_pairs={{8,16},{24,32},{40,48},{56,64},{72,80},{88,96},{104,112},{16,8},{3... | collective-permute-start | bytes 1572872 | tf_op jit(solution)/shard_map/ppermute | solution.py:470
  7.1 6.6 %collective-permute-start.2 = (bf16[4,16,256]{2,1,0:T(8,128)(2,1)S(1)}, bf16[4,16,256]{2,1,0:T(8,128)(2,1)S(1)}, u32[]{:S(2)}, u32[]{:S(2)}) collective-permute-start(bf16[4,16,256]{2,1,0:T(8,128)(2,1)S(1)} %get-tuple-element.27), channel_id=1, source_target_pairs={{0,1},{1,2},{2,3},{3,4},{4,5},{5,6},{6,7},{7,0},{8,9},{9,10},{10,1... | collective-permute-start | bytes 98312 | tf_op jit(solution)/shard_map/ppermute | solution.py:458
  8.4 5.3 %collective-permute-start.3 = (bf16[4,16,256]{2,1,0:T(8,128)(2,1)S(1)}, bf16[4,16,256]{2,1,0:T(8,128)(2,1)S(1)}, u32[]{:S(2)}, u32[]{:S(2)}) collective-permute-start(bf16[4,16,256]{2,1,0:T(8,128)(2,1)S(1)} %get-tuple-element.28), channel_id=1, source_target_pairs={{0,7},{1,0},{2,1},{3,2},{4,3},{5,4},{6,5},{7,6},{8,15},{9,8},{10,9... | collective-permute-start | bytes 98312 | tf_op jit(solution)/shard_map/ppermute | solution.py:458
  20.8 3.7 %collective-permute-start.4 = (bf16[20,128,128]{2,1,0:T(8,128)(2,1)S(1)}, bf16[20,128,128]{2,1,0:T(8,128)(2,1)S(1)}, u32[]{:S(2)}, u32[]{:S(2)}) collective-permute-start(bf16[20,128,128]{2,1,0:T(8,128)(2,1)S(1)} %get-tuple-element.38), channel_id=1, source_target_pairs={{0,8},{8,0},{1,9},{9,1},{2,10},{10,2},{3,11},{11,3},{4,12},{12,4},... | collective-permute-start | bytes 1966088 | tf_op jit(solution)/shard_map/ppermute | solution.py:480
  25.4 26.4 %all-to-all-start = ((bf16[64,40,128]{2,1,0:T(8,128)(2,1)}), bf16[64,40,128]{2,1,0:T(8,128)(2,1)S(1)}, u32[]{:S(2)}, u32[]{:S(2)}) async-start(bf16[64,40,128]{2,1,0:T(8,128)(2,1)} %bitcast.2), calls=%async_computation | async-start | bytes 1310720 | tf_op jit(solution)/shard_map/all_to_all | solution.py:483
  39.2 20.3 %collective-permute-start.7 = (bf16[2,560,256]{2,1,0:T(8,128)(2,1)S(1)}, bf16[2,560,256]{2,1,0:T(8,128)(2,1)S(1)}, u32[]{:S(2)}, u32[]{:S(2)}) collective-permute-start(bf16[2,560,256]{2,1,0:T(8,128)(2,1)S(1)} %ordered.7), channel_id=1, source_target_pairs={{0,8},{8,0},{1,9},{9,1},{2,10},{10,2},{3,11},{11,3},{4,12},{12,4},... | collective-permute-start | bytes 1720328 | tf_op jit(solution)/shard_map/ppermute | solution.py:485
  40.0 19.5 %collective-permute-start.8 = (bf16[2,560,256]{2,1,0:T(8,128)(2,1)S(1)}, bf16[2,560,256]{2,1,0:T(8,128)(2,1)S(1)}, u32[]{:S(2)}, u32[]{:S(2)}) collective-permute-start(bf16[2,560,256]{2,1,0:T(8,128)(2,1)S(1)} %ordered.8), channel_id=1, source_target_pairs={{8,16},{24,32},{40,48},{56,64},{72,80},{88,96},{104,112},{16,8},{3... | collective-permute-start | bytes 1720328 | tf_op jit(solution)/shard_map/ppermute | solution.py:484
  43.2 15.7 %collective-permute-start.5 = (f32[4,16,256]{2,1,0:T(8,128)S(1)}, f32[4,16,256]{2,1,0:T(8,128)S(1)}, u32[]{:S(2)}, u32[]{:S(2)}) collective-permute-start(f32[4,16,256]{2,1,0:T(8,128)S(1)} %ordered.5), channel_id=1, source_target_pairs={{0,1},{1,2},{2,3},{3,4},{4,5},{5,6},{6,7},{7,0},{8,9},{9,10},{10,1... | collective-permute-start | bytes 196616 | tf_op jit(solution)/shard_map/ppermute | solution.py:458
  44.4 14.4 %collective-permute-start.6 = (f32[4,16,256]{2,1,0:T(8,128)S(1)}, f32[4,16,256]{2,1,0:T(8,128)S(1)}, u32[]{:S(2)}, u32[]{:S(2)}) collective-permute-start(f32[4,16,256]{2,1,0:T(8,128)S(1)} %ordered.6), channel_id=1, source_target_pairs={{0,7},{1,0},{2,1},{3,2},{4,3},{5,4},{6,5},{7,6},{8,15},{9,8},{10,9... | collective-permute-start | bytes 196616 | tf_op jit(solution)/shard_map/ppermute | solution.py:458
  52.8 17.2 %all-to-all-start.1 = ((bf16[64,40,128]{2,1,0:T(8,128)(2,1)}), bf16[64,40,128]{2,1,0:T(8,128)(2,1)S(1)}, u32[]{:S(2)}, u32[]{:S(2)}) async-start(bf16[64,40,128]{2,1,0:T(8,128)(2,1)} %sum_part.1.__), calls=%async_computation.1 | async-start | bytes 1310720 | tf_op jit(solution)/shard_map/all_to_all | solution.py:490
  70.0 5.8 %collective-permute-start.9 = (bf16[20,128,128]{2,1,0:T(8,128)(2,1)S(1)}, bf16[20,128,128]{2,1,0:T(8,128)(2,1)S(1)}, u32[]{:S(2)}, u32[]{:S(2)}) collective-permute-start(bf16[20,128,128]{2,1,0:T(8,128)(2,1)S(1)} %ordered.9.own_ref), channel_id=1, source_target_pairs={{0,8},{8,0},{1,9},{9,1},{2,10},{10,2},{3,11},{11,3},{4,12},{12,4},... | collective-permute-start | bytes 1966088 | tf_op jit(solution)/shard_map/ppermute | solution.py:496

commit v4 on v3

v4 whole, which is shorter than its diff:
```python
import functools
import math

import jax
import jax.numpy as jnp
from jax import lax
from jax.experimental import pallas as pl
from jax.experimental.pallas import tpu as pltpu
from jax.sharding import Mesh
from jax.sharding import PartitionSpec as P

K = 9
RAD = 2
WIDTH = 2 * RAD + 1
TAPS = WIDTH * WIDTH
ROWS = 4
PLACES = ROWS + 2 * RAD
NJ = 512
C = 256
J = 32
STEPS = NJ // J
EDGE = 16
EXT_WINDOW = 48
EXT = NJ + 16
DEPTH = WIDTH * EXT_WINDOW
WIDE = NJ + 2 * EDGE + 16
LANES = 128
BLOCKS = 2 * K
PADDED_BLOCKS = 20
MIB = 1024 * 1024
BF = jnp.bfloat16
F32 = jnp.float32

IN_VMEM = pl.BlockSpec(memory_space=pltpu.VMEM)
IN_SMEM = pl.BlockSpec(memory_space=pltpu.SMEM)
IN_HBM = pl.BlockSpec(memory_space=pltpu.HBM)
ANYWHERE = pl.BlockSpec(memory_space=pl.ANY)


def in_hbm(array):
    return pltpu.with_memory_space_constraint(array, pltpu.HBM)


def params(mib):
    return pltpu.CompilerParams(vmem_limit_bytes=mib * MIB)


def cost(flops, moved):
    return pl.CostEstimate(flops=int(flops), bytes_accessed=int(moved), transcendentals=0)


def banded(line):
    return pltpu.roll(jnp.broadcast_to(line, (J, 256)), 0, axis=1, stride=1, stride_axis=0).astype(BF)


def one_hot(lane_of_tap):
    tap = lax.broadcasted_iota(jnp.int32, (LANES, 256), 0)
    lane = lax.broadcasted_iota(jnp.int32, (LANES, 256), 1)
    return jnp.where((lane == lane_of_tap(tap)) & (tap < TAPS), 1.0, 0.0).astype(BF)


def send_kernel(feat_ref, chip_ref, link_ref, sems):
    core = lax.axis_index("core")
    copies = [
        pltpu.make_async_copy(feat_ref.at[pl.ds(first, 2)], ref, sems.at[n])
        for n, (ref, first) in enumerate(((link_ref, 2 * core), (chip_ref, 2 - 2 * core)))
    ]
    for copy in copies:
        copy.start()
    for copy in copies:
        copy.wait()


def send_part(features):
    return pl.pallas_call(
        send_kernel,
        out_shape=(pltpu.VMEM((2, NJ, C), BF), pltpu.VMEM((2, NJ, C), BF)),
        in_specs=[IN_HBM],
        out_specs=[IN_VMEM] * 2,
        scratch_shapes=[pltpu.SemaphoreType.DMA((2,))],
        compiler_params=params(2),
        cost_estimate=cost(0, 1e6),
        name="send_part",
    )(in_hbm(features))


def own_kernel(lo_ref, hi_ref, basis_ref, cot_ref, feat_ref, _, to_right_ref, to_left_ref, kept_ref, turned_ref, extended_ref, bands_ref, lo, hi, basis, cot, feat, sems):
    copies = (
        (lo_ref, lo),
        (hi_ref, hi),
        (basis_ref, basis),
        (cot_ref, cot),
        (feat_ref, feat),
    )
    copies = [pltpu.make_async_copy(a, b, sems.at[n]) for n, (a, b) in enumerate(copies)]
    for copy in copies:
        copy.start()
    place = one_hot(lambda tap: tap // WIDTH * EXT_WINDOW + 8 - RAD + tap % WIDTH)
    offset = lax.broadcasted_iota(jnp.int32, (16, LANES), 1) // WIDTH - RAD
    for copy in copies[:3]:
        copy.wait()
    for i in range(ROWS):
        cells = jnp.pad(basis[:, i, :], ((0, 16 - K), (0, LANES - TAPS)))
        cells = jnp.where((offset >= lo[i]) & (offset <= hi[i]), cells, jnp.zeros_like(cells)).astype(BF)
        kept_ref[i] = cells
        line = jnp.dot(cells, place, preferred_element_type=F32)
        for k in range(K):
            bands_ref[i, k * J : (k + 1) * J, :] = banded(line[k : k + 1, :])[:, :DEPTH]
    copies[3].wait()
    to_right_ref[...] = cot[:, NJ - EDGE :, :]
    to_left_ref[...] = cot[:, :EDGE, :]
    for pair in range(2):
        turned_ref[pair] = cot[2 * pair : 2 * pair + 2].reshape(2 * NJ, C).T
    copies[4].wait()
    gap = jnp.zeros((8, C), BF)
    for i in range(ROWS):
        extended_ref[i] = jnp.concatenate([gap, feat[i], gap], axis=0)


def own_part(span_lo, span_hi, basis, cotangent, features, after):
    basis = jnp.transpose(basis, (1, 0, 2))
    return pl.pallas_call(
        own_kernel,
        out_shape=(
            pltpu.VMEM((ROWS, EDGE, C), BF),
            pltpu.VMEM((ROWS, EDGE, C), BF),
            pltpu.VMEM((ROWS, 16, LANES), BF),
            pltpu.VMEM((2, C, 2 * NJ), BF),
            pltpu.VMEM((ROWS, EXT, C), BF),
            pltpu.VMEM((ROWS, K * J, DEPTH), BF),
        ),
        in_specs=[IN_HBM] * 5 + [ANYWHERE],
        out_specs=[IN_VMEM] * 6,
        scratch_shapes=[
            pltpu.SMEM((ROWS,), jnp.int32),
            pltpu.SMEM((ROWS,), jnp.int32),
            pltpu.VMEM(basis.shape, F32),
            pltpu.VMEM((ROWS, NJ, C), BF),
            pltpu.VMEM((ROWS, NJ, C), BF),
            pltpu.SemaphoreType.DMA((5,)),
        ],
        compiler_params=params(6),
        cost_estimate=cost(4e9, 4e6),
        name="own_part",
    )(*map(in_hbm, (span_lo, span_hi, basis, cotangent, features)), after)


def row_pair(side):
    core = lax.axis_index("core")
    return core if side == 0 else 1 - core


def filter_kernel(side, halo_ref, extended_ref, bands_ref, *refs):
    copies = []
    if side == 0:
        turned_ref, weight_hbm, total_ref, filtered, weight_ref, rows, sem = refs
        copies.append(pltpu.make_async_copy(weight_hbm, weight_ref, sem))
    else:
        turned_ref, before_ref, kept_ref, cot_ref, total_ref, filtered, chip_cot_ref, link_cot_ref, rows, kept, sems = refs
        core = lax.axis_index("core")
        for n, (ref, first) in enumerate(((chip_cot_ref, 2 - 2 * core), (link_cot_ref, 2 * core))):
            kept[n] = jnp.zeros((2, 16, C), BF)
            for i in range(2):
                kept[n, i, :, 0:LANES] = kept_ref[first + i]
            for source, start, size in ((cot_ref.at[pl.ds(first, 2)], EDGE, NJ), (kept.at[n], 2 * EDGE + NJ, 16)):
                target = ref.at[:, pl.ds(start, size)]
                copies.append(pltpu.make_async_copy(source, target, sems.at[len(copies)]))
    for copy in copies:
        copy.start()
    pair = row_pair(side)
    gap = jnp.zeros((8, C), BF)
    for n in range(2):
        rows[4 - 4 * pair + n] = jnp.concatenate([gap, halo_ref[n], gap], axis=0)
    for n in range(ROWS):
        rows[2 * pair + n] = extended_ref[n]
    middle = jnp.zeros((EXT_WINDOW - 16, C), BF)
    for row in range(2):
        bands = bands_ref[2 - 2 * pair + row]
        for tile in range(STEPS + 1):
            if tile < STEPS:
                start = tile * J
                first = row * NJ + start
                cells = [rows[row + r, start : start + EXT_WINDOW, :] for r in range(WIDTH)]
            else:
                first = 2 * NJ + row * J
                cells = []
                for r in range(WIDTH):
                    cells += [rows[row + r, NJ : NJ + 8, :], middle, rows[row + r, 8:16, :]]
            found = jnp.dot(bands, jnp.concatenate(cells, axis=0), preferred_element_type=F32).astype(BF)
            for k in range(K):
                filtered[first : first + J, k * C : (k + 1) * C] = found[k * J : (k + 1) * J]
    for k in range(K):
        columns = slice(k * C, (k + 1) * C)
        part = jnp.dot(turned_ref[1 - pair], filtered[0 : 2 * NJ, columns], preferred_element_type=F32)
        total_ref[:, columns] = part if side == 0 else before_ref[:, columns] + part
    for copy in copies:
        copy.wait()


def filter_part(side, *operands):
    outs = [pltpu.VMEM((C, K * C), F32), pltpu.VMEM((2 * (NJ + J), K * C), BF)]
    scratch = [pltpu.VMEM((6, EXT, C), BF)]
    if side == 0:
        outs += [pltpu.VMEM((K * C, C), BF)]
        scratch += [pltpu.SemaphoreType.DMA(())]
    else:
        outs += [pltpu.VMEM((2, WIDE, C), BF)] * 2
        scratch += [pltpu.VMEM((2, 2, 16, C), BF), pltpu.SemaphoreType.DMA((4,))]
    return pl.pallas_call(
        functools.partial(filter_kernel, side),
        out_shape=tuple(outs),
        in_specs=[IN_VMEM] * (len(operands) - 1) + [IN_HBM],
        out_specs=[IN_VMEM] * len(outs),
        scratch_shapes=scratch,
        compiler_params=params(8),
        cost_estimate=cost(1e8, 1e5),
        name="filter_part",
    )(*operands[:-1], in_hbm(operands[-1]))


def edge_kernel(left_ref, right_ref, total_ref, near_ref, far_ref, _, __, own_ref, other_ref, chip_cot_ref, link_cot_ref, sems):
    core = lax.axis_index("core")
    copies = []
    for ref, first in ((chip_cot_ref, 2 - 2 * core), (link_cot_ref, 2 * core)):
        for source, start in ((left_ref, 0), (right_ref, EDGE + NJ)):
            target = ref.at[:, pl.ds(start, EDGE)]
            copies.append(pltpu.make_async_copy(source.at[pl.ds(first, 2)], target, sems.at[len(copies)]))
    for copy in copies:
        copy.start()
    edges = []
    for side in range(2):
        for row in range(2):
            i = 2 - 2 * row_pair(side) + row
            edges += [right_ref[i], left_ref[i]]
    edges = jnp.concatenate(edges, axis=0).T
    for k in range(K):
        columns = slice(k * C, (k + 1) * C)
        beyond = jnp.concatenate([near_ref[2 * NJ :, columns], far_ref[2 * NJ :, columns]], axis=0)
        total = total_ref[:, columns] + jnp.dot(edges, beyond, preferred_element_type=F32)
        first, second = total[:LANES], total[LANES:]
        mine = jnp.where(core == 0, first, second)
        theirs = jnp.where(core == 0, second, first).astype(BF)
        for part in range(2):
            lanes = slice(part * LANES, (part + 1) * LANES)
            own_ref[2 * k + part] = mine[:, lanes]
            other_ref[2 * k + part] = theirs[:, lanes]
    for block in range(BLOCKS, PADDED_BLOCKS):
        own_ref[block] = jnp.zeros((LANES, LANES), F32)
        other_ref[block] = jnp.zeros((LANES, LANES), BF)
    for copy in copies:
        copy.wait()


def edge_part(left, right, total, near, far, chip_cot, link_cot):
    shape = (PADDED_BLOCKS, LANES, LANES)
    return pl.pallas_call(
        edge_kernel,
        out_shape=(
            pltpu.VMEM(shape, F32),
            pltpu.VMEM(shape, BF),
            pltpu.VMEM((2, WIDE, C), BF),
            pltpu.VMEM((2, WIDE, C), BF),
        ),
        in_specs=[IN_VMEM] * 5 + [ANYWHERE] * 2,
        out_specs=[IN_VMEM] * 2 + [ANYWHERE] * 2,
        input_output_aliases={5: 2, 6: 3},
        scratch_shapes=[pltpu.SemaphoreType.DMA((4,))],
        compiler_params=params(4),
        cost_estimate=cost(1e9, 4e6),
        name="edge_part",
    )(left, right, total, near, far, chip_cot, link_cot)


def half_kernel(own_ref, other_ref, _, out_ref, half, sems):
    copies = []
    for n in range(4):
        part = pl.ds(n * PADDED_BLOCKS // 4, PADDED_BLOCKS // 4)
        half[part] = (own_ref[part] + other_ref[part].astype(F32)).astype(BF)
        copies.append(pltpu.make_async_copy(half.at[part], out_ref.at[part], sems.at[n]))
        copies[n].start()
    for copy in copies:
        copy.wait()


def half_part(own, other, after):
    return pl.pallas_call(
        half_kernel,
        out_shape=jax.ShapeDtypeStruct(own.shape, BF),
        in_specs=[IN_VMEM] * 2 + [ANYWHERE],
        out_specs=IN_HBM,
        scratch_shapes=[pltpu.VMEM(own.shape, BF), pltpu.SemaphoreType.DMA((4,))],
        compiler_params=params(4),
        cost_estimate=cost(1e6, 3e6),
        name="half_part",
    )(own, other, after)


def mixed_kernel(near_ref, far_ref, weight_ref, mixed_ref, ends_ref, to_right_ref, to_left_ref):
    for side, filtered_ref in enumerate((near_ref, far_ref)):
        first = 2 - 2 * row_pair(side)
        beyond = jnp.dot(filtered_ref[2 * NJ :, :], weight_ref[...], preferred_element_type=F32)
        for row in range(2):
            to_right_ref[first + row] = beyond[row * J : row * J + EDGE]
            to_left_ref[first + row] = beyond[row * J + EDGE : (row + 1) * J]
            found = jnp.dot(
                filtered_ref[row * NJ : (row + 1) * NJ, :], weight_ref[...], preferred_element_type=F32
            )
            ends_ref[first + row, 0:EDGE, :] = found[0:EDGE]
            ends_ref[first + row, EDGE:, :] = found[NJ - EDGE :]
            mixed_ref[first + row] = found.astype(BF)


def mixed_part(near, far, weight):
    return pl.pallas_call(
        mixed_kernel,
        out_shape=(
            pltpu.VMEM((ROWS, NJ, C), BF),
            pltpu.VMEM((ROWS, 2 * EDGE, C), F32),
            pltpu.VMEM((ROWS, EDGE, C), F32),
            pltpu.VMEM((ROWS, EDGE, C), F32),
        ),
        in_specs=[IN_VMEM] * 3,
        out_specs=[IN_VMEM] * 4,
        compiler_params=params(4),
        cost_estimate=cost(1e9, 2e6),
        name="mixed_part",
    )(near, far, weight)


def ends_kernel(ends_ref, left_ref, right_ref, mixed_ref, _, out_ref, done_ref, ends, sems):
    middle = pl.ds(EDGE, NJ - 2 * EDGE)
    copies = [pltpu.make_async_copy(mixed_ref.at[:, middle], out_ref.at[:, middle], sems.at[2])]
    copies[0].start()
    ends[0] = (ends_ref[:, 0:EDGE, :] + left_ref[...]).astype(BF)
    ends[1] = (ends_ref[:, EDGE:, :] + right_ref[...]).astype(BF)
    for n, first in enumerate((0, NJ - EDGE)):
        target = out_ref.at[:, pl.ds(first, EDGE)]
        copies.append(pltpu.make_async_copy(ends.at[n], target, sems.at[n]))
        copies[-1].start()
    done_ref[...] = jnp.zeros_like(done_ref)
    for copy in copies:
        copy.wait()


def ends_part(ends, left, right, mixed, after):
    return pl.pallas_call(
        ends_kernel,
        out_shape=(jax.ShapeDtypeStruct(mixed.shape, BF), pltpu.VMEM((8, LANES), F32)),
        in_specs=[IN_VMEM] * 4 + [ANYWHERE],
        out_specs=[IN_HBM, IN_VMEM],
        scratch_shapes=[pltpu.VMEM((2, ROWS, EDGE, C), BF), pltpu.SemaphoreType.DMA((3,))],
        compiler_params=params(4),
        cost_estimate=cost(1e6, 1e6),
        name="ends_part",
    )(ends, left, right, mixed, after)


def sum_kernel(scale, pieces_ref, out_ref):
    piece = (jnp.sum(pieces_ref[...].astype(F32), axis=0) * scale).astype(BF)
    out_ref[...] = jnp.broadcast_to(piece, out_ref.shape)


def sum_part(pieces, scale):
    return pl.pallas_call(
        functools.partial(sum_kernel, scale),
        out_shape=pltpu.VMEM(pieces.shape, BF),
        in_specs=[IN_VMEM],
        out_specs=IN_VMEM,
        compiler_params=params(4),
        cost_estimate=cost(1e6, 2e6),
        name="sum_part",
    )(pieces)


def order_kernel(*_):
    pass


def ordered(value, after):
    return pl.pallas_call(
        order_kernel,
        out_shape=jax.ShapeDtypeStruct(value.shape, value.dtype),
        in_specs=[ANYWHERE, ANYWHERE],
        out_specs=ANYWHERE,
        input_output_aliases={0: 0},
        compiler_params=params(1),
        name="ordered",
    )(value, after)


def result_kernel(side, half_ref, *refs):
    out_ref, block, sems = refs[-3:]
    core = lax.axis_index("core")
    lanes = pl.ds(pl.multiple_of((core if side == 0 else 1 - core) * LANES, LANES), LANES)
    copies = []
    for k in range(K):
        for part in range(2):
            block[k, part * LANES : (part + 1) * LANES, :] = half_ref[2 * k + part].astype(F32).T
        copies.append(pltpu.make_async_copy(block.at[k], out_ref.at[k, :, lanes], sems.at[k]))
        copies[k].start()
    for copy in copies:
        copy.wait()


def result_part(half, result=None):
    given = [] if result is None else [result]
    return pl.pallas_call(
        functools.partial(result_kernel, len(given)),
        out_shape=jax.ShapeDtypeStruct((K, C, C), F32),
        in_specs=[IN_VMEM] + [IN_HBM] * len(given),
        out_specs=IN_HBM,
        input_output_aliases={1: 0} if given else {},
        scratch_shapes=[pltpu.VMEM((K, C, LANES), F32), pltpu.SemaphoreType.DMA((K,))],
        compiler_params=params(6),
        cost_estimate=cost(1e6, 4e6),
        name="result_part",
    )(half, *given)


def extend(extended, n, row, left, right):
    extended[n] = jnp.concatenate([left, row, right], axis=0)


def grad_kernel(kept_ref, chip_ref, link_ref, left_ref, right_ref, weight_hbm, cot_hbm, _, out_ref, done_ref, weight, weight_turned, cot, extended, bands, cells, filtered, mixed, sems):
    core = lax.axis_index("core")
    cot_copy = pltpu.make_async_copy(cot_hbm, cot, sems.at[ROWS])
    cot_copy.start()
    weight_copy = pltpu.make_async_copy(weight_hbm, weight, sems.at[ROWS + 1])
    weight_copy.start()

    def fill(low, high):
        for n in range(2):
            extended[n] = low[n, 8 : 8 + EXT, :]
            extended[6 + n] = high[n, 8 : 8 + EXT, :]
            cells[n] = low[n, 2 * EDGE + NJ :, 0:LANES]
            cells[6 + n] = high[n, 2 * EDGE + NJ :, 0:LANES]

    pl.when(core == 0)(lambda: fill(link_ref, chip_ref))
    pl.when(core == 1)(lambda: fill(chip_ref, link_ref))
    for n in range(ROWS):
        cells[2 + n] = kept_ref[n]

    away = (TAPS - 1 - lax.broadcasted_iota(jnp.int32, (16, LANES), 1)) // WIDTH
    place = one_hot(lambda tap: (TAPS - 1 - tap) // WIDTH * EXT_WINDOW + 8 - RAD + (TAPS - 1 - tap) % WIDTH)
    lines = []
    for row in range(ROWS):
        taken = jnp.zeros((16, LANES), F32)
        for r in range(WIDTH):
            taken = jnp.where(away == r, cells[row + r].astype(F32), taken)
        lines.append(jnp.dot(taken.astype(BF), place, preferred_element_type=F32))
    cot_copy.wait()
    for n in range(ROWS):
        extend(extended, 2 + n, cot[n], left_ref[n, 8:, :], right_ref[n, :8, :])
    copies = [pltpu.make_async_copy(mixed.at[row], out_ref.at[row], sems.at[row]) for row in range(ROWS)]
    for row in range(ROWS):
        slot = row % 2
        for k in range(K):
            bands[slot, k * J : (k + 1) * J, :] = banded(lines[row][k : k + 1, :])[:, :DEPTH]
        for tile in range(STEPS):
            start = tile * J
            window = jnp.concatenate(
                [extended[row + r, start : start + EXT_WINDOW, :] for r in range(WIDTH)], axis=0
            )
            found = jnp.dot(bands[slot], window, preferred_element_type=F32).astype(BF)
            for k in range(K):
                filtered[slot, start : start + J, k * C : (k + 1) * C] = found[k * J : (k + 1) * J]
        if row == 0:
            weight_copy.wait()
            for k in range(K):
                columns = slice(k * C, (k + 1) * C)
                weight_turned[columns, :] = weight[columns, :].T
        mixed[row] = jnp.dot(filtered[slot], weight_turned[...], preferred_element_type=F32).astype(BF)
        copies[row].start()
    for copy in copies:
        copy.wait()
    done_ref[...] = jnp.zeros_like(done_ref)


def grad_part(kept, chip, link, left, right, weight, cotangent, after):
    return pl.pallas_call(
        grad_kernel,
        out_shape=(jax.ShapeDtypeStruct((ROWS, NJ, C), BF), pltpu.VMEM((8, LANES), F32)),
        in_specs=[IN_VMEM] * 5 + [IN_HBM, IN_HBM, ANYWHERE],
        out_specs=[IN_HBM, IN_VMEM],
        scratch_shapes=[
            pltpu.VMEM((K * C, C), BF),
            pltpu.VMEM((K * C, C), BF),
            pltpu.VMEM((ROWS, NJ, C), BF),
            pltpu.VMEM((PLACES, EXT, C), BF),
            pltpu.VMEM((2, K * J, DEPTH), BF),
            pltpu.VMEM((PLACES, 16, LANES), BF),
            pltpu.VMEM((2, NJ, K * C), BF),
            pltpu.VMEM((ROWS, NJ, C), BF),
            pltpu.SemaphoreType.DMA((ROWS + 2,)),
        ],
        compiler_params=params(20),
        cost_estimate=cost(8e9, 5e6),
        name="grad_input_part",
    )(kept, chip, link, left, right, in_hbm(weight), in_hbm(cotangent), after)


def shifted(block, axis, count, step, periodic):
    route = [(i, (i + step) % count) for i in range(count) if periodic or 0 <= i + step < count]
    return lax.ppermute(block, axis, route)


def per_device(features, basis, span_lo, span_hi, weight, cotangent):
    lat, chips = ("yz", "core"), ("yz", "lon")
    lats, lons = lax.axis_size("yz") * lax.axis_size("core"), lax.axis_size("lon")
    parts = lax.axis_size("yz") * lons
    swap = [(0, 1), (1, 0)]

    pairs = [(i, i + 1) for i in range(1, lats - 1, 2)]
    pairs = pairs + [(b, a) for a, b in pairs]
    chip, link = send_part(features)
    weight = weight.reshape(K * C, C)
    to_right, to_left, kept, turned, extended, bands = own_part(
        span_lo, span_hi, basis, cotangent, features, link
    )
    chip = lax.ppermute(chip, "core", swap)
    link = lax.ppermute(link, lat, pairs)
    near_left = shifted(to_right, "lon", lons, 1, True)
    near_right = shifted(to_left, "lon", lons, -1, True)
    total, near, weight_near = filter_part(0, chip, extended, bands, turned, weight)
    total, far, chip_cot, link_cot = filter_part(
        1, link, extended, bands, turned, total, kept, cotangent
    )
    own, other, chip_cot, link_cot = edge_part(near_left, near_right, total, near, far, chip_cot, link_cot)

    other = lax.ppermute(other, "core", swap)
    mixed, ends, to_right, to_left = mixed_part(near, far, weight_near)
    half = half_part(own, other, ends)
    pieces = lax.all_to_all(half.reshape(parts, -1, LANES), chips, 0, 0)
    link_cot = lax.ppermute(ordered(link_cot, half), lat, pairs)
    chip_cot = lax.ppermute(ordered(chip_cot, half), "core", swap)
    left = shifted(ordered(to_right, half), "lon", lons, 1, True)
    right = shifted(ordered(to_left, half), "lon", lons, -1, True)
    scale = 1.0 / math.sqrt(ROWS * lats * NJ * lons)
    copies = sum_part(pieces, scale)
    gathered = lax.all_to_all(copies, chips, 0, 0).reshape(PADDED_BLOCKS, LANES, LANES)
    mixed, mixed_done = ends_part(ends, left, right, mixed, copies)
    grad_input, grad_done = grad_part(
        kept, chip_cot, link_cot, near_left, near_right, weight, cotangent, mixed_done
    )
    gathered = ordered(gathered, grad_done)
    other = lax.ppermute(gathered, "core", swap)
    grad_weight = result_part(other, result_part(gathered))
    return mixed, grad_input, grad_weight


def solution(mesh):
    lats, lons = mesh.devices.shape
    split = Mesh(mesh.devices.reshape(lats // 2, 2, lons), ("yz", "core", "lon"))
    lat = ("yz", "core")
    return jax.shard_map(
        per_device,
        mesh=split,
        in_specs=(P(lat, "lon", None), P(lat, None, None), P(lat), P(lat), P(), P(lat, "lon", None)),
        out_specs=(P(lat, "lon", None), P(lat, "lon", None), P()),
        check_vma=False,
    )
```

time: 78.2 us -> 73.1 us (0.935)
  starting transfers between devices: 43.3 us -> 40.1 us
  waiting for transfers between devices: 7.55 us -> 4.48 us
  Pallas kernels: 26.1 us -> 27.1 us
    all_to_all x1, starting transfers between devices: 13.8 us -> 10.6 us  [per_device(): pieces = lax.all_to_all(half.reshape(parts, -1, LANES), chips, 0, 0)]
    all_to_all x1, waiting for transfers between devices: 1.96 us -> 0.41 us  [per_device(): lax.all_to_all(copies, chips, 0, 0).reshape(PADDED_BLOCKS, LANES, LANES)]
    pallas_call x1, Pallas kernels: 8.46 us -> 9.69 us  [grad_part(): pl.pallas_call(grad_kernel, out_shape=(jax.ShapeDtypeStruct((ROWS, NJ, C)...]
    ppermute x1, waiting for transfers between devices: 1.72 us -> 0.54 us  [per_device(): other = lax.ppermute(gathered, 'core', swap)]
    pallas_call x5 -> x8, Pallas kernels: 14.6 us -> 14.2 us  [the longest x2 5.65 us: filter_part(): pl.pallas_call(functools.partial(filter_kernel, side), out_shape=tuple(ou...]
  transfers between devices with their start and end apart: 12 -> 12, of which waited for: 4 -> 3; matrix products, arithmetic and copies ran while one was open for 0% -> 0% of each run, Pallas kernels for 19% -> 32%
where the time goes in v4:
time: 73.1 us; the launch traced here: 72.7 us
  starting transfers between devices  40.1 us (55%)
  Pallas kernels  27.1 us (37%)
  waiting for transfers between devices  4.48 us (6%)
  between operations  1.01 us (1%)
    all_to_all x1, starting transfers between devices, per_device(): pieces = lax.all_to_all(half.reshape(parts, -1, LANES), chips, 0, 0)  10.6 us
    ppermute x4, starting transfers between devices, shifted(): return lax.ppermute(block, axis, route)  10.4 us
    pallas_call x1, Pallas kernels, grad_part(): pl.pallas_call(grad_kernel, out_shape=(jax.ShapeDtypeStruct((ROWS, NJ, C)...  9.69 us
    all_to_all x1, starting transfers between devices, per_device(): lax.all_to_all(copies, chips, 0, 0).reshape(PADDED_BLOCKS, LANES, LANES)  6.02 us
    pallas_call x2, Pallas kernels, filter_part(): pl.pallas_call(functools.partial(filter_kernel, side), out_shape=tuple(ou...  5.65 us
    ppermute x1, starting transfers between devices, per_device(): other = lax.ppermute(gathered, 'core', swap)  4.07 us
    ppermute x1, starting transfers between devices, per_device(): link = lax.ppermute(link, lat, pairs)  3.53 us
    all_to_all x1, waiting for transfers between devices, per_device(): pieces = lax.all_to_all(half.reshape(parts, -1, LANES), chips, 0, 0)  3.52 us
  transfers between devices with their start and end apart: 12, of which 3 were waited for; matrix products, arithmetic and copies ran while one was open for 0% of the time, Pallas kernels for 32%

profile of v4, /device:TPU:1, one launch (start us, length us, event | category | flops | bytes accessed | tf_op | source)
XLA Modules:
  0.0 72.7 jit_solution(14397998493189205769)
XLA Ops:
  0.6 1.2 %send_part.1 = (bf16[2,512,256]{2,1,0:T(8,128)(2,1)S(1)}, bf16[2,512,256]{2,1,0:T(8,128)(2,1)S(1)}) custom-call(bf16[4,512,256]{2,1,0:T(8,128)(2,1)} %feat_ref.3), custom_call_target="tpu_custom_call" | custom-call | bytes 1000000 | tf_op jit(solution)/shard_map/send_part/pallas_call | solution.py:75
  1.9 1.5 %collective-permute-start = (bf16[2,512,256]{2,1,0:T(8,128)(2,1)S(1)}, bf16[2,512,256]{2,1,0:T(8,128)(2,1)S(1)}, u32[]{:S(2)}, u32[]{:S(2)}) collective-permute-start(bf16[2,512,256]{2,1,0:T(8,128)(2,1)S(1)} %get-tuple-element.30), channel_id=1, source_target_pairs={{0,8},{8,0},{1,9},{9,1},{2,10},{10,2},{3,11},{11,3},{4,12},{12,4},... | collective-permute-start | bytes 1572872 | tf_op jit(solution)/shard_map/ppermute | solution.py:520
  3.4 3.5 %collective-permute-start.1 = (bf16[2,512,256]{2,1,0:T(8,128)(2,1)S(1)}, bf16[2,512,256]{2,1,0:T(8,128)(2,1)S(1)}, u32[]{:S(2)}, u32[]{:S(2)}) collective-permute-start(bf16[2,512,256]{2,1,0:T(8,128)(2,1)S(1)} %get-tuple-element.31._), channel_id=1, source_target_pairs={{8,16},{24,32},{40,48},{56,64},{72,80},{88,96},{104,112},{16,8},{3... | collective-permute-start | bytes 1572872 | tf_op jit(solution)/shard_map/ppermute | solution.py:521
  6.9 1.7 %own_part.1 = (bf16[4,16,256]{2,1,0:T(8,128)(2,1)S(1)}, bf16[4,16,256]{2,1,0:T(8,128)(2,1)S(1)}, bf16[4,16,128]{2,1,0:T(8,128)(2,1)S(1)}, bf16[2,256,1024]{2,1,0...) custom-call(s32[4]{0:T(128)} %lo_ref.1, s32[4]{0:T(128)} %hi_ref.1, ...), custom_call_target="tpu_custom_call" | custom-call | flops 4000000000 | bytes 4000000 | tf_op jit(solution)/shard_map/own_part/pallas_call | solution.py:122
  8.6 1.3 %collective-permute-start.2 = (bf16[4,16,256]{2,1,0:T(8,128)(2,1)S(1)}, bf16[4,16,256]{2,1,0:T(8,128)(2,1)S(1)}, u32[]{:S(2)}, u32[]{:S(2)}) collective-permute-start(bf16[4,16,256]{2,1,0:T(8,128)(2,1)S(1)} %get-tuple-element.42), channel_id=1, source_target_pairs={{0,1},{1,2},{2,3},{3,4},{4,5},{5,6},{6,7},{7,0},{8,9},{9,10},{10,1... | collective-permute-start | bytes 98312 | tf_op jit(solution)/shard_map/ppermute | solution.py:504
  9.9 4.0 %collective-permute-start.3 = (bf16[4,16,256]{2,1,0:T(8,128)(2,1)S(1)}, bf16[4,16,256]{2,1,0:T(8,128)(2,1)S(1)}, u32[]{:S(2)}, u32[]{:S(2)}) collective-permute-start(bf16[4,16,256]{2,1,0:T(8,128)(2,1)S(1)} %get-tuple-element.43), channel_id=1, source_target_pairs={{0,7},{1,0},{2,1},{3,2},{4,3},{5,4},{6,5},{7,6},{8,15},{9,8},{10,9... | collective-permute-start | bytes 98312 | tf_op jit(solution)/shard_map/ppermute | solution.py:504
  13.9 2.8 %filter_part.2 = (f32[256,2304]{1,0:T(8,128)S(1)}, bf16[1088,2304]{1,0:T(8,128)(2,1)S(1)}, bf16[2304,256]{1,0:T(8,128)(2,1)S(1)}) custom-call(bf16[2,512,256]{2,1,0:T(8,128)(2,1)S(1)} %collective-permute-done.halo_ref, bf16[4,528,256]{2,1,0:T(8,128)(2,1)S(1)} %get-tuple-element.32.extended_ref, bf16[4,288,240]{2,1,0:T(8,128)(2,1)S(1)} %get-tuple-element.33.bands_ref, ...), custom_call_target="tpu_custom_call" | custom-call | flops 100000000 | bytes 100000 | tf_op jit(solution)/shard_map/filter_part/pallas_call | solution.py:209
  16.7 2.9 %filter_part.3 = (f32[256,2304]{1,0:T(8,128)S(1)}, bf16[1088,2304]{1,0:T(8,128)(2,1)S(1)}, bf16[2,560,256]{2,1,0:T(8,128)(2,1)S(1)}, bf16[2,560,256]{2,1,0:T(8,128)(2,1)S(1)}) custom-call(bf16[2,512,256]{2,1,0:T(8,128)(2,1)S(1)} %collective-permute-done.1.halo_ref, bf16[4,528,256]{2,1,0:T(8,128)(2,1)S(1)} %get-tuple-element.32.extended_ref, ...), custom_call_target="tpu_custom_call" | custom-call | flops 100000000 | bytes 100000 | tf_op jit(solution)/shard_map/filter_part/pallas_call | solution.py:209
  19.6 0.6 edge_part.1
  20.3 3.0 %mixed_part.1 = (bf16[4,512,256]{2,1,0:T(8,128)(2,1)S(1)}, f32[4,32,256]{2,1,0:T(8,128)S(1)}, f32[4,16,256]{2,1,0:T(8,128)S(1)}, f32[4,16,256]{2,1,0:T(8,128)S(1)}) custom-call(bf16[1088,2304]{1,0:T(8,128)(2,1)S(1)} %get-tuple-element.35.near_ref, bf16[1088,2304]{1,0:T(8,128)(2,1)S(1)} %get-tuple-element.38.far_ref, ...), custom_call_target="tpu_custom_call" | custom-call | flops 1000000000 | bytes 2000000 | tf_op jit(solution)/shard_map/mixed_part/pallas_call | solution.py:314
  23.3 0.9 %half_part.1.__1_ = bf16[20,128,128]{2,1,0:T(8,128)(2,1)} custom-call(f32[20,128,128]{2,1,0:T(8,128)S(1)} %get-tuple-element.47.own_ref, bf16[20,128,128]{2,1,0:T(8,128)(2,1)S(1)} %collective-permute-done.4.other_ref, f32[4,32,256]{2,1,0:T(8,128)S(1)} %get-tuple-element.40._.ends_ref), custom_call_target="tpu_custom_call" | custom-call | flops 1000000 | bytes 3000000 | tf_op jit(solution)/shard_map/half_part/pallas_call | solution.py:286
  24.2 10.6 %all-to-all-start = ((bf16[64,40,128]{2,1,0:T(8,128)(2,1)}), bf16[64,40,128]{2,1,0:T(8,128)(2,1)S(1)}, u32[]{:S(2)}, u32[]{:S(2)}) async-start(bf16[64,40,128]{2,1,0:T(8,128)(2,1)} %bitcast.2), calls=%async_computation | async-start | bytes 1310720 | tf_op jit(solution)/shard_map/all_to_all | solution.py:533
  34.8 0.8 %collective-permute-start.7 = (bf16[2,560,256]{2,1,0:T(8,128)(2,1)S(1)}, bf16[2,560,256]{2,1,0:T(8,128)(2,1)}, u32[]{:S(2)}, u32[]{:S(2)}) collective-permute-start(bf16[2,560,256]{2,1,0:T(8,128)(2,1)S(1)} %ordered.7), channel_id=1, source_target_pairs={{0,8},{8,0},{1,9},{9,1},{2,10},{10,2},{3,11},{11,3},{4,12},{12,4},... | collective-permute-start | bytes 1720328 | tf_op jit(solution)/shard_map/ppermute | solution.py:535
  35.7 3.1 %collective-permute-start.8 = (bf16[2,560,256]{2,1,0:T(8,128)(2,1)S(1)}, bf16[2,560,256]{2,1,0:T(8,128)(2,1)}, u32[]{:S(2)}, u32[]{:S(2)}) collective-permute-start(bf16[2,560,256]{2,1,0:T(8,128)(2,1)S(1)} %ordered.8), channel_id=1, source_target_pairs={{8,16},{24,32},{40,48},{56,64},{72,80},{88,96},{104,112},{16,8},{3... | collective-permute-start | bytes 1720328 | tf_op jit(solution)/shard_map/ppermute | solution.py:534
  38.8 1.3 %collective-permute-start.5 = (f32[4,16,256]{2,1,0:T(8,128)S(1)}, f32[4,16,256]{2,1,0:T(8,128)S(1)}, u32[]{:S(2)}, u32[]{:S(2)}) collective-permute-start(f32[4,16,256]{2,1,0:T(8,128)S(1)} %ordered.5), channel_id=1, source_target_pairs={{0,1},{1,2},{2,3},{3,4},{4,5},{5,6},{6,7},{7,0},{8,9},{9,10},{10,1... | collective-permute-start | bytes 196616 | tf_op jit(solution)/shard_map/ppermute | solution.py:504
  40.1 3.9 %collective-permute-start.6 = (f32[4,16,256]{2,1,0:T(8,128)S(1)}, f32[4,16,256]{2,1,0:T(8,128)S(1)}, u32[]{:S(2)}, u32[]{:S(2)}) collective-permute-start(f32[4,16,256]{2,1,0:T(8,128)S(1)} %ordered.6), channel_id=1, source_target_pairs={{0,7},{1,0},{2,1},{3,2},{4,3},{5,4},{6,5},{7,6},{8,15},{9,8},{10,9... | collective-permute-start | bytes 196616 | tf_op jit(solution)/shard_map/ppermute | solution.py:504
  44.0 3.5 %all-to-all-done.pieces_ref = bf16[64,40,128]{2,1,0:T(8,128)(2,1)S(1)} async-done(((bf16[64,40,128]{2,1,0:T(8,128)(2,1)}), bf16[64,40,128]{2,1,0:T(8,128)(2,1)S(1)}, u32[]{:S(2)}, u32[]{:S(2)}) %all-to-all-start) | async-done | bytes 655392 | tf_op jit(solution)/shard_map/all_to_all | solution.py:533
  47.5 1.0 %sum_part.1._ = bf16[64,40,128]{2,1,0:T(8,128)(2,1)} custom-call(bf16[64,40,128]{2,1,0:T(8,128)(2,1)S(1)} %all-to-all-done.pieces_ref), custom_call_target="tpu_custom_call" | custom-call | flops 1000000 | bytes 2000000 | tf_op jit(solution)/shard_map/sum_part/pallas_call | solution.py:364
  48.4 6.0 %all-to-all-start.1 = ((bf16[64,40,128]{2,1,0:T(8,128)(2,1)}), bf16[64,40,128]{2,1,0:T(8,128)(2,1)S(1)}, u32[]{:S(2)}, u32[]{:S(2)}) async-start(bf16[64,40,128]{2,1,0:T(8,128)(2,1)} %sum_part.1._), calls=%async_computation.1 | async-start | bytes 1310720 | tf_op jit(solution)/shard_map/all_to_all | solution.py:540
  54.5 1.0 %ends_part.1 = (bf16[4,512,256]{2,1,0:T(8,128)(2,1)}, f32[8,128]{1,0:T(8,128)S(1)}) custom-call(f32[4,32,256]{2,1,0:T(8,128)S(1)} %get-tuple-element.40._.ends_ref, f32[4,16,256]{2,1,0:T(8,128)S(1)} %collective-permute-done.5.left_ref, f32[4,16,256]{2,1,0:T(8,128)S(1)} %collective-permute-done.6.right_ref, ...), custom_call_target="tpu_custom_call" | custom-call | flops 1000000 | bytes 1000000 | tf_op jit(solution)/shard_map/ends_part/pallas_call | solution.py:346
  55.5 9.7 %grad_input_part.1 = (bf16[4,512,256]{2,1,0:T(8,128)(2,1)}, f32[8,128]{1,0:T(8,128)S(1)}) custom-call(bf16[4,16,128]{2,1,0:T(8,128)(2,1)S(1)} %get-tuple-element.37.refs_2_.kept_ref, bf16[2,560,256]{2,1,0:T(8,128)(2,1)} %collective-permute-done.7.chip_ref, bf16[2,560,256]{2,1,0:T(8,128)(2,1)} %collective-permute-done.8.link_ref, ...), custom_call_target="tpu_custom_call" | custom-call | flops 8000000000 | bytes 5000000 | tf_op jit(solution)/shard_map/grad_input_part/pallas_call | solution.py:480
  65.6 4.1 %collective-permute-start.9 = (bf16[20,128,128]{2,1,0:T(8,128)(2,1)S(1)}, bf16[20,128,128]{2,1,0:T(8,128)(2,1)S(1)}, u32[]{:S(2)}, u32[]{:S(2)}) collective-permute-start(bf16[20,128,128]{2,1,0:T(8,128)(2,1)S(1)} %ordered.9.half_ref), channel_id=1, source_target_pairs={{0,8},{8,0},{1,9},{9,1},{2,10},{10,2},{3,11},{11,3},{4,12},{12,4},... | collective-permute-start | bytes 1966088 | tf_op jit(solution)/shard_map/ppermute | solution.py:546
  69.7 1.2 %result_part.2.refs_0_ = f32[9,256,256]{2,1,0:T(8,128)} custom-call(bf16[20,128,128]{2,1,0:T(8,128)(2,1)S(1)} %ordered.9.half_ref), custom_call_target="tpu_custom_call" | custom-call | flops 1000000 | bytes 4000000 | tf_op jit(solution)/shard_map/result_part/pallas_call | solution.py:407
  71.4 1.2 %result_part.3 = f32[9,256,256]{2,1,0:T(8,128)} custom-call(bf16[20,128,128]{2,1,0:T(8,128)(2,1)S(1)} %collective-permute-done.9.half_ref, f32[9,256,256]{2,1,0:T(8,128)} %result_part.2.refs_0_), custom_call_target="tpu_custom_call", output_to_operand_aliasing={{}: (1, {})} | custom-call | flops 1000000 | bytes 4000000 | tf_op jit(solution)/shard_map/result_part/pallas_call | solution.py:407
  (17 shorter events, 1.1 us)
Async XLA Ops:
  1.9 12.0 %collective-permute-start = (bf16[2,512,256]{2,1,0:T(8,128)(2,1)S(1)}, bf16[2,512,256]{2,1,0:T(8,128)(2,1)S(1)}, u32[]{:S(2)}, u32[]{:S(2)}) collective-permute-start(bf16[2,512,256]{2,1,0:T(8,128)(2,1)S(1)} %get-tuple-element.30), channel_id=1, source_target_pairs={{0,8},{8,0},{1,9},{9,1},{2,10},{10,2},{3,11},{11,3},{4,12},{12,4},... | collective-permute-start | bytes 1572872 | tf_op jit(solution)/shard_map/ppermute | solution.py:520
  3.4 13.3 %collective-permute-start.1 = (bf16[2,512,256]{2,1,0:T(8,128)(2,1)S(1)}, bf16[2,512,256]{2,1,0:T(8,128)(2,1)S(1)}, u32[]{:S(2)}, u32[]{:S(2)}) collective-permute-start(bf16[2,512,256]{2,1,0:T(8,128)(2,1)S(1)} %get-tuple-element.31._), channel_id=1, source_target_pairs={{8,16},{24,32},{40,48},{56,64},{72,80},{88,96},{104,112},{16,8},{3... | collective-permute-start | bytes 1572872 | tf_op jit(solution)/shard_map/ppermute | solution.py:521
  8.6 10.9 %collective-permute-start.2 = (bf16[4,16,256]{2,1,0:T(8,128)(2,1)S(1)}, bf16[4,16,256]{2,1,0:T(8,128)(2,1)S(1)}, u32[]{:S(2)}, u32[]{:S(2)}) collective-permute-start(bf16[4,16,256]{2,1,0:T(8,128)(2,1)S(1)} %get-tuple-element.42), channel_id=1, source_target_pairs={{0,1},{1,2},{2,3},{3,4},{4,5},{5,6},{6,7},{7,0},{8,9},{9,10},{10,1... | collective-permute-start | bytes 98312 | tf_op jit(solution)/shard_map/ppermute | solution.py:504
  9.9 9.7 %collective-permute-start.3 = (bf16[4,16,256]{2,1,0:T(8,128)(2,1)S(1)}, bf16[4,16,256]{2,1,0:T(8,128)(2,1)S(1)}, u32[]{:S(2)}, u32[]{:S(2)}) collective-permute-start(bf16[4,16,256]{2,1,0:T(8,128)(2,1)S(1)} %get-tuple-element.43), channel_id=1, source_target_pairs={{0,7},{1,0},{2,1},{3,2},{4,3},{5,4},{6,5},{7,6},{8,15},{9,8},{10,9... | collective-permute-start | bytes 98312 | tf_op jit(solution)/shard_map/ppermute | solution.py:504
  20.2 3.1 %collective-permute-start.4 = (bf16[20,128,128]{2,1,0:T(8,128)(2,1)S(1)}, bf16[20,128,128]{2,1,0:T(8,128)(2,1)S(1)}, u32[]{:S(2)}, u32[]{:S(2)}) collective-permute-start(bf16[20,128,128]{2,1,0:T(8,128)(2,1)S(1)} %get-tuple-element.48), channel_id=1, source_target_pairs={{0,8},{8,0},{1,9},{9,1},{2,10},{10,2},{3,11},{11,3},{4,12},{12,4},... | collective-permute-start | bytes 1966088 | tf_op jit(solution)/shard_map/ppermute | solution.py:530
  24.2 23.2 %all-to-all-start = ((bf16[64,40,128]{2,1,0:T(8,128)(2,1)}), bf16[64,40,128]{2,1,0:T(8,128)(2,1)S(1)}, u32[]{:S(2)}, u32[]{:S(2)}) async-start(bf16[64,40,128]{2,1,0:T(8,128)(2,1)} %bitcast.2), calls=%async_computation | async-start | bytes 1310720 | tf_op jit(solution)/shard_map/all_to_all | solution.py:533
  34.8 20.6 %collective-permute-start.7 = (bf16[2,560,256]{2,1,0:T(8,128)(2,1)S(1)}, bf16[2,560,256]{2,1,0:T(8,128)(2,1)}, u32[]{:S(2)}, u32[]{:S(2)}) collective-permute-start(bf16[2,560,256]{2,1,0:T(8,128)(2,1)S(1)} %ordered.7), channel_id=1, source_target_pairs={{0,8},{8,0},{1,9},{9,1},{2,10},{10,2},{3,11},{11,3},{4,12},{12,4},... | collective-permute-start | bytes 1720328 | tf_op jit(solution)/shard_map/ppermute | solution.py:535
  35.7 19.8 %collective-permute-start.8 = (bf16[2,560,256]{2,1,0:T(8,128)(2,1)S(1)}, bf16[2,560,256]{2,1,0:T(8,128)(2,1)}, u32[]{:S(2)}, u32[]{:S(2)}) collective-permute-start(bf16[2,560,256]{2,1,0:T(8,128)(2,1)S(1)} %ordered.8), channel_id=1, source_target_pairs={{8,16},{24,32},{40,48},{56,64},{72,80},{88,96},{104,112},{16,8},{3... | collective-permute-start | bytes 1720328 | tf_op jit(solution)/shard_map/ppermute | solution.py:534
  38.8 15.7 %collective-permute-start.5 = (f32[4,16,256]{2,1,0:T(8,128)S(1)}, f32[4,16,256]{2,1,0:T(8,128)S(1)}, u32[]{:S(2)}, u32[]{:S(2)}) collective-permute-start(f32[4,16,256]{2,1,0:T(8,128)S(1)} %ordered.5), channel_id=1, source_target_pairs={{0,1},{1,2},{2,3},{3,4},{4,5},{5,6},{6,7},{7,0},{8,9},{9,10},{10,1... | collective-permute-start | bytes 196616 | tf_op jit(solution)/shard_map/ppermute | solution.py:504
  40.1 14.4 %collective-permute-start.6 = (f32[4,16,256]{2,1,0:T(8,128)S(1)}, f32[4,16,256]{2,1,0:T(8,128)S(1)}, u32[]{:S(2)}, u32[]{:S(2)}) collective-permute-start(f32[4,16,256]{2,1,0:T(8,128)S(1)} %ordered.6), channel_id=1, source_target_pairs={{0,7},{1,0},{2,1},{3,2},{4,3},{5,4},{6,5},{7,6},{8,15},{9,8},{10,9... | collective-permute-start | bytes 196616 | tf_op jit(solution)/shard_map/ppermute | solution.py:504
  48.4 17.2 %all-to-all-start.1 = ((bf16[64,40,128]{2,1,0:T(8,128)(2,1)}), bf16[64,40,128]{2,1,0:T(8,128)(2,1)S(1)}, u32[]{:S(2)}, u32[]{:S(2)}) async-start(bf16[64,40,128]{2,1,0:T(8,128)(2,1)} %sum_part.1._), calls=%async_computation.1 | async-start | bytes 1310720 | tf_op jit(solution)/shard_map/all_to_all | solution.py:540
  65.6 5.8 %collective-permute-start.9 = (bf16[20,128,128]{2,1,0:T(8,128)(2,1)S(1)}, bf16[20,128,128]{2,1,0:T(8,128)(2,1)S(1)}, u32[]{:S(2)}, u32[]{:S(2)}) collective-permute-start(bf16[20,128,128]{2,1,0:T(8,128)(2,1)S(1)} %ordered.9.half_ref), channel_id=1, source_target_pairs={{0,8},{8,0},{1,9},{9,1},{2,10},{10,2},{3,11},{11,3},{4,12},{12,4},... | collective-permute-start | bytes 1966088 | tf_op jit(solution)/shard_map/ppermute | solution.py:546

commit v5 on v4

--- a/solution.py
+++ b/solution.py
@@ -156,7 +156,7 @@
         turned_ref, weight_hbm, total_ref, filtered, weight_ref, rows, sem = refs
         copies.append(pltpu.make_async_copy(weight_hbm, weight_ref, sem))
     else:
-        turned_ref, before_ref, kept_ref, cot_ref, total_ref, filtered, chip_cot_ref, link_cot_ref, rows, kept, sems = refs
+        turned_ref, before_ref, kept_ref, _, cot_ref, total_ref, filtered, chip_cot_ref, link_cot_ref, rows, kept, sems = refs
         core = lax.axis_index("core")
         for n, (ref, first) in enumerate(((chip_cot_ref, 2 - 2 * core), (link_cot_ref, 2 * core))):
             kept[n] = jnp.zeros((2, 16, C), BF)
@@ -295,64 +295,71 @@
     )(own, other, after)
 
 
-def mixed_kernel(near_ref, far_ref, weight_ref, mixed_ref, ends_ref, to_right_ref, to_left_ref):
-    for side, filtered_ref in enumerate((near_ref, far_ref)):
-        first = 2 - 2 * row_pair(side)
-        beyond = jnp.dot(filtered_ref[2 * NJ :, :], weight_ref[...], preferred_element_type=F32)
-        for row in range(2):
-            to_right_ref[first + row] = beyond[row * J : row * J + EDGE]
-            to_left_ref[first + row] = beyond[row * J + EDGE : (row + 1) * J]
-            found = jnp.dot(
-                filtered_ref[row * NJ : (row + 1) * NJ, :], weight_ref[...], preferred_element_type=F32
-            )
-            ends_ref[first + row, 0:EDGE, :] = found[0:EDGE]
-            ends_ref[first + row, EDGE:, :] = found[NJ - EDGE :]
-            mixed_ref[first + row] = found.astype(BF)
-
-
-def mixed_part(near, far, weight):
-    return pl.pallas_call(
-        mixed_kernel,
+def mixed_kernel(side, filtered_ref, weight_ref, *refs):
+    mixed_ref, ends_ref, to_right_ref, to_left_ref = refs[-4:]
+    place = 2 * side
+    if side == 1:
+        to_right_ref[0:2] = refs[0][...]
+        to_left_ref[0:2] = refs[1][...]
+    beyond = jnp.dot(filtered_ref[2 * NJ :, :], weight_ref[...], preferred_element_type=F32)
+    for row in range(2):
+        to_right_ref[place + row] = beyond[row * J : row * J + EDGE]
+        to_left_ref[place + row] = beyond[row * J + EDGE : (row + 1) * J]
+        found = jnp.dot(
+            filtered_ref[row * NJ : (row + 1) * NJ, :], weight_ref[...], preferred_element_type=F32
+        )
+        ends_ref[row, 0:EDGE, :] = found[0:EDGE]
+        ends_ref[row, EDGE:, :] = found[NJ - EDGE :]
+        mixed_ref[row] = found.astype(BF)
+
+
+def mixed_part(side, *operands):
+    return pl.pallas_call(
+        functools.partial(mixed_kernel, side),
         out_shape=(
-            pltpu.VMEM((ROWS, NJ, C), BF),
-            pltpu.VMEM((ROWS, 2 * EDGE, C), F32),
-            pltpu.VMEM((ROWS, EDGE, C), F32),
-            pltpu.VMEM((ROWS, EDGE, C), F32),
+            pltpu.VMEM((2, NJ, C), BF),
+            pltpu.VMEM((2, 2 * EDGE, C), F32),
+            pltpu.VMEM((2 + 2 * side, EDGE, C), F32),
+            pltpu.VMEM((2 + 2 * side, EDGE, C), F32),
         ),
-        in_specs=[IN_VMEM] * 3,
+        in_specs=[IN_VMEM] * len(operands),
         out_specs=[IN_VMEM] * 4,
         compiler_params=params(4),
-        cost_estimate=cost(1e9, 2e6),
+        cost_estimate=cost(1e8, 1e5),
         name="mixed_part",
-    )(near, far, weight)
-
-
-def ends_kernel(ends_ref, left_ref, right_ref, mixed_ref, _, out_ref, done_ref, ends, sems):
+    )(*operands)
+
+
+def ends_kernel(near_ends_ref, far_ends_ref, left_ref, right_ref, near_ref, far_ref, _, out_ref, done_ref, ends, sems):
     middle = pl.ds(EDGE, NJ - 2 * EDGE)
-    copies = [pltpu.make_async_copy(mixed_ref.at[:, middle], out_ref.at[:, middle], sems.at[2])]
-    copies[0].start()
-    ends[0] = (ends_ref[:, 0:EDGE, :] + left_ref[...]).astype(BF)
-    ends[1] = (ends_ref[:, EDGE:, :] + right_ref[...]).astype(BF)
-    for n, first in enumerate((0, NJ - EDGE)):
-        target = out_ref.at[:, pl.ds(first, EDGE)]
-        copies.append(pltpu.make_async_copy(ends.at[n], target, sems.at[n]))
+    copies = []
+    for side, (ends_ref, mixed_ref) in enumerate(((near_ends_ref, near_ref), (far_ends_ref, far_ref))):
+        rows = pl.ds(2 - 2 * row_pair(side), 2)
+        places = slice(2 * side, 2 * side + 2)
+        copies.append(pltpu.make_async_copy(mixed_ref.at[:, middle], out_ref.at[rows, middle], sems.at[side, 2]))
         copies[-1].start()
+        ends[side, 0] = (ends_ref[:, 0:EDGE, :] + left_ref[places]).astype(BF)
+        ends[side, 1] = (ends_ref[:, EDGE:, :] + right_ref[places]).astype(BF)
+        for n, first in enumerate((0, NJ - EDGE)):
+            target = out_ref.at[rows, pl.ds(first, EDGE)]
+            copies.append(pltpu.make_async_copy(ends.at[side, n], target, sems.at[side, n]))
+            copies[-1].start()
     done_ref[...] = jnp.zeros_like(done_ref)
     for copy in copies:
         copy.wait()
 
 
-def ends_part(ends, left, right, mixed, after):
+def ends_part(near_ends, far_ends, left, right, near, far, after):
     return pl.pallas_call(
         ends_kernel,
-        out_shape=(jax.ShapeDtypeStruct(mixed.shape, BF), pltpu.VMEM((8, LANES), F32)),
-        in_specs=[IN_VMEM] * 4 + [ANYWHERE],
+        out_shape=(jax.ShapeDtypeStruct((ROWS, NJ, C), BF), pltpu.VMEM((8, LANES), F32)),
+        in_specs=[IN_VMEM] * 6 + [ANYWHERE],
         out_specs=[IN_HBM, IN_VMEM],
-        scratch_shapes=[pltpu.VMEM((2, ROWS, EDGE, C), BF), pltpu.SemaphoreType.DMA((3,))],
+        scratch_shapes=[pltpu.VMEM((2, 2, 2, EDGE, C), BF), pltpu.SemaphoreType.DMA((2, 3))],
         compiler_params=params(4),
         cost_estimate=cost(1e6, 1e6),
         name="ends_part",
-    )(ends, left, right, mixed, after)
+    )(near_ends, far_ends, left, right, near, far, after)
 
 
 def sum_kernel(scale, pieces_ref, out_ref):
@@ -522,14 +529,15 @@
     near_left = shifted(to_right, "lon", lons, 1, True)
     near_right = shifted(to_left, "lon", lons, -1, True)
     total, near, weight_near = filter_part(0, chip, extended, bands, turned, weight)
+    near_mixed, near_ends, to_right, to_left = mixed_part(0, near, weight_near)
     total, far, chip_cot, link_cot = filter_part(
-        1, link, extended, bands, turned, total, kept, cotangent
+        1, link, extended, bands, turned, total, kept, to_right, cotangent
     )
     own, other, chip_cot, link_cot = edge_part(near_left, near_right, total, near, far, chip_cot, link_cot)
 
     other = lax.ppermute(other, "core", swap)
-    mixed, ends, to_right, to_left = mixed_part(near, far, weight_near)
-    half = half_part(own, other, ends)
+    far_mixed, far_ends, to_right, to_left = mixed_part(1, far, weight_near, to_right, to_left)
+    half = half_part(own, other, far_ends)
     pieces = lax.all_to_all(half.reshape(parts, -1, LANES), chips, 0, 0)
     link_cot = lax.ppermute(ordered(link_cot, half), lat, pairs)
     chip_cot = lax.ppermute(ordered(chip_cot, half), "core", swap)
@@ -538,7 +546,7 @@
     scale = 1.0 / math.sqrt(ROWS * lats * NJ * lons)
     copies = sum_part(pieces, scale)
     gathered = lax.all_to_all(copies, chips, 0, 0).reshape(PADDED_BLOCKS, LANES, LANES)
-    mixed, mixed_done = ends_part(ends, left, right, mixed, copies)
+    mixed, mixed_done = ends_part(near_ends, far_ends, left, right, near_mixed, far_mixed, copies)
     grad_input, grad_done = grad_part(
         kept, chip_cot, link_cot, near_left, near_right, weight, cotangent, mixed_done
     )

time: 73.1 us -> 72.3 us (0.989)
  starting transfers between devices: 40.1 us -> 38 us
  waiting for transfers between devices: 4.48 us -> 5.6 us
    all_to_all x1, starting transfers between devices: 10.6 us -> 8.98 us  [per_device(): pieces = lax.all_to_all(half.reshape(parts, -1, LANES), chips, 0, 0)]
    pallas_call x2 -> x3, Pallas kernels: 3.99 us -> 4.18 us  [the longest x2 3.16 us: mixed_part(): pl.pallas_call(functools.partial(mixed_kernel, side), out_shape=(pltpu.VM...]
  transfers between devices with their start and end apart: 12 -> 12, of which waited for: 3 -> 4; matrix products, arithmetic and copies ran while one was open for 0% -> 0% of each run, Pallas kernels for 32% -> 33%
where the time goes in v5:
time: 72.3 us; the launch traced here: 71.9 us
  starting transfers between devices  38 us (53%)
  Pallas kernels  27.3 us (38%)
  waiting for transfers between devices  5.6 us (8%)
  between operations  1.01 us (1%)
    ppermute x4, starting transfers between devices, shifted(): return lax.ppermute(block, axis, route)  10.4 us
    pallas_call x1, Pallas kernels, grad_part(): pl.pallas_call(grad_kernel, out_shape=(jax.ShapeDtypeStruct((ROWS, NJ, C)...  9.69 us
    all_to_all x1, starting transfers between devices, per_device(): pieces = lax.all_to_all(half.reshape(parts, -1, LANES), chips, 0, 0)  8.98 us
    all_to_all x1, starting transfers between devices, per_device(): lax.all_to_all(copies, chips, 0, 0).reshape(PADDED_BLOCKS, LANES, LANES)  5.84 us
    pallas_call x2, Pallas kernels, filter_part(): pl.pallas_call(functools.partial(filter_kernel, side), out_shape=tuple(ou...  5.65 us
    all_to_all x1, waiting for transfers between devices, per_device(): pieces = lax.all_to_all(half.reshape(parts, -1, LANES), chips, 0, 0)  4.17 us
    ppermute x1, starting transfers between devices, per_device(): other = lax.ppermute(gathered, 'core', swap)  4.06 us
    ppermute x1, starting transfers between devices, per_device(): link = lax.ppermute(link, lat, pairs)  3.53 us
  transfers between devices with their start and end apart: 12, of which 4 were waited for; matrix products, arithmetic and copies ran while one was open for 0% of the time, Pallas kernels for 33%

profile of v5, /device:TPU:1, one launch (start us, length us, event | category | flops | bytes accessed | tf_op | source)
XLA Modules:
  0.0 71.9 jit_solution(2967177333229664110)
XLA Ops:
  0.6 1.2 %send_part.1 = (bf16[2,512,256]{2,1,0:T(8,128)(2,1)S(1)}, bf16[2,512,256]{2,1,0:T(8,128)(2,1)S(1)}) custom-call(bf16[4,512,256]{2,1,0:T(8,128)(2,1)} %feat_ref.3), custom_call_target="tpu_custom_call" | custom-call | bytes 1000000 | tf_op jit(solution)/shard_map/send_part/pallas_call | solution.py:75
  1.9 1.5 %collective-permute-start = (bf16[2,512,256]{2,1,0:T(8,128)(2,1)S(1)}, bf16[2,512,256]{2,1,0:T(8,128)(2,1)S(1)}, u32[]{:S(2)}, u32[]{:S(2)}) collective-permute-start(bf16[2,512,256]{2,1,0:T(8,128)(2,1)S(1)} %get-tuple-element.34), channel_id=1, source_target_pairs={{0,8},{8,0},{1,9},{9,1},{2,10},{10,2},{3,11},{11,3},{4,12},{12,4},... | collective-permute-start | bytes 1572872 | tf_op jit(solution)/shard_map/ppermute | solution.py:527
  3.4 3.5 %collective-permute-start.1 = (bf16[2,512,256]{2,1,0:T(8,128)(2,1)S(1)}, bf16[2,512,256]{2,1,0:T(8,128)(2,1)S(1)}, u32[]{:S(2)}, u32[]{:S(2)}) collective-permute-start(bf16[2,512,256]{2,1,0:T(8,128)(2,1)S(1)} %get-tuple-element.35._), channel_id=1, source_target_pairs={{8,16},{24,32},{40,48},{56,64},{72,80},{88,96},{104,112},{16,8},{3... | collective-permute-start | bytes 1572872 | tf_op jit(solution)/shard_map/ppermute | solution.py:528
  6.9 1.7 %own_part.1 = (bf16[4,16,256]{2,1,0:T(8,128)(2,1)S(1)}, bf16[4,16,256]{2,1,0:T(8,128)(2,1)S(1)}, bf16[4,16,128]{2,1,0:T(8,128)(2,1)S(1)}, bf16[2,256,1024]{2,1,0...) custom-call(s32[4]{0:T(128)} %lo_ref.1, s32[4]{0:T(128)} %hi_ref.1, ...), custom_call_target="tpu_custom_call" | custom-call | flops 4000000000 | bytes 4000000 | tf_op jit(solution)/shard_map/own_part/pallas_call | solution.py:122
  8.6 1.3 %collective-permute-start.2 = (bf16[4,16,256]{2,1,0:T(8,128)(2,1)S(1)}, bf16[4,16,256]{2,1,0:T(8,128)(2,1)S(1)}, u32[]{:S(2)}, u32[]{:S(2)}) collective-permute-start(bf16[4,16,256]{2,1,0:T(8,128)(2,1)S(1)} %get-tuple-element.49), channel_id=1, source_target_pairs={{0,1},{1,2},{2,3},{3,4},{4,5},{5,6},{6,7},{7,0},{8,9},{9,10},{10,1... | collective-permute-start | bytes 98312 | tf_op jit(solution)/shard_map/ppermute | solution.py:511
  9.9 4.0 %collective-permute-start.3 = (bf16[4,16,256]{2,1,0:T(8,128)(2,1)S(1)}, bf16[4,16,256]{2,1,0:T(8,128)(2,1)S(1)}, u32[]{:S(2)}, u32[]{:S(2)}) collective-permute-start(bf16[4,16,256]{2,1,0:T(8,128)(2,1)S(1)} %get-tuple-element.50), channel_id=1, source_target_pairs={{0,7},{1,0},{2,1},{3,2},{4,3},{5,4},{6,5},{7,6},{8,15},{9,8},{10,9... | collective-permute-start | bytes 98312 | tf_op jit(solution)/shard_map/ppermute | solution.py:511
  13.9 2.8 %filter_part.2 = (f32[256,2304]{1,0:T(8,128)S(1)}, bf16[1088,2304]{1,0:T(8,128)(2,1)S(1)}, bf16[2304,256]{1,0:T(8,128)(2,1)S(1)}) custom-call(bf16[2,512,256]{2,1,0:T(8,128)(2,1)S(1)} %collective-permute-done.halo_ref, bf16[4,528,256]{2,1,0:T(8,128)(2,1)S(1)} %get-tuple-element.36.extended_ref, bf16[4,288,240]{2,1,0:T(8,128)(2,1)S(1)} %get-tuple-element.37.bands_ref, ...), custom_call_target="tpu_custom_call" | custom-call | flops 100000000 | bytes 100000 | tf_op jit(solution)/shard_map/filter_part/pallas_call | solution.py:209
  16.7 1.6 %mixed_part.2 = (bf16[2,512,256]{2,1,0:T(8,128)(2,1)S(1)}, f32[2,32,256]{2,1,0:T(8,128)S(1)}, f32[2,16,256]{2,1,0:T(8,128)S(1)}, f32[2,16,256]{2,1,0:T(8,128)S(1)}) custom-call(bf16[1088,2304]{1,0:T(8,128)(2,1)S(1)} %get-tuple-element.39.filtered_ref.near_ref, bf16[2304,256]{1,0:T(8,128)(2,1)S(1)} %get-tuple-element.40.weight_ref), custom_call_target="tpu_custom_call" | custom-call | flops 100000000 | bytes 100000 | tf_op jit(solution)/shard_map/mixed_part/pallas_call | solution.py:317
  18.3 2.9 %filter_part.3 = (f32[256,2304]{1,0:T(8,128)S(1)}, bf16[1088,2304]{1,0:T(8,128)(2,1)S(1)}, bf16[2,560,256]{2,1,0:T(8,128)(2,1)S(1)}, bf16[2,560,256]{2,1,0:T(8,128)(2,1)S(1)}) custom-call(bf16[2,512,256]{2,1,0:T(8,128)(2,1)S(1)} %collective-permute-done.1.halo_ref, bf16[4,528,256]{2,1,0:T(8,128)(2,1)S(1)} %get-tuple-element.36.extended_ref, ...), custom_call_target="tpu_custom_call" | custom-call | flops 100000000 | bytes 100000 | tf_op jit(solution)/shard_map/filter_part/pallas_call | solution.py:209
  21.2 0.6 edge_part.1
  21.9 1.6 %mixed_part.3 = (bf16[2,512,256]{2,1,0:T(8,128)(2,1)S(1)}, f32[2,32,256]{2,1,0:T(8,128)S(1)}, f32[4,16,256]{2,1,0:T(8,128)S(1)}, f32[4,16,256]{2,1,0:T(8,128)S(1)}) custom-call(bf16[1088,2304]{1,0:T(8,128)(2,1)S(1)} %get-tuple-element.45.filtered_ref.far_ref, bf16[2304,256]{1,0:T(8,128)(2,1)S(1)} %get-tuple-element.40.weight_ref, ...), custom_call_target="tpu_custom_call" | custom-call | flops 100000000 | bytes 100000 | tf_op jit(solution)/shard_map/mixed_part/pallas_call | solution.py:317
  24.0 0.9 %half_part.1.__1_ = bf16[20,128,128]{2,1,0:T(8,128)(2,1)} custom-call(f32[20,128,128]{2,1,0:T(8,128)S(1)} %get-tuple-element.54.own_ref, bf16[20,128,128]{2,1,0:T(8,128)(2,1)S(1)} %collective-permute-done.4.other_ref, f32[2,32,256]{2,1,0:T(8,128)S(1)} %get-tuple-element.47._.far_ends_ref), custom_call_target="tpu_custom_call" | custom-call | flops 1000000 | bytes 3000000 | tf_op jit(solution)/shard_map/half_part/pallas_call | solution.py:286
  24.9 9.0 %all-to-all-start = ((bf16[64,40,128]{2,1,0:T(8,128)(2,1)}), bf16[64,40,128]{2,1,0:T(8,128)(2,1)S(1)}, u32[]{:S(2)}, u32[]{:S(2)}) async-start(bf16[64,40,128]{2,1,0:T(8,128)(2,1)} %bitcast.2), calls=%async_computation | async-start | bytes 1310720 | tf_op jit(solution)/shard_map/all_to_all | solution.py:541
  34.4 3.1 %collective-permute-start.8 = (bf16[2,560,256]{2,1,0:T(8,128)(2,1)S(1)}, bf16[2,560,256]{2,1,0:T(8,128)(2,1)}, u32[]{:S(2)}, u32[]{:S(2)}) collective-permute-start(bf16[2,560,256]{2,1,0:T(8,128)(2,1)S(1)} %ordered.8), channel_id=1, source_target_pairs={{8,16},{24,32},{40,48},{56,64},{72,80},{88,96},{104,112},{16,8},{3... | collective-permute-start | bytes 1720328 | tf_op jit(solution)/shard_map/ppermute | solution.py:542
  37.5 1.3 %collective-permute-start.5 = (f32[4,16,256]{2,1,0:T(8,128)S(1)}, f32[4,16,256]{2,1,0:T(8,128)S(1)}, u32[]{:S(2)}, u32[]{:S(2)}) collective-permute-start(f32[4,16,256]{2,1,0:T(8,128)S(1)} %ordered.5), channel_id=1, source_target_pairs={{0,1},{1,2},{2,3},{3,4},{4,5},{5,6},{6,7},{7,0},{8,9},{9,10},{10,1... | collective-permute-start | bytes 196616 | tf_op jit(solution)/shard_map/ppermute | solution.py:511
  38.8 3.9 %collective-permute-start.6 = (f32[4,16,256]{2,1,0:T(8,128)S(1)}, f32[4,16,256]{2,1,0:T(8,128)S(1)}, u32[]{:S(2)}, u32[]{:S(2)}) collective-permute-start(f32[4,16,256]{2,1,0:T(8,128)S(1)} %ordered.6), channel_id=1, source_target_pairs={{0,7},{1,0},{2,1},{3,2},{4,3},{5,4},{6,5},{7,6},{8,15},{9,8},{10,9... | collective-permute-start | bytes 196616 | tf_op jit(solution)/shard_map/ppermute | solution.py:511
  42.7 4.2 %all-to-all-done.pieces_ref = bf16[64,40,128]{2,1,0:T(8,128)(2,1)S(1)} async-done(((bf16[64,40,128]{2,1,0:T(8,128)(2,1)}), bf16[64,40,128]{2,1,0:T(8,128)(2,1)S(1)}, u32[]{:S(2)}, u32[]{:S(2)}) %all-to-all-start) | async-done | bytes 655392 | tf_op jit(solution)/shard_map/all_to_all | solution.py:541
  46.8 1.0 %sum_part.1._ = bf16[64,40,128]{2,1,0:T(8,128)(2,1)} custom-call(bf16[64,40,128]{2,1,0:T(8,128)(2,1)S(1)} %all-to-all-done.pieces_ref), custom_call_target="tpu_custom_call" | custom-call | flops 1000000 | bytes 2000000 | tf_op jit(solution)/shard_map/sum_part/pallas_call | solution.py:371
  47.8 5.8 %all-to-all-start.1 = ((bf16[64,40,128]{2,1,0:T(8,128)(2,1)}), bf16[64,40,128]{2,1,0:T(8,128)(2,1)S(1)}, u32[]{:S(2)}, u32[]{:S(2)}) async-start(bf16[64,40,128]{2,1,0:T(8,128)(2,1)} %sum_part.1._), calls=%async_computation.1 | async-start | bytes 1310720 | tf_op jit(solution)/shard_map/all_to_all | solution.py:548
  53.7 1.0 %ends_part.1 = (bf16[4,512,256]{2,1,0:T(8,128)(2,1)}, f32[8,128]{1,0:T(8,128)S(1)}) custom-call(f32[2,32,256]{2,1,0:T(8,128)S(1)} %get-tuple-element.41.near_ends_ref, f32[2,32,256]{2,1,0:T(8,128)S(1)} %get-tuple-element.47._.far_ends_ref, f32[4,16,256]{2,1,0:T(8,128)S(1)} %collective-permute-done.5.left_ref, ...), custom_call_target="tpu_custom_call" | custom-call | flops 1000000 | bytes 1000000 | tf_op jit(solution)/shard_map/ends_part/pallas_call | solution.py:353
  54.7 9.7 %grad_input_part.1 = (bf16[4,512,256]{2,1,0:T(8,128)(2,1)}, f32[8,128]{1,0:T(8,128)S(1)}) custom-call(bf16[4,16,128]{2,1,0:T(8,128)(2,1)S(1)} %get-tuple-element.43.refs_2_.kept_ref, bf16[2,560,256]{2,1,0:T(8,128)(2,1)} %collective-permute-done.7.chip_ref, bf16[2,560,256]{2,1,0:T(8,128)(2,1)} %collective-permute-done.8.link_ref, ...), custom_call_target="tpu_custom_call" | custom-call | flops 8000000000 | bytes 5000000 | tf_op jit(solution)/shard_map/grad_input_part/pallas_call | solution.py:487
  64.8 4.1 %collective-permute-start.9 = (bf16[20,128,128]{2,1,0:T(8,128)(2,1)S(1)}, bf16[20,128,128]{2,1,0:T(8,128)(2,1)S(1)}, u32[]{:S(2)}, u32[]{:S(2)}) collective-permute-start(bf16[20,128,128]{2,1,0:T(8,128)(2,1)S(1)} %ordered.9.half_ref), channel_id=1, source_target_pairs={{0,8},{8,0},{1,9},{9,1},{2,10},{10,2},{3,11},{11,3},{4,12},{12,4},... | collective-permute-start | bytes 1966088 | tf_op jit(solution)/shard_map/ppermute | solution.py:554
  68.9 1.2 %result_part.2.refs_0_ = f32[9,256,256]{2,1,0:T(8,128)} custom-call(bf16[20,128,128]{2,1,0:T(8,128)(2,1)S(1)} %ordered.9.half_ref), custom_call_target="tpu_custom_call" | custom-call | flops 1000000 | bytes 4000000 | tf_op jit(solution)/shard_map/result_part/pallas_call | solution.py:414
  70.6 1.2 %result_part.3 = f32[9,256,256]{2,1,0:T(8,128)} custom-call(bf16[20,128,128]{2,1,0:T(8,128)(2,1)S(1)} %collective-permute-done.9.half_ref, f32[9,256,256]{2,1,0:T(8,128)} %result_part.2.refs_0_), custom_call_target="tpu_custom_call", output_to_operand_aliasing={{}: (1, {})} | custom-call | flops 1000000 | bytes 4000000 | tf_op jit(solution)/shard_map/result_part/pallas_call | solution.py:414
  (18 shorter events, 2.0 us)
Async XLA Ops:
  1.9 12.0 %collective-permute-start = (bf16[2,512,256]{2,1,0:T(8,128)(2,1)S(1)}, bf16[2,512,256]{2,1,0:T(8,128)(2,1)S(1)}, u32[]{:S(2)}, u32[]{:S(2)}) collective-permute-start(bf16[2,512,256]{2,1,0:T(8,128)(2,1)S(1)} %get-tuple-element.34), channel_id=1, source_target_pairs={{0,8},{8,0},{1,9},{9,1},{2,10},{10,2},{3,11},{11,3},{4,12},{12,4},... | collective-permute-start | bytes 1572872 | tf_op jit(solution)/shard_map/ppermute | solution.py:527
  3.4 14.9 %collective-permute-start.1 = (bf16[2,512,256]{2,1,0:T(8,128)(2,1)S(1)}, bf16[2,512,256]{2,1,0:T(8,128)(2,1)S(1)}, u32[]{:S(2)}, u32[]{:S(2)}) collective-permute-start(bf16[2,512,256]{2,1,0:T(8,128)(2,1)S(1)} %get-tuple-element.35._), channel_id=1, source_target_pairs={{8,16},{24,32},{40,48},{56,64},{72,80},{88,96},{104,112},{16,8},{3... | collective-permute-start | bytes 1572872 | tf_op jit(solution)/shard_map/ppermute | solution.py:528
  8.6 12.5 %collective-permute-start.2 = (bf16[4,16,256]{2,1,0:T(8,128)(2,1)S(1)}, bf16[4,16,256]{2,1,0:T(8,128)(2,1)S(1)}, u32[]{:S(2)}, u32[]{:S(2)}) collective-permute-start(bf16[4,16,256]{2,1,0:T(8,128)(2,1)S(1)} %get-tuple-element.49), channel_id=1, source_target_pairs={{0,1},{1,2},{2,3},{3,4},{4,5},{5,6},{6,7},{7,0},{8,9},{9,10},{10,1... | collective-permute-start | bytes 98312 | tf_op jit(solution)/shard_map/ppermute | solution.py:511
  9.9 11.3 %collective-permute-start.3 = (bf16[4,16,256]{2,1,0:T(8,128)(2,1)S(1)}, bf16[4,16,256]{2,1,0:T(8,128)(2,1)S(1)}, u32[]{:S(2)}, u32[]{:S(2)}) collective-permute-start(bf16[4,16,256]{2,1,0:T(8,128)(2,1)S(1)} %get-tuple-element.50), channel_id=1, source_target_pairs={{0,7},{1,0},{2,1},{3,2},{4,3},{5,4},{6,5},{7,6},{8,15},{9,8},{10,9... | collective-permute-start | bytes 98312 | tf_op jit(solution)/shard_map/ppermute | solution.py:511
  21.8 2.2 %collective-permute-start.4 = (bf16[20,128,128]{2,1,0:T(8,128)(2,1)S(1)}, bf16[20,128,128]{2,1,0:T(8,128)(2,1)S(1)}, u32[]{:S(2)}, u32[]{:S(2)}) collective-permute-start(bf16[20,128,128]{2,1,0:T(8,128)(2,1)S(1)} %get-tuple-element.55), channel_id=1, source_target_pairs={{0,8},{8,0},{1,9},{9,1},{2,10},{10,2},{3,11},{11,3},{4,12},{12,4},... | collective-permute-start | bytes 1966088 | tf_op jit(solution)/shard_map/ppermute | solution.py:538
  24.9 22.0 %all-to-all-start = ((bf16[64,40,128]{2,1,0:T(8,128)(2,1)}), bf16[64,40,128]{2,1,0:T(8,128)(2,1)S(1)}, u32[]{:S(2)}, u32[]{:S(2)}) async-start(bf16[64,40,128]{2,1,0:T(8,128)(2,1)} %bitcast.2), calls=%async_computation | async-start | bytes 1310720 | tf_op jit(solution)/shard_map/all_to_all | solution.py:541
  33.9 20.8 %collective-permute-start.7 = (bf16[2,560,256]{2,1,0:T(8,128)(2,1)S(1)}, bf16[2,560,256]{2,1,0:T(8,128)(2,1)}, u32[]{:S(2)}, u32[]{:S(2)}) collective-permute-start(bf16[2,560,256]{2,1,0:T(8,128)(2,1)S(1)} %ordered.7), channel_id=1, source_target_pairs={{0,8},{8,0},{1,9},{9,1},{2,10},{10,2},{3,11},{11,3},{4,12},{12,4},... | collective-permute-start | bytes 1720328 | tf_op jit(solution)/shard_map/ppermute | solution.py:543
  34.4 20.3 %collective-permute-start.8 = (bf16[2,560,256]{2,1,0:T(8,128)(2,1)S(1)}, bf16[2,560,256]{2,1,0:T(8,128)(2,1)}, u32[]{:S(2)}, u32[]{:S(2)}) collective-permute-start(bf16[2,560,256]{2,1,0:T(8,128)(2,1)S(1)} %ordered.8), channel_id=1, source_target_pairs={{8,16},{24,32},{40,48},{56,64},{72,80},{88,96},{104,112},{16,8},{3... | collective-permute-start | bytes 1720328 | tf_op jit(solution)/shard_map/ppermute | solution.py:542
  37.5 16.1 %collective-permute-start.5 = (f32[4,16,256]{2,1,0:T(8,128)S(1)}, f32[4,16,256]{2,1,0:T(8,128)S(1)}, u32[]{:S(2)}, u32[]{:S(2)}) collective-permute-start(f32[4,16,256]{2,1,0:T(8,128)S(1)} %ordered.5), channel_id=1, source_target_pairs={{0,1},{1,2},{2,3},{3,4},{4,5},{5,6},{6,7},{7,0},{8,9},{9,10},{10,1... | collective-permute-start | bytes 196616 | tf_op jit(solution)/shard_map/ppermute | solution.py:511
  38.8 14.9 %collective-permute-start.6 = (f32[4,16,256]{2,1,0:T(8,128)S(1)}, f32[4,16,256]{2,1,0:T(8,128)S(1)}, u32[]{:S(2)}, u32[]{:S(2)}) collective-permute-start(f32[4,16,256]{2,1,0:T(8,128)S(1)} %ordered.6), channel_id=1, source_target_pairs={{0,7},{1,0},{2,1},{3,2},{4,3},{5,4},{6,5},{7,6},{8,15},{9,8},{10,9... | collective-permute-start | bytes 196616 | tf_op jit(solution)/shard_map/ppermute | solution.py:511
  47.8 17.0 %all-to-all-start.1 = ((bf16[64,40,128]{2,1,0:T(8,128)(2,1)}), bf16[64,40,128]{2,1,0:T(8,128)(2,1)S(1)}, u32[]{:S(2)}, u32[]{:S(2)}) async-start(bf16[64,40,128]{2,1,0:T(8,128)(2,1)} %sum_part.1._), calls=%async_computation.1 | async-start | bytes 1310720 | tf_op jit(solution)/shard_map/all_to_all | solution.py:548
  64.8 5.8 %collective-permute-start.9 = (bf16[20,128,128]{2,1,0:T(8,128)(2,1)S(1)}, bf16[20,128,128]{2,1,0:T(8,128)(2,1)S(1)}, u32[]{:S(2)}, u32[]{:S(2)}) collective-permute-start(bf16[20,128,128]{2,1,0:T(8,128)(2,1)S(1)} %ordered.9.half_ref), channel_id=1, source_target_pairs={{0,8},{8,0},{1,9},{9,1},{2,10},{10,2},{3,11},{11,3},{4,12},{12,4},... | collective-permute-start | bytes 1966088 | tf_op jit(solution)/shard_map/ppermute | solution.py:554

commit v6 on v5

--- a/solution.py
+++ b/solution.py
@@ -32,7 +32,6 @@
 F32 = jnp.float32
 
 IN_VMEM = pl.BlockSpec(memory_space=pltpu.VMEM)
-IN_SMEM = pl.BlockSpec(memory_space=pltpu.SMEM)
 IN_HBM = pl.BlockSpec(memory_space=pltpu.HBM)
 ANYWHERE = pl.BlockSpec(memory_space=pl.ANY)
 
@@ -84,13 +83,12 @@
     )(in_hbm(features))
 
 
-def own_kernel(lo_ref, hi_ref, basis_ref, cot_ref, feat_ref, _, to_right_ref, to_left_ref, kept_ref, turned_ref, extended_ref, bands_ref, lo, hi, basis, cot, feat, sems):
+def own_kernel(lo_ref, hi_ref, basis_ref, cot_ref, _, to_right_ref, to_left_ref, kept_ref, cot, bands_ref, lo, hi, basis, sems):
     copies = (
         (lo_ref, lo),
         (hi_ref, hi),
         (basis_ref, basis),
         (cot_ref, cot),
-        (feat_ref, feat),
     )
     copies = [pltpu.make_async_copy(a, b, sems.at[n]) for n, (a, b) in enumerate(copies)]
     for copy in copies:
@@ -106,18 +104,13 @@
         line = jnp.dot(cells, place, preferred_element_type=F32)
         for k in range(K):
             bands_ref[i, k * J : (k + 1) * J, :] = banded(line[k : k + 1, :])[:, :DEPTH]
-    copies[3].wait()
+    for copy in copies[3:]:
+        copy.wait()
     to_right_ref[...] = cot[:, NJ - EDGE :, :]
     to_left_ref[...] = cot[:, :EDGE, :]
-    for pair in range(2):
-        turned_ref[pair] = cot[2 * pair : 2 * pair + 2].reshape(2 * NJ, C).T
-    copies[4].wait()
-    gap = jnp.zeros((8, C), BF)
-    for i in range(ROWS):
-        extended_ref[i] = jnp.concatenate([gap, feat[i], gap], axis=0)
-
-
-def own_part(span_lo, span_hi, basis, cotangent, features, after):
+
+
+def own_part(span_lo, span_hi, basis, cotangent, after):
     basis = jnp.transpose(basis, (1, 0, 2))
     return pl.pallas_call(
         own_kernel,
@@ -125,24 +118,21 @@
             pltpu.VMEM((ROWS, EDGE, C), BF),
             pltpu.VMEM((ROWS, EDGE, C), BF),
             pltpu.VMEM((ROWS, 16, LANES), BF),
-            pltpu.VMEM((2, C, 2 * NJ), BF),
-            pltpu.VMEM((ROWS, EXT, C), BF),
+            pltpu.VMEM((ROWS, NJ, C), BF),
             pltpu.VMEM((ROWS, K * J, DEPTH), BF),
         ),
-        in_specs=[IN_HBM] * 5 + [ANYWHERE],
-        out_specs=[IN_VMEM] * 6,
+        in_specs=[IN_HBM] * 4 + [ANYWHERE],
+        out_specs=[IN_VMEM] * 5,
         scratch_shapes=[
             pltpu.SMEM((ROWS,), jnp.int32),
             pltpu.SMEM((ROWS,), jnp.int32),
             pltpu.VMEM(basis.shape, F32),
-            pltpu.VMEM((ROWS, NJ, C), BF),
-            pltpu.VMEM((ROWS, NJ, C), BF),
-            pltpu.SemaphoreType.DMA((5,)),
+            pltpu.SemaphoreType.DMA((4,)),
         ],
         compiler_params=params(6),
         cost_estimate=cost(4e9, 4e6),
         name="own_part",
-    )(*map(in_hbm, (span_lo, span_hi, basis, cotangent, features)), after)
+    )(*map(in_hbm, (span_lo, span_hi, basis, cotangent)), after)
 
 
 def row_pair(side):
@@ -150,13 +140,13 @@
     return core if side == 0 else 1 - core
 
 
-def filter_kernel(side, halo_ref, extended_ref, bands_ref, *refs):
+def filter_kernel(side, halo_ref, sent_chip_ref, sent_link_ref, bands_ref, near_cot_ref, *refs):
     copies = []
     if side == 0:
-        turned_ref, weight_hbm, total_ref, filtered, weight_ref, rows, sem = refs
+        weight_hbm, total_ref, filtered, weight_ref, rows, turned, sem = refs
         copies.append(pltpu.make_async_copy(weight_hbm, weight_ref, sem))
     else:
-        turned_ref, before_ref, kept_ref, _, cot_ref, total_ref, filtered, chip_cot_ref, link_cot_ref, rows, kept, sems = refs
+        before_ref, kept_ref, _, cot_ref, total_ref, filtered, chip_cot_ref, link_cot_ref, rows, turned, kept, sems = refs
         core = lax.axis_index("core")
         for n, (ref, first) in enumerate(((chip_cot_ref, 2 - 2 * core), (link_cot_ref, 2 * core))):
             kept[n] = jnp.zeros((2, 16, C), BF)
@@ -171,8 +161,11 @@
     gap = jnp.zeros((8, C), BF)
     for n in range(2):
         rows[4 - 4 * pair + n] = jnp.concatenate([gap, halo_ref[n], gap], axis=0)
-    for n in range(ROWS):
-        rows[2 * pair + n] = extended_ref[n]
+    own_core = lax.axis_index("core")
+    for n in range(2):
+        rows[2 * pair + 2 * own_core + n] = jnp.concatenate([gap, sent_link_ref[n], gap], axis=0)
+        rows[2 * pair + 2 - 2 * own_core + n] = jnp.concatenate([gap, sent_chip_ref[n], gap], axis=0)
+    turned[...] = near_cot_ref[pl.ds(2 - 2 * pair, 2)].reshape(2 * NJ, C).T
     middle = jnp.zeros((EXT_WINDOW - 16, C), BF)
     for row in range(2):
         bands = bands_ref[2 - 2 * pair + row]
@@ -191,7 +184,7 @@
                 filtered[first : first + J, k * C : (k + 1) * C] = found[k * J : (k + 1) * J]
     for k in range(K):
         columns = slice(k * C, (k + 1) * C)
-        part = jnp.dot(turned_ref[1 - pair], filtered[0 : 2 * NJ, columns], preferred_element_type=F32)
+        part = jnp.dot(turned[...], filtered[0 : 2 * NJ, columns], preferred_element_type=F32)
         total_ref[:, columns] = part if side == 0 else before_ref[:, columns] + part
     for copy in copies:
         copy.wait()
@@ -199,7 +192,7 @@
 
 def filter_part(side, *operands):
     outs = [pltpu.VMEM((C, K * C), F32), pltpu.VMEM((2 * (NJ + J), K * C), BF)]
-    scratch = [pltpu.VMEM((6, EXT, C), BF)]
+    scratch = [pltpu.VMEM((6, EXT, C), BF), pltpu.VMEM((C, 2 * NJ), BF)]
     if side == 0:
         outs += [pltpu.VMEM((K * C, C), BF)]
         scratch += [pltpu.SemaphoreType.DMA(())]
@@ -519,19 +512,19 @@
 
     pairs = [(i, i + 1) for i in range(1, lats - 1, 2)]
     pairs = pairs + [(b, a) for a, b in pairs]
-    chip, link = send_part(features)
+    sent_chip, sent_link = send_part(features)
     weight = weight.reshape(K * C, C)
-    to_right, to_left, kept, turned, extended, bands = own_part(
-        span_lo, span_hi, basis, cotangent, features, link
+    to_right, to_left, kept, near_cot, bands = own_part(
+        span_lo, span_hi, basis, cotangent, sent_link
     )
-    chip = lax.ppermute(chip, "core", swap)
-    link = lax.ppermute(link, lat, pairs)
+    chip = lax.ppermute(sent_chip, "core", swap)
+    link = lax.ppermute(sent_link, lat, pairs)
     near_left = shifted(to_right, "lon", lons, 1, True)
     near_right = shifted(to_left, "lon", lons, -1, True)
-    total, near, weight_near = filter_part(0, chip, extended, bands, turned, weight)
+    total, near, weight_near = filter_part(0, chip, sent_chip, sent_link, bands, near_cot, weight)
     near_mixed, near_ends, to_right, to_left = mixed_part(0, near, weight_near)
     total, far, chip_cot, link_cot = filter_part(
-        1, link, extended, bands, turned, total, kept, to_right, cotangent
+        1, link, sent_chip, sent_link, bands, near_cot, total, kept, to_right, cotangent
     )
     own, other, chip_cot, link_cot = edge_part(near_left, near_right, total, near, far, chip_cot, link_cot)
 

time: 72.3 us -> 72.5 us (level)
  transfers between devices with their start and end apart: 12 -> 12, of which waited for: 4 -> 4; matrix products, arithmetic and copies ran while one was open for 0% -> 0% of each run, Pallas kernels for 33% -> 32%
where the time goes in v6:
time: 72.5 us; the launch traced here: 72.1 us
  starting transfers between devices  38.6 us (53%)
  Pallas kernels  26.9 us (37%)
  waiting for transfers between devices  5.61 us (8%)
  between operations  1.01 us (1%)
    ppermute x4, starting transfers between devices, shifted(): return lax.ppermute(block, axis, route)  10.4 us
    pallas_call x1, Pallas kernels, grad_part(): pl.pallas_call(grad_kernel, out_shape=(jax.ShapeDtypeStruct((ROWS, NJ, C)...  9.69 us
    all_to_all x1, starting transfers between devices, per_device(): pieces = lax.all_to_all(half.reshape(parts, -1, LANES), chips, 0, 0)  9.43 us
    all_to_all x1, starting transfers between devices, per_device(): lax.all_to_all(copies, chips, 0, 0).reshape(PADDED_BLOCKS, LANES, LANES)  6.02 us
    pallas_call x2, Pallas kernels, filter_part(): pl.pallas_call(functools.partial(filter_kernel, side), out_shape=tuple(ou...  5.64 us
    all_to_all x1, waiting for transfers between devices, per_device(): pieces = lax.all_to_all(half.reshape(parts, -1, LANES), chips, 0, 0)  4.17 us
    ppermute x1, starting transfers between devices, per_device(): other = lax.ppermute(gathered, 'core', swap)  4.06 us
    ppermute x1, starting transfers between devices, per_device(): link = lax.ppermute(sent_link, lat, pairs)  3.53 us
  transfers between devices with their start and end apart: 12, of which 4 were waited for; matrix products, arithmetic and copies ran while one was open for 0% of the time, Pallas kernels for 32%

profile of v6, /device:TPU:1, one launch (start us, length us, event | category | flops | bytes accessed | tf_op | source)
XLA Modules:
  0.0 72.1 jit_solution(430023345988891244)
XLA Ops:
  0.6 1.2 %send_part.1 = (bf16[2,512,256]{2,1,0:T(8,128)(2,1)S(1)}, bf16[2,512,256]{2,1,0:T(8,128)(2,1)S(1)}) custom-call(bf16[4,512,256]{2,1,0:T(8,128)(2,1)} %feat_ref.1), custom_call_target="tpu_custom_call" | custom-call | bytes 1000000 | tf_op jit(solution)/shard_map/send_part/pallas_call | solution.py:74
  1.9 1.5 %collective-permute-start = (bf16[2,512,256]{2,1,0:T(8,128)(2,1)S(1)}, bf16[2,512,256]{2,1,0:T(8,128)(2,1)S(1)}, u32[]{:S(2)}, u32[]{:S(2)}) collective-permute-start(bf16[2,512,256]{2,1,0:T(8,128)(2,1)S(1)} %get-tuple-element.33.sent_chip_ref), channel_id=1, source_target_pairs={{0,8},{8,0},{1,9},{9,1},{2,10},{10,2},{3,11},{11,3},{4,12},{12,4},... | collective-permute-start | bytes 1572872 | tf_op jit(solution)/shard_map/ppermute | solution.py:520
  3.4 3.5 %collective-permute-start.1 = (bf16[2,512,256]{2,1,0:T(8,128)(2,1)S(1)}, bf16[2,512,256]{2,1,0:T(8,128)(2,1)S(1)}, u32[]{:S(2)}, u32[]{:S(2)}) collective-permute-start(bf16[2,512,256]{2,1,0:T(8,128)(2,1)S(1)} %get-tuple-element.34._.sent_link_ref), channel_id=1, source_target_pairs={{8,16},{24,32},{40,48},{56,64},{72,80},{88,96},{104,112},{16,8},{3... | collective-permute-start | bytes 1572872 | tf_op jit(solution)/shard_map/ppermute | solution.py:521
  6.9 1.3 %own_part.1 = (bf16[4,16,256]{2,1,0:T(8,128)(2,1)S(1)}, bf16[4,16,256]{2,1,0:T(8,128)(2,1)S(1)}, bf16[4,16,128]{2,1,0:T(8,128)(2,1)S(1)}, bf16[4,512,256]{2,1,0:T(8,128)(2,1)S(1)}, bf16[4,288,240]{2,1,0:T(8,128)(2,1)S(1)}) custom-call(s32[4]{0:T(128)} %lo_ref.1, s32[4]{0:T(128)} %hi_ref.1, f32[9,4,25]{2,1,0:T(4,128)} %bitcast.7, ...), custom_call_target="tpu_custom_call" | custom-call | flops 4000000000 | bytes 4000000 | tf_op jit(solution)/shard_map/own_part/pallas_call | solution.py:115
  8.2 1.3 %collective-permute-start.2 = (bf16[4,16,256]{2,1,0:T(8,128)(2,1)S(1)}, bf16[4,16,256]{2,1,0:T(8,128)(2,1)S(1)}, u32[]{:S(2)}, u32[]{:S(2)}) collective-permute-start(bf16[4,16,256]{2,1,0:T(8,128)(2,1)S(1)} %get-tuple-element.47), channel_id=1, source_target_pairs={{0,1},{1,2},{2,3},{3,4},{4,5},{5,6},{6,7},{7,0},{8,9},{9,10},{10,1... | collective-permute-start | bytes 98312 | tf_op jit(solution)/shard_map/ppermute | solution.py:504
  9.5 4.0 %collective-permute-start.3 = (bf16[4,16,256]{2,1,0:T(8,128)(2,1)S(1)}, bf16[4,16,256]{2,1,0:T(8,128)(2,1)S(1)}, u32[]{:S(2)}, u32[]{:S(2)}) collective-permute-start(bf16[4,16,256]{2,1,0:T(8,128)(2,1)S(1)} %get-tuple-element.48), channel_id=1, source_target_pairs={{0,7},{1,0},{2,1},{3,2},{4,3},{5,4},{6,5},{7,6},{8,15},{9,8},{10,9... | collective-permute-start | bytes 98312 | tf_op jit(solution)/shard_map/ppermute | solution.py:504
  13.5 2.8 %filter_part.2 = (f32[256,2304]{1,0:T(8,128)S(1)}, bf16[1088,2304]{1,0:T(8,128)(2,1)S(1)}, bf16[2304,256]{1,0:T(8,128)(2,1)S(1)}) custom-call(bf16[2,512,256]{2,1,0:T(8,128)(2,1)S(1)} %collective-permute-done.halo_ref, bf16[2,512,256]{2,1,0:T(8,128)(2,1)S(1)} %get-tuple-element.33.sent_chip_ref, bf16[2,512,256]{2,1,0:T(8,128)(2,1)S(1)} %get-tuple-element.34._.sent_link_ref, ...), custom_call_target="tpu_custom_call" | custom-call | flops 100000000 | bytes 100000 | tf_op jit(solution)/shard_map/filter_part/pallas_call | solution.py:202
  16.2 1.6 %mixed_part.2 = (bf16[2,512,256]{2,1,0:T(8,128)(2,1)S(1)}, f32[2,32,256]{2,1,0:T(8,128)S(1)}, f32[2,16,256]{2,1,0:T(8,128)S(1)}, f32[2,16,256]{2,1,0:T(8,128)S(1)}) custom-call(bf16[1088,2304]{1,0:T(8,128)(2,1)S(1)} %get-tuple-element.37.filtered_ref.near_ref, bf16[2304,256]{1,0:T(8,128)(2,1)S(1)} %get-tuple-element.38.weight_ref), custom_call_target="tpu_custom_call" | custom-call | flops 100000000 | bytes 100000 | tf_op jit(solution)/shard_map/mixed_part/pallas_call | solution.py:310
  17.8 2.9 %filter_part.3 = (f32[256,2304]{1,0:T(8,128)S(1)}, bf16[1088,2304]{1,0:T(8,128)(2,1)S(1)}, bf16[2,560,256]{2,1,0:T(8,128)(2,1)S(1)}, bf16[2,560,256]{2,1,0:T(8,128)(2,1)S(1)}) custom-call(bf16[2,512,256]{2,1,0:T(8,128)(2,1)S(1)} %collective-permute-done.1.halo_ref, bf16[2,512,256]{2,1,0:T(8,128)(2,1)S(1)} %get-tuple-element.33.sent_chip_ref, ...), custom_call_target="tpu_custom_call" | custom-call | flops 100000000 | bytes 100000 | tf_op jit(solution)/shard_map/filter_part/pallas_call | solution.py:202
  20.7 0.6 edge_part.1
  21.4 1.6 %mixed_part.3 = (bf16[2,512,256]{2,1,0:T(8,128)(2,1)S(1)}, f32[2,32,256]{2,1,0:T(8,128)S(1)}, f32[4,16,256]{2,1,0:T(8,128)S(1)}, f32[4,16,256]{2,1,0:T(8,128)S(1)}) custom-call(bf16[1088,2304]{1,0:T(8,128)(2,1)S(1)} %get-tuple-element.43.filtered_ref.far_ref, bf16[2304,256]{1,0:T(8,128)(2,1)S(1)} %get-tuple-element.38.weight_ref, ...), custom_call_target="tpu_custom_call" | custom-call | flops 100000000 | bytes 100000 | tf_op jit(solution)/shard_map/mixed_part/pallas_call | solution.py:310
  23.5 0.9 %half_part.1.__1_ = bf16[20,128,128]{2,1,0:T(8,128)(2,1)} custom-call(f32[20,128,128]{2,1,0:T(8,128)S(1)} %get-tuple-element.52.own_ref, bf16[20,128,128]{2,1,0:T(8,128)(2,1)S(1)} %collective-permute-done.4.other_ref, f32[2,32,256]{2,1,0:T(8,128)S(1)} %get-tuple-element.45._.far_ends_ref), custom_call_target="tpu_custom_call" | custom-call | flops 1000000 | bytes 3000000 | tf_op jit(solution)/shard_map/half_part/pallas_call | solution.py:279
  24.4 9.4 %all-to-all-start = ((bf16[64,40,128]{2,1,0:T(8,128)(2,1)}), bf16[64,40,128]{2,1,0:T(8,128)(2,1)S(1)}, u32[]{:S(2)}, u32[]{:S(2)}) async-start(bf16[64,40,128]{2,1,0:T(8,128)(2,1)} %bitcast.2), calls=%async_computation | async-start | bytes 1310720 | tf_op jit(solution)/shard_map/all_to_all | solution.py:534
  34.4 3.1 %collective-permute-start.8 = (bf16[2,560,256]{2,1,0:T(8,128)(2,1)S(1)}, bf16[2,560,256]{2,1,0:T(8,128)(2,1)}, u32[]{:S(2)}, u32[]{:S(2)}) collective-permute-start(bf16[2,560,256]{2,1,0:T(8,128)(2,1)S(1)} %ordered.8), channel_id=1, source_target_pairs={{8,16},{24,32},{40,48},{56,64},{72,80},{88,96},{104,112},{16,8},{3... | collective-permute-start | bytes 1720328 | tf_op jit(solution)/shard_map/ppermute | solution.py:535
  37.5 1.3 %collective-permute-start.5 = (f32[4,16,256]{2,1,0:T(8,128)S(1)}, f32[4,16,256]{2,1,0:T(8,128)S(1)}, u32[]{:S(2)}, u32[]{:S(2)}) collective-permute-start(f32[4,16,256]{2,1,0:T(8,128)S(1)} %ordered.5), channel_id=1, source_target_pairs={{0,1},{1,2},{2,3},{3,4},{4,5},{5,6},{6,7},{7,0},{8,9},{9,10},{10,1... | collective-permute-start | bytes 196616 | tf_op jit(solution)/shard_map/ppermute | solution.py:504
  38.8 3.9 %collective-permute-start.6 = (f32[4,16,256]{2,1,0:T(8,128)S(1)}, f32[4,16,256]{2,1,0:T(8,128)S(1)}, u32[]{:S(2)}, u32[]{:S(2)}) collective-permute-start(f32[4,16,256]{2,1,0:T(8,128)S(1)} %ordered.6), channel_id=1, source_target_pairs={{0,7},{1,0},{2,1},{3,2},{4,3},{5,4},{6,5},{7,6},{8,15},{9,8},{10,9... | collective-permute-start | bytes 196616 | tf_op jit(solution)/shard_map/ppermute | solution.py:504
  42.7 4.2 %all-to-all-done.pieces_ref = bf16[64,40,128]{2,1,0:T(8,128)(2,1)S(1)} async-done(((bf16[64,40,128]{2,1,0:T(8,128)(2,1)}), bf16[64,40,128]{2,1,0:T(8,128)(2,1)S(1)}, u32[]{:S(2)}, u32[]{:S(2)}) %all-to-all-start) | async-done | bytes 655392 | tf_op jit(solution)/shard_map/all_to_all | solution.py:534
  46.9 1.0 %sum_part.1._ = bf16[64,40,128]{2,1,0:T(8,128)(2,1)} custom-call(bf16[64,40,128]{2,1,0:T(8,128)(2,1)S(1)} %all-to-all-done.pieces_ref), custom_call_target="tpu_custom_call" | custom-call | flops 1000000 | bytes 2000000 | tf_op jit(solution)/shard_map/sum_part/pallas_call | solution.py:364
  47.8 6.0 %all-to-all-start.1 = ((bf16[64,40,128]{2,1,0:T(8,128)(2,1)}), bf16[64,40,128]{2,1,0:T(8,128)(2,1)S(1)}, u32[]{:S(2)}, u32[]{:S(2)}) async-start(bf16[64,40,128]{2,1,0:T(8,128)(2,1)} %sum_part.1._), calls=%async_computation.1 | async-start | bytes 1310720 | tf_op jit(solution)/shard_map/all_to_all | solution.py:541
  53.9 1.0 %ends_part.1 = (bf16[4,512,256]{2,1,0:T(8,128)(2,1)}, f32[8,128]{1,0:T(8,128)S(1)}) custom-call(f32[2,32,256]{2,1,0:T(8,128)S(1)} %get-tuple-element.39.near_ends_ref, f32[2,32,256]{2,1,0:T(8,128)S(1)} %get-tuple-element.45._.far_ends_ref, f32[4,16,256]{2,1,0:T(8,128)S(1)} %collective-permute-done.5.left_ref, ...), custom_call_target="tpu_custom_call" | custom-call | flops 1000000 | bytes 1000000 | tf_op jit(solution)/shard_map/ends_part/pallas_call | solution.py:346
  54.9 9.7 %grad_input_part.1 = (bf16[4,512,256]{2,1,0:T(8,128)(2,1)}, f32[8,128]{1,0:T(8,128)S(1)}) custom-call(bf16[4,16,128]{2,1,0:T(8,128)(2,1)S(1)} %get-tuple-element.41.refs_1_.kept_ref, bf16[2,560,256]{2,1,0:T(8,128)(2,1)} %collective-permute-done.7.chip_ref, bf16[2,560,256]{2,1,0:T(8,128)(2,1)} %collective-permute-done.8.link_ref, ...), custom_call_target="tpu_custom_call" | custom-call | flops 8000000000 | bytes 5000000 | tf_op jit(solution)/shard_map/grad_input_part/pallas_call | solution.py:480
  65.0 4.1 %collective-permute-start.9 = (bf16[20,128,128]{2,1,0:T(8,128)(2,1)S(1)}, bf16[20,128,128]{2,1,0:T(8,128)(2,1)S(1)}, u32[]{:S(2)}, u32[]{:S(2)}) collective-permute-start(bf16[20,128,128]{2,1,0:T(8,128)(2,1)S(1)} %ordered.9.half_ref), channel_id=1, source_target_pairs={{0,8},{8,0},{1,9},{9,1},{2,10},{10,2},{3,11},{11,3},{4,12},{12,4},... | collective-permute-start | bytes 1966088 | tf_op jit(solution)/shard_map/ppermute | solution.py:547
  69.0 1.2 %result_part.2.refs_0_ = f32[9,256,256]{2,1,0:T(8,128)} custom-call(bf16[20,128,128]{2,1,0:T(8,128)(2,1)S(1)} %ordered.9.half_ref), custom_call_target="tpu_custom_call" | custom-call | flops 1000000 | bytes 4000000 | tf_op jit(solution)/shard_map/result_part/pallas_call | solution.py:407
  70.8 1.2 %result_part.3 = f32[9,256,256]{2,1,0:T(8,128)} custom-call(bf16[20,128,128]{2,1,0:T(8,128)(2,1)S(1)} %collective-permute-done.9.half_ref, f32[9,256,256]{2,1,0:T(8,128)} %result_part.2.refs_0_), custom_call_target="tpu_custom_call", output_to_operand_aliasing={{}: (1, {})} | custom-call | flops 1000000 | bytes 4000000 | tf_op jit(solution)/shard_map/result_part/pallas_call | solution.py:407
  (18 shorter events, 2.0 us)
Async XLA Ops:
  1.9 11.6 %collective-permute-start = (bf16[2,512,256]{2,1,0:T(8,128)(2,1)S(1)}, bf16[2,512,256]{2,1,0:T(8,128)(2,1)S(1)}, u32[]{:S(2)}, u32[]{:S(2)}) collective-permute-start(bf16[2,512,256]{2,1,0:T(8,128)(2,1)S(1)} %get-tuple-element.33.sent_chip_ref), channel_id=1, source_target_pairs={{0,8},{8,0},{1,9},{9,1},{2,10},{10,2},{3,11},{11,3},{4,12},{12,4},... | collective-permute-start | bytes 1572872 | tf_op jit(solution)/shard_map/ppermute | solution.py:520
  3.4 14.4 %collective-permute-start.1 = (bf16[2,512,256]{2,1,0:T(8,128)(2,1)S(1)}, bf16[2,512,256]{2,1,0:T(8,128)(2,1)S(1)}, u32[]{:S(2)}, u32[]{:S(2)}) collective-permute-start(bf16[2,512,256]{2,1,0:T(8,128)(2,1)S(1)} %get-tuple-element.34._.sent_link_ref), channel_id=1, source_target_pairs={{8,16},{24,32},{40,48},{56,64},{72,80},{88,96},{104,112},{16,8},{3... | collective-permute-start | bytes 1572872 | tf_op jit(solution)/shard_map/ppermute | solution.py:521
  8.2 12.5 %collective-permute-start.2 = (bf16[4,16,256]{2,1,0:T(8,128)(2,1)S(1)}, bf16[4,16,256]{2,1,0:T(8,128)(2,1)S(1)}, u32[]{:S(2)}, u32[]{:S(2)}) collective-permute-start(bf16[4,16,256]{2,1,0:T(8,128)(2,1)S(1)} %get-tuple-element.47), channel_id=1, source_target_pairs={{0,1},{1,2},{2,3},{3,4},{4,5},{5,6},{6,7},{7,0},{8,9},{9,10},{10,1... | collective-permute-start | bytes 98312 | tf_op jit(solution)/shard_map/ppermute | solution.py:504
  9.5 11.2 %collective-permute-start.3 = (bf16[4,16,256]{2,1,0:T(8,128)(2,1)S(1)}, bf16[4,16,256]{2,1,0:T(8,128)(2,1)S(1)}, u32[]{:S(2)}, u32[]{:S(2)}) collective-permute-start(bf16[4,16,256]{2,1,0:T(8,128)(2,1)S(1)} %get-tuple-element.48), channel_id=1, source_target_pairs={{0,7},{1,0},{2,1},{3,2},{4,3},{5,4},{6,5},{7,6},{8,15},{9,8},{10,9... | collective-permute-start | bytes 98312 | tf_op jit(solution)/shard_map/ppermute | solution.py:504
  21.3 2.2 %collective-permute-start.4 = (bf16[20,128,128]{2,1,0:T(8,128)(2,1)S(1)}, bf16[20,128,128]{2,1,0:T(8,128)(2,1)S(1)}, u32[]{:S(2)}, u32[]{:S(2)}) collective-permute-start(bf16[20,128,128]{2,1,0:T(8,128)(2,1)S(1)} %get-tuple-element.53), channel_id=1, source_target_pairs={{0,8},{8,0},{1,9},{9,1},{2,10},{10,2},{3,11},{11,3},{4,12},{12,4},... | collective-permute-start | bytes 1966088 | tf_op jit(solution)/shard_map/ppermute | solution.py:531
  24.4 22.4 %all-to-all-start = ((bf16[64,40,128]{2,1,0:T(8,128)(2,1)}), bf16[64,40,128]{2,1,0:T(8,128)(2,1)S(1)}, u32[]{:S(2)}, u32[]{:S(2)}) async-start(bf16[64,40,128]{2,1,0:T(8,128)(2,1)} %bitcast.2), calls=%async_computation | async-start | bytes 1310720 | tf_op jit(solution)/shard_map/all_to_all | solution.py:534
  33.9 21.0 %collective-permute-start.7 = (bf16[2,560,256]{2,1,0:T(8,128)(2,1)S(1)}, bf16[2,560,256]{2,1,0:T(8,128)(2,1)}, u32[]{:S(2)}, u32[]{:S(2)}) collective-permute-start(bf16[2,560,256]{2,1,0:T(8,128)(2,1)S(1)} %ordered.7), channel_id=1, source_target_pairs={{0,8},{8,0},{1,9},{9,1},{2,10},{10,2},{3,11},{11,3},{4,12},{12,4},... | collective-permute-start | bytes 1720328 | tf_op jit(solution)/shard_map/ppermute | solution.py:536
  34.4 20.5 %collective-permute-start.8 = (bf16[2,560,256]{2,1,0:T(8,128)(2,1)S(1)}, bf16[2,560,256]{2,1,0:T(8,128)(2,1)}, u32[]{:S(2)}, u32[]{:S(2)}) collective-permute-start(bf16[2,560,256]{2,1,0:T(8,128)(2,1)S(1)} %ordered.8), channel_id=1, source_target_pairs={{8,16},{24,32},{40,48},{56,64},{72,80},{88,96},{104,112},{16,8},{3... | collective-permute-start | bytes 1720328 | tf_op jit(solution)/shard_map/ppermute | solution.py:535
  37.5 16.3 %collective-permute-start.5 = (f32[4,16,256]{2,1,0:T(8,128)S(1)}, f32[4,16,256]{2,1,0:T(8,128)S(1)}, u32[]{:S(2)}, u32[]{:S(2)}) collective-permute-start(f32[4,16,256]{2,1,0:T(8,128)S(1)} %ordered.5), channel_id=1, source_target_pairs={{0,1},{1,2},{2,3},{3,4},{4,5},{5,6},{6,7},{7,0},{8,9},{9,10},{10,1... | collective-permute-start | bytes 196616 | tf_op jit(solution)/shard_map/ppermute | solution.py:504
  38.8 15.1 %collective-permute-start.6 = (f32[4,16,256]{2,1,0:T(8,128)S(1)}, f32[4,16,256]{2,1,0:T(8,128)S(1)}, u32[]{:S(2)}, u32[]{:S(2)}) collective-permute-start(f32[4,16,256]{2,1,0:T(8,128)S(1)} %ordered.6), channel_id=1, source_target_pairs={{0,7},{1,0},{2,1},{3,2},{4,3},{5,4},{6,5},{7,6},{8,15},{9,8},{10,9... | collective-permute-start | bytes 196616 | tf_op jit(solution)/shard_map/ppermute | solution.py:504
  47.8 17.2 %all-to-all-start.1 = ((bf16[64,40,128]{2,1,0:T(8,128)(2,1)}), bf16[64,40,128]{2,1,0:T(8,128)(2,1)S(1)}, u32[]{:S(2)}, u32[]{:S(2)}) async-start(bf16[64,40,128]{2,1,0:T(8,128)(2,1)} %sum_part.1._), calls=%async_computation.1 | async-start | bytes 1310720 | tf_op jit(solution)/shard_map/all_to_all | solution.py:541
  65.0 5.8 %collective-permute-start.9 = (bf16[20,128,128]{2,1,0:T(8,128)(2,1)S(1)}, bf16[20,128,128]{2,1,0:T(8,128)(2,1)S(1)}, u32[]{:S(2)}, u32[]{:S(2)}) collective-permute-start(bf16[20,128,128]{2,1,0:T(8,128)(2,1)S(1)} %ordered.9.half_ref), channel_id=1, source_target_pairs={{0,8},{8,0},{1,9},{9,1},{2,10},{10,2},{3,11},{11,3},{4,12},{12,4},... | collective-permute-start | bytes 1966088 | tf_op jit(solution)/shard_map/ppermute | solution.py:547

commit v7 on v6

--- a/solution.py
+++ b/solution.py
@@ -83,12 +83,13 @@
     )(in_hbm(features))
 
 
-def own_kernel(lo_ref, hi_ref, basis_ref, cot_ref, _, to_right_ref, to_left_ref, kept_ref, cot, bands_ref, lo, hi, basis, sems):
+def own_kernel(lo_ref, hi_ref, basis_ref, cot_ref, _, to_right_ref, to_left_ref, kept_ref, bands_ref, lo, hi, basis, sems):
     copies = (
         (lo_ref, lo),
         (hi_ref, hi),
         (basis_ref, basis),
-        (cot_ref, cot),
+        (cot_ref.at[:, pl.ds(NJ - EDGE, EDGE)], to_right_ref),
+        (cot_ref.at[:, pl.ds(0, EDGE)], to_left_ref),
     )
     copies = [pltpu.make_async_copy(a, b, sems.at[n]) for n, (a, b) in enumerate(copies)]
     for copy in copies:
@@ -106,8 +107,6 @@
             bands_ref[i, k * J : (k + 1) * J, :] = banded(line[k : k + 1, :])[:, :DEPTH]
     for copy in copies[3:]:
         copy.wait()
-    to_right_ref[...] = cot[:, NJ - EDGE :, :]
-    to_left_ref[...] = cot[:, :EDGE, :]
 
 
 def own_part(span_lo, span_hi, basis, cotangent, after):
@@ -118,16 +117,15 @@
             pltpu.VMEM((ROWS, EDGE, C), BF),
             pltpu.VMEM((ROWS, EDGE, C), BF),
             pltpu.VMEM((ROWS, 16, LANES), BF),
-            pltpu.VMEM((ROWS, NJ, C), BF),
             pltpu.VMEM((ROWS, K * J, DEPTH), BF),
         ),
         in_specs=[IN_HBM] * 4 + [ANYWHERE],
-        out_specs=[IN_VMEM] * 5,
+        out_specs=[IN_VMEM] * 4,
         scratch_shapes=[
             pltpu.SMEM((ROWS,), jnp.int32),
             pltpu.SMEM((ROWS,), jnp.int32),
             pltpu.VMEM(basis.shape, F32),
-            pltpu.SemaphoreType.DMA((4,)),
+            pltpu.SemaphoreType.DMA((5,)),
         ],
         compiler_params=params(6),
         cost_estimate=cost(4e9, 4e6),
@@ -514,17 +512,17 @@
     pairs = pairs + [(b, a) for a, b in pairs]
     sent_chip, sent_link = send_part(features)
     weight = weight.reshape(K * C, C)
-    to_right, to_left, kept, near_cot, bands = own_part(
+    to_right, to_left, kept, bands = own_part(
         span_lo, span_hi, basis, cotangent, sent_link
     )
     chip = lax.ppermute(sent_chip, "core", swap)
     link = lax.ppermute(sent_link, lat, pairs)
     near_left = shifted(to_right, "lon", lons, 1, True)
     near_right = shifted(to_left, "lon", lons, -1, True)
-    total, near, weight_near = filter_part(0, chip, sent_chip, sent_link, bands, near_cot, weight)
+    total, near, weight_near = filter_part(0, chip, sent_chip, sent_link, bands, cotangent, weight)
     near_mixed, near_ends, to_right, to_left = mixed_part(0, near, weight_near)
     total, far, chip_cot, link_cot = filter_part(
-        1, link, sent_chip, sent_link, bands, near_cot, total, kept, to_right, cotangent
+        1, link, sent_chip, sent_link, bands, cotangent, total, kept, to_right, cotangent
     )
     own, other, chip_cot, link_cot = edge_part(near_left, near_right, total, near, far, chip_cot, link_cot)
 

time: 72.5 us -> 73.8 us (1.018)
  Pallas kernels: 26.9 us -> 28 us
    pallas_call x2, Pallas kernels: 5.64 us -> 6.84 us  [filter_part(): pl.pallas_call(functools.partial(filter_kernel, side), out_shape=tuple(ou...]
  transfers between devices with their start and end apart: 12 -> 12, of which waited for: 4 -> 4; matrix products, arithmetic and copies ran while one was open for 0% -> 0% of each run, Pallas kernels for 32% -> 33%
where the time goes in v7:
time: 73.8 us; the launch traced here: 73.3 us
  starting transfers between devices  38.7 us (52%)
  Pallas kernels  28 us (38%)
  waiting for transfers between devices  5.6 us (8%)
  between operations  1.02 us (1%)
    ppermute x4, starting transfers between devices, shifted(): return lax.ppermute(block, axis, route)  10.4 us
    pallas_call x1, Pallas kernels, grad_part(): pl.pallas_call(grad_kernel, out_shape=(jax.ShapeDtypeStruct((ROWS, NJ, C)...  9.69 us
    all_to_all x1, starting transfers between devices, per_device(): pieces = lax.all_to_all(half.reshape(parts, -1, LANES), chips, 0, 0)  9.5 us
    pallas_call x2, Pallas kernels, filter_part(): pl.pallas_call(functools.partial(filter_kernel, side), out_shape=tuple(ou...  6.84 us
    all_to_all x1, starting transfers between devices, per_device(): lax.all_to_all(copies, chips, 0, 0).reshape(PADDED_BLOCKS, LANES, LANES)  6.02 us
    all_to_all x1, waiting for transfers between devices, per_device(): pieces = lax.all_to_all(half.reshape(parts, -1, LANES), chips, 0, 0)  4.17 us
    ppermute x1, starting transfers between devices, per_device(): other = lax.ppermute(gathered, 'core', swap)  4.06 us
    ppermute x1, starting transfers between devices, per_device(): link = lax.ppermute(sent_link, lat, pairs)  3.53 us
  transfers between devices with their start and end apart: 12, of which 4 were waited for; matrix products, arithmetic and copies ran while one was open for 0% of the time, Pallas kernels for 33%

profile of v7, /device:TPU:1, one launch (start us, length us, event | category | flops | bytes accessed | tf_op | source)
XLA Modules:
  0.0 73.3 jit_solution(11026025644300718916)
XLA Ops:
  0.6 1.2 %send_part.1 = (bf16[2,512,256]{2,1,0:T(8,128)(2,1)S(1)}, bf16[2,512,256]{2,1,0:T(8,128)(2,1)S(1)}) custom-call(bf16[4,512,256]{2,1,0:T(8,128)(2,1)} %feat_ref.1), custom_call_target="tpu_custom_call" | custom-call | bytes 1000000 | tf_op jit(solution)/shard_map/send_part/pallas_call | solution.py:74
  1.9 1.5 %collective-permute-start = (bf16[2,512,256]{2,1,0:T(8,128)(2,1)S(1)}, bf16[2,512,256]{2,1,0:T(8,128)(2,1)S(1)}, u32[]{:S(2)}, u32[]{:S(2)}) collective-permute-start(bf16[2,512,256]{2,1,0:T(8,128)(2,1)S(1)} %get-tuple-element.32.sent_chip_ref), channel_id=1, source_target_pairs={{0,8},{8,0},{1,9},{9,1},{2,10},{10,2},{3,11},{11,3},{4,12},{12,4},... | collective-permute-start | bytes 1572872 | tf_op jit(solution)/shard_map/ppermute | solution.py:518
  3.4 3.5 %collective-permute-start.1 = (bf16[2,512,256]{2,1,0:T(8,128)(2,1)S(1)}, bf16[2,512,256]{2,1,0:T(8,128)(2,1)S(1)}, u32[]{:S(2)}, u32[]{:S(2)}) collective-permute-start(bf16[2,512,256]{2,1,0:T(8,128)(2,1)S(1)} %get-tuple-element.33._.sent_link_ref), channel_id=1, source_target_pairs={{8,16},{24,32},{40,48},{56,64},{72,80},{88,96},{104,112},{16,8},{3... | collective-permute-start | bytes 1572872 | tf_op jit(solution)/shard_map/ppermute | solution.py:519
  6.9 1.2 %own_part.1 = (bf16[4,16,256]{2,1,0:T(8,128)(2,1)S(1)}, bf16[4,16,256]{2,1,0:T(8,128)(2,1)S(1)}, bf16[4,16,128]{2,1,0:T(8,128)(2,1)S(1)}, bf16[4,288,240]{2,1,0:T(8,128)(2,1)S(1)}) custom-call(s32[4]{0:T(128)} %lo_ref.1, s32[4]{0:T(128)} %hi_ref.1, f32[9,4,25]{2,1,0:T(4,128)} %bitcast.7, bf16[4,512,256]{2,1,0:T(8,128)(2,1)} %cot_hbm.1, ...), custom_call_target="tpu_custom_call" | custom-call | flops 4000000000 | bytes 4000000 | tf_op jit(solution)/shard_map/own_part/pallas_call | solution.py:114
  8.1 1.3 %collective-permute-start.2 = (bf16[4,16,256]{2,1,0:T(8,128)(2,1)S(1)}, bf16[4,16,256]{2,1,0:T(8,128)(2,1)S(1)}, u32[]{:S(2)}, u32[]{:S(2)}) collective-permute-start(bf16[4,16,256]{2,1,0:T(8,128)(2,1)S(1)} %get-tuple-element.45), channel_id=1, source_target_pairs={{0,1},{1,2},{2,3},{3,4},{4,5},{5,6},{6,7},{7,0},{8,9},{9,10},{10,1... | collective-permute-start | bytes 98312 | tf_op jit(solution)/shard_map/ppermute | solution.py:502
  9.4 4.0 %collective-permute-start.3 = (bf16[4,16,256]{2,1,0:T(8,128)(2,1)S(1)}, bf16[4,16,256]{2,1,0:T(8,128)(2,1)S(1)}, u32[]{:S(2)}, u32[]{:S(2)}) collective-permute-start(bf16[4,16,256]{2,1,0:T(8,128)(2,1)S(1)} %get-tuple-element.46), channel_id=1, source_target_pairs={{0,7},{1,0},{2,1},{3,2},{4,3},{5,4},{6,5},{7,6},{8,15},{9,8},{10,9... | collective-permute-start | bytes 98312 | tf_op jit(solution)/shard_map/ppermute | solution.py:502
  13.4 2.8 %filter_part.2 = (f32[256,2304]{1,0:T(8,128)S(1)}, bf16[1088,2304]{1,0:T(8,128)(2,1)S(1)}, bf16[2304,256]{1,0:T(8,128)(2,1)S(1)}) custom-call(bf16[2,512,256]{2,1,0:T(8,128)(2,1)S(1)} %collective-permute-done.halo_ref, bf16[2,512,256]{2,1,0:T(8,128)(2,1)S(1)} %get-tuple-element.32.sent_chip_ref, bf16[2,512,256]{2,1,0:T(8,128)(2,1)S(1)} %get-tuple-element.33._.sent_link_ref, ...), custom_call_target="tpu_custom_call" | custom-call | flops 100000000 | bytes 100000 | tf_op jit(solution)/shard_map/filter_part/pallas_call | solution.py:200
  16.2 1.6 %mixed_part.2 = (bf16[2,512,256]{2,1,0:T(8,128)(2,1)S(1)}, f32[2,32,256]{2,1,0:T(8,128)S(1)}, f32[2,16,256]{2,1,0:T(8,128)S(1)}, f32[2,16,256]{2,1,0:T(8,128)S(1)}) custom-call(bf16[1088,2304]{1,0:T(8,128)(2,1)S(1)} %get-tuple-element.35.filtered_ref.near_ref, bf16[2304,256]{1,0:T(8,128)(2,1)S(1)} %get-tuple-element.36.weight_ref), custom_call_target="tpu_custom_call" | custom-call | flops 100000000 | bytes 100000 | tf_op jit(solution)/shard_map/mixed_part/pallas_call | solution.py:308
  17.8 4.1 %filter_part.3 = (f32[256,2304]{1,0:T(8,128)S(1)}, bf16[1088,2304]{1,0:T(8,128)(2,1)S(1)}, bf16[2,560,256]{2,1,0:T(8,128)(2,1)S(1)}, bf16[2,560,256]{2,1,0:T(8,128)(2,1)S(1)}) custom-call(bf16[2,512,256]{2,1,0:T(8,128)(2,1)S(1)} %collective-permute-done.1.halo_ref, bf16[2,512,256]{2,1,0:T(8,128)(2,1)S(1)} %get-tuple-element.32.sent_chip_ref, ...), custom_call_target="tpu_custom_call" | custom-call | flops 100000000 | bytes 100000 | tf_op jit(solution)/shard_map/filter_part/pallas_call | solution.py:200
  21.9 0.6 edge_part.1
  22.6 1.6 %mixed_part.3 = (bf16[2,512,256]{2,1,0:T(8,128)(2,1)S(1)}, f32[2,32,256]{2,1,0:T(8,128)S(1)}, f32[4,16,256]{2,1,0:T(8,128)S(1)}, f32[4,16,256]{2,1,0:T(8,128)S(1)}) custom-call(bf16[1088,2304]{1,0:T(8,128)(2,1)S(1)} %get-tuple-element.41.filtered_ref.far_ref, bf16[2304,256]{1,0:T(8,128)(2,1)S(1)} %get-tuple-element.36.weight_ref, ...), custom_call_target="tpu_custom_call" | custom-call | flops 100000000 | bytes 100000 | tf_op jit(solution)/shard_map/mixed_part/pallas_call | solution.py:308
  24.7 0.9 %half_part.1.__1_ = bf16[20,128,128]{2,1,0:T(8,128)(2,1)} custom-call(f32[20,128,128]{2,1,0:T(8,128)S(1)} %get-tuple-element.50.own_ref, bf16[20,128,128]{2,1,0:T(8,128)(2,1)S(1)} %collective-permute-done.4.other_ref, f32[2,32,256]{2,1,0:T(8,128)S(1)} %get-tuple-element.43._.far_ends_ref), custom_call_target="tpu_custom_call" | custom-call | flops 1000000 | bytes 3000000 | tf_op jit(solution)/shard_map/half_part/pallas_call | solution.py:277
  25.6 9.5 %all-to-all-start = ((bf16[64,40,128]{2,1,0:T(8,128)(2,1)}), bf16[64,40,128]{2,1,0:T(8,128)(2,1)S(1)}, u32[]{:S(2)}, u32[]{:S(2)}) async-start(bf16[64,40,128]{2,1,0:T(8,128)(2,1)} %bitcast.2), calls=%async_computation | async-start | bytes 1310720 | tf_op jit(solution)/shard_map/all_to_all | solution.py:532
  35.6 3.1 %collective-permute-start.8 = (bf16[2,560,256]{2,1,0:T(8,128)(2,1)S(1)}, bf16[2,560,256]{2,1,0:T(8,128)(2,1)}, u32[]{:S(2)}, u32[]{:S(2)}) collective-permute-start(bf16[2,560,256]{2,1,0:T(8,128)(2,1)S(1)} %ordered.8), channel_id=1, source_target_pairs={{8,16},{24,32},{40,48},{56,64},{72,80},{88,96},{104,112},{16,8},{3... | collective-permute-start | bytes 1720328 | tf_op jit(solution)/shard_map/ppermute | solution.py:533
  38.7 1.3 %collective-permute-start.5 = (f32[4,16,256]{2,1,0:T(8,128)S(1)}, f32[4,16,256]{2,1,0:T(8,128)S(1)}, u32[]{:S(2)}, u32[]{:S(2)}) collective-permute-start(f32[4,16,256]{2,1,0:T(8,128)S(1)} %ordered.5), channel_id=1, source_target_pairs={{0,1},{1,2},{2,3},{3,4},{4,5},{5,6},{6,7},{7,0},{8,9},{9,10},{10,1... | collective-permute-start | bytes 196616 | tf_op jit(solution)/shard_map/ppermute | solution.py:502
  40.0 3.9 %collective-permute-start.6 = (f32[4,16,256]{2,1,0:T(8,128)S(1)}, f32[4,16,256]{2,1,0:T(8,128)S(1)}, u32[]{:S(2)}, u32[]{:S(2)}) collective-permute-start(f32[4,16,256]{2,1,0:T(8,128)S(1)} %ordered.6), channel_id=1, source_target_pairs={{0,7},{1,0},{2,1},{3,2},{4,3},{5,4},{6,5},{7,6},{8,15},{9,8},{10,9... | collective-permute-start | bytes 196616 | tf_op jit(solution)/shard_map/ppermute | solution.py:502
  43.9 4.2 %all-to-all-done.pieces_ref = bf16[64,40,128]{2,1,0:T(8,128)(2,1)S(1)} async-done(((bf16[64,40,128]{2,1,0:T(8,128)(2,1)}), bf16[64,40,128]{2,1,0:T(8,128)(2,1)S(1)}, u32[]{:S(2)}, u32[]{:S(2)}) %all-to-all-start) | async-done | bytes 655392 | tf_op jit(solution)/shard_map/all_to_all | solution.py:532
  48.1 1.0 %sum_part.1._ = bf16[64,40,128]{2,1,0:T(8,128)(2,1)} custom-call(bf16[64,40,128]{2,1,0:T(8,128)(2,1)S(1)} %all-to-all-done.pieces_ref), custom_call_target="tpu_custom_call" | custom-call | flops 1000000 | bytes 2000000 | tf_op jit(solution)/shard_map/sum_part/pallas_call | solution.py:362
  49.0 6.0 %all-to-all-start.1 = ((bf16[64,40,128]{2,1,0:T(8,128)(2,1)}), bf16[64,40,128]{2,1,0:T(8,128)(2,1)S(1)}, u32[]{:S(2)}, u32[]{:S(2)}) async-start(bf16[64,40,128]{2,1,0:T(8,128)(2,1)} %sum_part.1._), calls=%async_computation.1 | async-start | bytes 1310720 | tf_op jit(solution)/shard_map/all_to_all | solution.py:539
  55.1 1.0 %ends_part.1 = (bf16[4,512,256]{2,1,0:T(8,128)(2,1)}, f32[8,128]{1,0:T(8,128)S(1)}) custom-call(f32[2,32,256]{2,1,0:T(8,128)S(1)} %get-tuple-element.37.near_ends_ref, f32[2,32,256]{2,1,0:T(8,128)S(1)} %get-tuple-element.43._.far_ends_ref, f32[4,16,256]{2,1,0:T(8,128)S(1)} %collective-permute-done.5.left_ref, ...), custom_call_target="tpu_custom_call" | custom-call | flops 1000000 | bytes 1000000 | tf_op jit(solution)/shard_map/ends_part/pallas_call | solution.py:344
  56.1 9.7 %grad_input_part.1 = (bf16[4,512,256]{2,1,0:T(8,128)(2,1)}, f32[8,128]{1,0:T(8,128)S(1)}) custom-call(bf16[4,16,128]{2,1,0:T(8,128)(2,1)S(1)} %get-tuple-element.39.refs_1_.kept_ref, bf16[2,560,256]{2,1,0:T(8,128)(2,1)} %collective-permute-done.7.chip_ref, bf16[2,560,256]{2,1,0:T(8,128)(2,1)} %collective-permute-done.8.link_ref, ...), custom_call_target="tpu_custom_call" | custom-call | flops 8000000000 | bytes 5000000 | tf_op jit(solution)/shard_map/grad_input_part/pallas_call | solution.py:478
  66.2 4.1 %collective-permute-start.9 = (bf16[20,128,128]{2,1,0:T(8,128)(2,1)S(1)}, bf16[20,128,128]{2,1,0:T(8,128)(2,1)S(1)}, u32[]{:S(2)}, u32[]{:S(2)}) collective-permute-start(bf16[20,128,128]{2,1,0:T(8,128)(2,1)S(1)} %ordered.9.half_ref), channel_id=1, source_target_pairs={{0,8},{8,0},{1,9},{9,1},{2,10},{10,2},{3,11},{11,3},{4,12},{12,4},... | collective-permute-start | bytes 1966088 | tf_op jit(solution)/shard_map/ppermute | solution.py:545
  70.3 1.2 %result_part.2.refs_0_ = f32[9,256,256]{2,1,0:T(8,128)} custom-call(bf16[20,128,128]{2,1,0:T(8,128)(2,1)S(1)} %ordered.9.half_ref), custom_call_target="tpu_custom_call" | custom-call | flops 1000000 | bytes 4000000 | tf_op jit(solution)/shard_map/result_part/pallas_call | solution.py:405
  72.0 1.2 %result_part.3 = f32[9,256,256]{2,1,0:T(8,128)} custom-call(bf16[20,128,128]{2,1,0:T(8,128)(2,1)S(1)} %collective-permute-done.9.half_ref, f32[9,256,256]{2,1,0:T(8,128)} %result_part.2.refs_0_), custom_call_target="tpu_custom_call", output_to_operand_aliasing={{}: (1, {})} | custom-call | flops 1000000 | bytes 4000000 | tf_op jit(solution)/shard_map/result_part/pallas_call | solution.py:405
  (20 shorter events, 2.0 us)
Async XLA Ops:
  1.9 11.5 %collective-permute-start = (bf16[2,512,256]{2,1,0:T(8,128)(2,1)S(1)}, bf16[2,512,256]{2,1,0:T(8,128)(2,1)S(1)}, u32[]{:S(2)}, u32[]{:S(2)}) collective-permute-start(bf16[2,512,256]{2,1,0:T(8,128)(2,1)S(1)} %get-tuple-element.32.sent_chip_ref), channel_id=1, source_target_pairs={{0,8},{8,0},{1,9},{9,1},{2,10},{10,2},{3,11},{11,3},{4,12},{12,4},... | collective-permute-start | bytes 1572872 | tf_op jit(solution)/shard_map/ppermute | solution.py:518
  3.4 14.4 %collective-permute-start.1 = (bf16[2,512,256]{2,1,0:T(8,128)(2,1)S(1)}, bf16[2,512,256]{2,1,0:T(8,128)(2,1)S(1)}, u32[]{:S(2)}, u32[]{:S(2)}) collective-permute-start(bf16[2,512,256]{2,1,0:T(8,128)(2,1)S(1)} %get-tuple-element.33._.sent_link_ref), channel_id=1, source_target_pairs={{8,16},{24,32},{40,48},{56,64},{72,80},{88,96},{104,112},{16,8},{3... | collective-permute-start | bytes 1572872 | tf_op jit(solution)/shard_map/ppermute | solution.py:519
  6.9 6.5 %copy-start = (bf16[4,512,256]{2,1,0:T(8,128)(2,1)S(1)}, bf16[4,512,256]{2,1,0:T(8,128)(2,1)}, u32[]{:S(2)}) copy-start(bf16[4,512,256]{2,1,0:T(8,128)(2,1)} %cot_hbm.1) | copy-start | bytes 3145732
  8.1 13.7 %collective-permute-start.2 = (bf16[4,16,256]{2,1,0:T(8,128)(2,1)S(1)}, bf16[4,16,256]{2,1,0:T(8,128)(2,1)S(1)}, u32[]{:S(2)}, u32[]{:S(2)}) collective-permute-start(bf16[4,16,256]{2,1,0:T(8,128)(2,1)S(1)} %get-tuple-element.45), channel_id=1, source_target_pairs={{0,1},{1,2},{2,3},{3,4},{4,5},{5,6},{6,7},{7,0},{8,9},{9,10},{10,1... | collective-permute-start | bytes 98312 | tf_op jit(solution)/shard_map/ppermute | solution.py:502
  9.4 12.5 %collective-permute-start.3 = (bf16[4,16,256]{2,1,0:T(8,128)(2,1)S(1)}, bf16[4,16,256]{2,1,0:T(8,128)(2,1)S(1)}, u32[]{:S(2)}, u32[]{:S(2)}) collective-permute-start(bf16[4,16,256]{2,1,0:T(8,128)(2,1)S(1)} %get-tuple-element.46), channel_id=1, source_target_pairs={{0,7},{1,0},{2,1},{3,2},{4,3},{5,4},{6,5},{7,6},{8,15},{9,8},{10,9... | collective-permute-start | bytes 98312 | tf_op jit(solution)/shard_map/ppermute | solution.py:502
  22.5 2.2 %collective-permute-start.4 = (bf16[20,128,128]{2,1,0:T(8,128)(2,1)S(1)}, bf16[20,128,128]{2,1,0:T(8,128)(2,1)S(1)}, u32[]{:S(2)}, u32[]{:S(2)}) collective-permute-start(bf16[20,128,128]{2,1,0:T(8,128)(2,1)S(1)} %get-tuple-element.51), channel_id=1, source_target_pairs={{0,8},{8,0},{1,9},{9,1},{2,10},{10,2},{3,11},{11,3},{4,12},{12,4},... | collective-permute-start | bytes 1966088 | tf_op jit(solution)/shard_map/ppermute | solution.py:529
  25.6 22.5 %all-to-all-start = ((bf16[64,40,128]{2,1,0:T(8,128)(2,1)}), bf16[64,40,128]{2,1,0:T(8,128)(2,1)S(1)}, u32[]{:S(2)}, u32[]{:S(2)}) async-start(bf16[64,40,128]{2,1,0:T(8,128)(2,1)} %bitcast.2), calls=%async_computation | async-start | bytes 1310720 | tf_op jit(solution)/shard_map/all_to_all | solution.py:532
  35.1 21.0 %collective-permute-start.7 = (bf16[2,560,256]{2,1,0:T(8,128)(2,1)S(1)}, bf16[2,560,256]{2,1,0:T(8,128)(2,1)}, u32[]{:S(2)}, u32[]{:S(2)}) collective-permute-start(bf16[2,560,256]{2,1,0:T(8,128)(2,1)S(1)} %ordered.7), channel_id=1, source_target_pairs={{0,8},{8,0},{1,9},{9,1},{2,10},{10,2},{3,11},{11,3},{4,12},{12,4},... | collective-permute-start | bytes 1720328 | tf_op jit(solution)/shard_map/ppermute | solution.py:534
  35.6 20.5 %collective-permute-start.8 = (bf16[2,560,256]{2,1,0:T(8,128)(2,1)S(1)}, bf16[2,560,256]{2,1,0:T(8,128)(2,1)}, u32[]{:S(2)}, u32[]{:S(2)}) collective-permute-start(bf16[2,560,256]{2,1,0:T(8,128)(2,1)S(1)} %ordered.8), channel_id=1, source_target_pairs={{8,16},{24,32},{40,48},{56,64},{72,80},{88,96},{104,112},{16,8},{3... | collective-permute-start | bytes 1720328 | tf_op jit(solution)/shard_map/ppermute | solution.py:533
  38.7 16.3 %collective-permute-start.5 = (f32[4,16,256]{2,1,0:T(8,128)S(1)}, f32[4,16,256]{2,1,0:T(8,128)S(1)}, u32[]{:S(2)}, u32[]{:S(2)}) collective-permute-start(f32[4,16,256]{2,1,0:T(8,128)S(1)} %ordered.5), channel_id=1, source_target_pairs={{0,1},{1,2},{2,3},{3,4},{4,5},{5,6},{6,7},{7,0},{8,9},{9,10},{10,1... | collective-permute-start | bytes 196616 | tf_op jit(solution)/shard_map/ppermute | solution.py:502
  40.0 15.1 %collective-permute-start.6 = (f32[4,16,256]{2,1,0:T(8,128)S(1)}, f32[4,16,256]{2,1,0:T(8,128)S(1)}, u32[]{:S(2)}, u32[]{:S(2)}) collective-permute-start(f32[4,16,256]{2,1,0:T(8,128)S(1)} %ordered.6), channel_id=1, source_target_pairs={{0,7},{1,0},{2,1},{3,2},{4,3},{5,4},{6,5},{7,6},{8,15},{9,8},{10,9... | collective-permute-start | bytes 196616 | tf_op jit(solution)/shard_map/ppermute | solution.py:502
  49.0 17.2 %all-to-all-start.1 = ((bf16[64,40,128]{2,1,0:T(8,128)(2,1)}), bf16[64,40,128]{2,1,0:T(8,128)(2,1)S(1)}, u32[]{:S(2)}, u32[]{:S(2)}) async-start(bf16[64,40,128]{2,1,0:T(8,128)(2,1)} %sum_part.1._), calls=%async_computation.1 | async-start | bytes 1310720 | tf_op jit(solution)/shard_map/all_to_all | solution.py:539
  66.2 5.8 %collective-permute-start.9 = (bf16[20,128,128]{2,1,0:T(8,128)(2,1)S(1)}, bf16[20,128,128]{2,1,0:T(8,128)(2,1)S(1)}, u32[]{:S(2)}, u32[]{:S(2)}) collective-permute-start(bf16[20,128,128]{2,1,0:T(8,128)(2,1)S(1)} %ordered.9.half_ref), channel_id=1, source_target_pairs={{0,8},{8,0},{1,9},{9,1},{2,10},{10,2},{3,11},{11,3},{4,12},{12,4},... | collective-permute-start | bytes 1966088 | tf_op jit(solution)/shard_map/ppermute | solution.py:545
